TPU v7x, 32 devices: a whole 2x2x4 slice. The times are simulated.
32 devices in a mesh: dp: 4 (over y, x), table: 8 (over z, core).
Axes of the slice: x: 2, y: 2, z: 4, core: 2. Of those that a mesh axis runs over, the one named last changes fastest.
Arguments:
- shard_of: int32 [256, 200, 3], P(('dp', 'table')), may hold values from 0 to 7, all different within a row; in each aligned block of 1600 rows (0 to 1599, 1600 to 3199, ..., all dimensions but the last counted through in order) at most 1200 rows name the same one
- offsets: int32 [256, 200, 3], P(('dp', 'table')), may hold values from 0 to 2047
- table: bfloat16 [3, 16384, 256], P(None, 'table'), may hold values from -4 to 4
- weight_one: bfloat16 [768, 256], replicated, may hold values from -0.21875 to 0.21875
- gain_one: float32 [256], replicated, may hold values from 0.5 to 1.5
- weight_two: bfloat16 [768, 256], replicated, may hold values from -0.21875 to 0.21875
- gain_two: float32 [256], replicated, may hold values from 0.5 to 1.5
- grad_out: bfloat16 [256, 200, 256], P(('dp', 'table')), may hold values from -6 to 6
Outputs:
- block_out: bfloat16 [256, 200, 256], P(('dp', 'table'))
- grad_weight_one: float32 [768, 256], replicated
- grad_weight_two: float32 [768, 256], replicated
- grad_gain_one: float32 [256], replicated
- grad_gain_two: float32 [256], replicated
- table_grad: float32 [3, 16384, 256], P(None, 'table', 'dp')
Inputs may be any that keep to these rules, and one draw needn't show every extreme that they name: `shard_of`: the three lookups of one item go to three different shards; at most 1200 lookups of the items of one device go to one shard, and exactly 1200 for some shard of some device.
All inputs are finite; a program needn't handle non-finite values.
Results may differ from a plain program's by a relative error of at most 0.017.
Values may be sent and summed in bfloat16 or wider, within the bound.
No kernel may reach another device: no remote copies, remote signals or barrier semaphores. Data moves between devices by JAX's collectives and lax.ppermute only.
A program may use at most 128 MiB of HBM per device.

v0:
```python
import math

import jax
import jax.numpy as jnp
from jax import lax
from jax.sharding import PartitionSpec as P

GELU_C = 0.7978845608028654
GELU_K = 0.044715


def shifted(values, spacing):
    return jnp.pad(values, ((0, 0), (spacing, 0), (0, 0)))[:, : values.shape[1], :]


def unshifted(values, spacing):
    return jnp.pad(values, ((0, 0), (0, spacing), (0, 0)))[:, spacing:, :]


def stack_taps(values, spacing):
    return jnp.concatenate(
        [values, shifted(values, spacing), shifted(values, 2 * spacing)], axis=-1
    )


def gelu_parts(inputs):
    inner = GELU_C * (inputs + GELU_K * inputs * inputs * inputs)
    tangent = jnp.tanh(inner)
    output = 0.5 * inputs * (1.0 + tangent)
    slope = 0.5 * (1.0 + tangent) + 0.5 * inputs * (1.0 - tangent * tangent) * GELU_C * (
        1.0 + 3.0 * GELU_K * inputs * inputs
    )
    return (output, slope)


def layer_forward(values, weight, gain, spacing):
    sessions, length, width = values.shape
    stacked = stack_taps(values, spacing).reshape(sessions * length, 3 * width)
    before_norm = jnp.dot(stacked, weight, preferred_element_type=jnp.float32)
    centred = before_norm - jnp.mean(before_norm, axis=-1, keepdims=True)
    inv_std = lax.rsqrt(jnp.mean(centred * centred, axis=-1, keepdims=True) + 1e-05)
    normal = centred * inv_std
    output, slope = gelu_parts(normal * gain)
    return (output, (stacked, normal, inv_std, slope))


def layer_backward(grad_output, weight, gain, saved, spacing, sessions, length):
    stacked, normal, inv_std, slope = saved
    width = weight.shape[1]
    grad_scaled = grad_output * slope
    grad_gain = jnp.sum(grad_scaled * normal, axis=0)
    grad_normal = grad_scaled * gain
    grad_before = inv_std * (
        grad_normal
        - jnp.mean(grad_normal, axis=-1, keepdims=True)
        - normal * jnp.mean(grad_normal * normal, axis=-1, keepdims=True)
    )
    grad_before = grad_before.astype(jnp.bfloat16)
    grad_weight = lax.dot_general(
        stacked, grad_before, (((0,), (0,)), ((), ())), preferred_element_type=jnp.float32
    )
    grad_taps = lax.dot_general(
        grad_before, weight, (((1,), (1,)), ((), ())), preferred_element_type=jnp.float32
    ).reshape(sessions, length, 3 * width)
    grad_input = (
        grad_taps[..., :width]
        + unshifted(grad_taps[..., width : 2 * width], spacing)
        + unshifted(grad_taps[..., 2 * width :], 2 * spacing)
    )
    return (grad_input, grad_weight, grad_gain)


def to_owners(grad_rows, slot_place, shards, slot_count, width):
    outgoing = (
        jnp.zeros((shards * slot_count, width), jnp.bfloat16)
        .at[slot_place]
        .set(grad_rows)
        .reshape(shards, slot_count, width)
    )
    return lax.all_to_all(outgoing, "table", split_axis=0, concat_axis=0, tiled=True)


def on_device(shard_of, offsets, table, weight_one, gain_one, weight_two, gain_two, grad_out):
    sessions, length, _ = shard_of.shape
    width = table.shape[2]
    rows_dev = table.shape[1]
    item_count = sessions * length
    shards = lax.axis_size("table")
    groups = lax.axis_size("dp")
    quarter = width // groups
    slot_count = 8 * ((6 * item_count + 8 * shards - 1) // (8 * shards))
    target = shard_of.reshape(-1)
    table_pick = jnp.tile(jnp.arange(3, dtype=jnp.int32), item_count)
    row_codes = table_pick * rows_dev + offsets.reshape(-1)
    onehot = (jnp.arange(shards, dtype=jnp.int32)[:, None] == target[None, :]).astype(jnp.int32)
    before = jnp.cumsum(onehot, axis=1) - onehot
    slot_rank = jnp.sum(before * onehot, axis=0)
    slot_place = target * slot_count + slot_rank
    requests = (
        jnp.full((shards * slot_count,), -1, jnp.int32)
        .at[slot_place]
        .set(row_codes)
        .reshape(shards, slot_count)
    )
    table_flat = table.reshape(3 * rows_dev, width)
    asked_rows = lax.all_to_all(requests, "table", split_axis=0, concat_axis=0, tiled=True)
    found_rows = jnp.take(table_flat, jnp.maximum(asked_rows, 0), axis=0)
    found_rows = jnp.where((asked_rows >= 0)[..., None], found_rows, jnp.zeros((), jnp.bfloat16))
    sent_back = lax.all_to_all(found_rows, "table", split_axis=0, concat_axis=0, tiled=True)
    picked = jnp.take(sent_back.reshape(shards * slot_count, width), slot_place, axis=0).reshape(
        item_count, 3, width
    )
    embedded = (
        jnp.sum(picked.astype(jnp.float32), axis=1)
        .astype(jnp.bfloat16)
        .reshape(sessions, length, width)
    )
    act_one, saved_one = layer_forward(embedded, weight_one, gain_one, 1)
    hidden = act_one.astype(jnp.bfloat16).reshape(sessions, length, width)
    act_two, saved_two = layer_forward(hidden, weight_two, gain_two, 2)
    block_out = (
        (embedded.reshape(item_count, width).astype(jnp.float32) + act_two)
        .astype(jnp.bfloat16)
        .reshape(sessions, length, width)
    )
    grad_top = grad_out.reshape(item_count, width).astype(jnp.float32)
    scale = 1.0 / math.sqrt(item_count * groups * shards)
    grad_hidden, second_weights, second_gains = layer_backward(
        grad_top, weight_two, gain_two, saved_two, 2, sessions, length
    )
    grad_inner, first_weights, first_gains = layer_backward(
        grad_hidden.reshape(item_count, width), weight_one, gain_one, saved_one, 1, sessions, length
    )
    grad_embed = (grad_top + grad_inner.reshape(item_count, width)).astype(jnp.bfloat16)
    repeated = jnp.repeat(grad_embed, 3, axis=0)
    arrived = to_owners(repeated, slot_place, shards, slot_count, width)
    dense_grad = (
        jnp.zeros((3 * rows_dev, width), jnp.float32)
        .at[jnp.maximum(asked_rows, 0).reshape(-1)]
        .add(arrived.reshape(-1, width).astype(jnp.float32))
    )
    table_grad = lax.psum_scatter(
        dense_grad.astype(jnp.bfloat16), "dp", scatter_dimension=1, tiled=True
    ).astype(jnp.float32)
    table_grad = table_grad.reshape(3, rows_dev, quarter)
    totals = lax.psum((first_weights, second_weights, first_gains, second_gains), ("dp", "table"))
    return (
        block_out,
        totals[0] * scale,
        totals[1] * scale,
        totals[2] * scale,
        totals[3] * scale,
        table_grad,
    )


def solution(mesh):
    placed = (
        P(("dp", "table"), None, None),
        P(("dp", "table"), None, None),
        P(None, "table", None),
        P(),
        P(),
        P(),
        P(),
        P(("dp", "table"), None, None),
    )
    return jax.shard_map(
        on_device,
        mesh=mesh,
        in_specs=placed,
        out_specs=(P(("dp", "table"), None, None), P(), P(), P(), P(), P(None, "table", "dp")),
        check_vma=False,
    )
```

profile of v0, /device:TPU:0, one launch (start us, length us, event | category | flops | bytes accessed | tf_op | source)
XLA Modules:
  0.0 556.7 jit_solution(5028934634280955311)
XLA Ops:
  8.9 2.0 copy.44
  13.1 2.3 mul.226
  16.6 1.6 reshape.223
  18.2 1.6 reshape.220
  20.0 2.3 reduce-window.6
  23.1 1.6 mul.229
  24.8 22.8 %scatter_custom_fusion = s32[9600]{0:T(1024)S(1)} fusion(s32[4800]{0:T(1024)S(1)} %fusion.30, s32[4800]{0:T(1024)S(1)} %add.145, s32[]{:T(128)} %constant.40.clone.1), kind=kCustom, calls=%fused_computation.84 | custom fusion | bytes 38404 | tf_op jit(solution)/shard_map/scatter | solution.py:102
  47.7 11.9 %all_to_all.19 = s32[8,1,1200]{2,1,0:T(1,128)S(1)} all-to-all(s32[8,1,1200]{2,1,0:T(1,128)S(1)} %all_to_all.12), channel_id=1, replica_groups=mesh['dp'=4,'table'=8] {'table'}, dimensions={0} | all-to-all | bytes 76800 | tf_op jit(solution)/shard_map/all_to_all | solution.py:106
  59.8 27.7 %gather_fusion = bf16[9600,256]{1,0:T(8,128)(2,1)} fusion(bf16[6144,256]{1,0:T(8,128)(2,1)S(1)} %bitcast.56, s32[10240]{0:T(1024)S(1)} %pad_clamp_fusion), kind=kCustom, calls=%fused_computation | custom fusion | bytes 9868800 | tf_op jit(solution)/shard_map/jit(_take)/gather | solution.py:107
  87.5 10.5 %select_select_fusion = bf16[8,1200,256]{2,1,0:T(8,128)(2,1)} fusion(bf16[8,1200,256]{2,1,0:T(8,128)(2,1)} %bitcast.62, pred[8,1200]{1,0:T(8,128)(4,1)S(1)} %get-tuple-element.57, pred[8,1200]{1,0:T(8,128)(4,1)S(1)} %get-tuple-element.56), kind=kLoop, calls=%fused_computation.7 | loop fusion | flops 4915200 | bytes 9849600 | tf_op jit(solution)/shard_map/jit(_where)/select_n | solution.py:108
  98.0 4.8 all-to-all-start.1
  104.3 107.9 %all-to-all-done.1 = bf16[8,1200,256]{2,1,0:T(8,128)(2,1)} async-done(((bf16[8,1200,256]{2,1,0:T(8,128)(2,1)}), bf16[8,1200,256]{2,1,0:T(8,128)(2,1)}, u32[]{:S(2)}, u32[]{:S(2)}) %all-to-all-start.1) | async-done | bytes 4915232 | tf_op jit(solution)/shard_map/all_to_all | solution.py:109
  212.3 13.8 %gather_fusion.1 = bf16[4800,256]{1,0:T(8,128)(2,1)S(1)} fusion(bf16[9600,256]{1,0:T(8,128)(2,1)} %bitcast.5, s32[5120]{0:T(1024)S(1)} %pad_clamp_fusion.1), kind=kCustom, calls=%fused_computation.1 | custom fusion | bytes 4934400 | tf_op jit(solution)/shard_map/jit(_take)/gather | solution.py:110
  226.0 3.8 gather.12
  229.8 13.2 %select_reduce_fusion = bf16[1600,256]{1,0:T(8,128)(2,1)S(1)} fusion(bf16[1600,3,256]{2,1,0:T(4,128)(2,1)} %gather.12, pred[1600,3]{1,0:T(8,128)(4,1)S(1)} %copy.47), kind=kLoop, calls=%fused_computation.8 | loop fusion | flops 2048000 | bytes 3281600 | tf_op jit(solution)/shard_map/reduce_sum | solution.py:114
  250.2 1.5 convert_multiply_fusion
  252.7 2.4 multiply_convert_fusion.1
  256.6 1.7 fusion.20
  262.4 7.5 %broadcast_in_dim.70 = bf16[1600,3,256]{2,1,0:T(4,128)(2,1)} broadcast(bf16[1600,256]{1,0:T(8,128)(2,1)S(1)} %fusion.9), dimensions={0,2} | broadcast | bytes 3276800 | tf_op jit(solution)/shard_map/broadcast_in_dim | solution.py:135
  269.8 7.2 %reshape.269 = bf16[4800,256]{1,0:T(8,128)(2,1)} reshape(bf16[1600,3,256]{2,1,0:T(4,128)(2,1)} %broadcast_in_dim.70) | data formatting | bytes 4915200 | tf_op jit(solution)/shard_map/reshape | solution.py:135
  277.1 28.4 %scatter_custom_fusion.1 = bf16[9600,256]{1,0:T(8,128)(2,1)} fusion(s32[4800]{0:T(1024)S(1)} %fusion.30, bf16[4800,256]{1,0:T(8,128)(2,1)} %reshape.269, bf16[]{:T(256)} %constant.72.clone.1), kind=kCustom, calls=%fused_computation.12 | custom fusion | bytes 4915712 | tf_op jit(solution)/shard_map/scatter | solution.py:77
  305.5 4.7 all-to-all-start.2
  310.6 3.6 fusion.21
  314.2 1.8 fusion.23
  316.1 113.7 %all-to-all-done.2 = bf16[8,1200,256]{2,1,0:T(8,128)(2,1)} async-done(((bf16[8,1200,256]{2,1,0:T(8,128)(2,1)}), bf16[8,1200,256]{2,1,0:T(8,128)(2,1)}, u32[]{:S(2)}, u32[]{:S(2)}) %all-to-all-start.2) | async-done | bytes 4915232 | tf_op jit(solution)/shard_map/all_to_all | solution.py:80
  429.8 64.6 %scatter_custom_fusion.2 = f32[6144,256]{1,0:T(8,128)} fusion(s32[9600]{0:T(1024)S(1)} %reshape.243, bf16[9600,256]{1,0:T(8,128)(2,1)} %bitcast.23, f32[]{:T(128)} %constant.73.clone.1), kind=kCustom, calls=%fused_computation.5 | custom fusion | flops 4915200 | bytes 11206660 | tf_op jit(solution)/shard_map/scatter-add | solution.py:140
  494.3 3.1 convert_element_type.64
  497.4 3.1 copy.54
  500.6 40.0 %all-reduce.9 = (f32[256]{0:T(256)S(1)}, f32[256]{0:T(256)S(1)}) all-reduce(f32[256]{0:T(256)S(1)} %get-tuple-element.38, f32[256]{0:T(256)S(1)} %get-tuple-element.36), channel_id=1, replica_groups=mesh['dp'=4,'table'=8] {'dp','table'}, use_global_device_ids=true, to_apply=%region_16.17 | all-reduce | flops 512 | bytes 4096 | tf_op jit(solution)/shard_map/psum | solution.py:146
  541.7 2.2 broadcast_multiply_fusion.1
  544.9 1.3 reduce-scatter.4.cloned.1.call-done
  546.2 1.4 bitcast_convert_fusion
  (100 shorter events, 24.0 us)
Async XLA Ops:
  8.0 51.8 %copy-start = (bf16[3,2048,256]{2,1,0:T(8,128)(2,1)S(1)}, bf16[3,2048,256]{2,1,0:T(8,128)(2,1)}, u32[]{:S(2)}) copy-start(bf16[3,2048,256]{2,1,0:T(8,128)(2,1)} %param.10) | copy-start | bytes 9437188
  8.9 6.5 %copy-start.18 = (s32[8,200,3]{1,0,2:T(8,128)S(1)}, s32[8,200,3]{1,0,2:T(8,128)}, u32[]{:S(2)}) copy-start(s32[8,200,3]{1,0,2:T(8,128)} %param.9) | copy-start | bytes 57604
  22.3 2.4 copy-start.17
  98.0 114.3 %all-to-all-start.1 = ((bf16[8,1200,256]{2,1,0:T(8,128)(2,1)}), bf16[8,1200,256]{2,1,0:T(8,128)(2,1)}, u32[]{:S(2)}, u32[]{:S(2)}) async-start(bf16[8,1200,256]{2,1,0:T(8,128)(2,1)} %select_select_fusion), calls=%async_computation.1 | async-start | bytes 9830400 | tf_op jit(solution)/shard_map/all_to_all | solution.py:109
  243.0 1.0 copy-start.16
  243.4 1.6 copy-start.8
  243.4 1.6 copy-start.10
  245.0 0.7 copy-start.19
  246.8 2.2 copy-start.6
  246.8 1.3 copy-start.15
  247.2 1.8 copy-start.12
  247.2 1.8 copy-start.13
  249.0 1.1 copy-start.7
  249.0 1.1 copy-start.20
  255.1 0.9 copy-start.2
  260.7 0.9 copy-start.4
  305.5 5.1 copy-start.3
  305.5 124.3 %all-to-all-start.2 = ((bf16[8,1200,256]{2,1,0:T(8,128)(2,1)}), bf16[8,1200,256]{2,1,0:T(8,128)(2,1)}, u32[]{:S(2)}, u32[]{:S(2)}) async-start(bf16[8,1200,256]{2,1,0:T(8,128)(2,1)} %bitcast.61), calls=%async_computation.2 | async-start | bytes 9830400 | tf_op jit(solution)/shard_map/all_to_all | solution.py:80
  310.2 3.9 copy-start.5
  310.3 231.5 %all-reduce.13.cloned.1.call-start = ((), (), s32[]{:S(2)}) async-start(), calls=%async_computation.5 | async-start | bytes 3145728 | tf_op jit(solution)/shard_map/psum | solution.py:146
  310.6 3.6 copy-start.9
  310.6 3.6 copy-start.11
  316.0 230.2 %reduce-scatter.4.cloned.1.call-start = ((), (), s32[]{:S(2)}) async-start(), calls=%async_computation.4 | async-start | bytes 3932160
  541.7 2.2 copy-start.14
  546.2 2.6 copy-start.1
Sparse Core Ops, SparseCore 0:
  317.1 172.8 all-reduce.12
Sparse Core Ops, SparseCore 1:
  500.7 45.5 reduce-scatter.3
where the time goes:
time: 563 us; the launch traced here: 557 us
  waiting for transfers between devices  223 us (40%)
  local copies, waits for them, and re-layouts  133 us (24%)
  other arithmetic  114 us (20%)
  blocking collectives  51.9 us (9%)
  between operations  16.4 us (3%)
  starting transfers between devices  9.88 us (2%)
  matrix products  8.87 us (2%)
    all_to_all x1, waiting for transfers between devices, to_owners(): lax.all_to_all(outgoing, 'table', split_axis=0, concat_axis=0, tiled=True)  114 us
    all_to_all x1, waiting for transfers between devices, on_device(): lax.all_to_all(found_rows, 'table', split_axis=0, concat_axis=0, tiled=True)  108 us
    scatter-add x1, other arithmetic, on_device(): dense_grad = jnp.zeros((3 * rows_dev, width), jnp.float32).at[jnp.maximum...  64.6 us
    psum x1, blocking collectives, on_device(): lax.psum((first_weights, second_weights, first_gains, second_gains), ('dp...  40 us
    scatter x1, local copies, waits for them, and re-layouts, to_owners(): outgoing = jnp.zeros((shards * slot_count, width), jnp.bfloat16).at[slot_...  28.4 us
    gather x1, local copies, waits for them, and re-layouts, on_device(): found_rows = jnp.take(table_flat, jnp.maximum(asked_rows, 0), axis=0)  27.7 us
    scatter x1, local copies, waits for them, and re-layouts, on_device(): requests = jnp.full((shards * slot_count,), -1, jnp.int32).at[slot_place]...  22.8 us
    gather x2, local copies, waits for them, and re-layouts, on_device(): jnp.take(sent_back.reshape(shards * slot_count, width), slot_place, axis=0)  17.6 us
  transfers between devices with their start and end apart: 4, of which 3 were waited for; matrix products, arithmetic and copies ran while one was open for 15% of the time, Pallas kernels for 0%

commit v1 on v0

--- a/solution.py
+++ b/solution.py
@@ -3,10 +3,16 @@
 import jax
 import jax.numpy as jnp
 from jax import lax
+from jax.experimental import pallas as pl
+from jax.experimental.pallas import tpu as pltpu
 from jax.sharding import PartitionSpec as P
 
 GELU_C = 0.7978845608028654
 GELU_K = 0.044715
+LANES = 128
+MIB = 2**20
+CHAINS = 4
+UNROLL = 4
 
 
 def shifted(values, spacing):
@@ -80,7 +86,7 @@
     return lax.all_to_all(outgoing, "table", split_axis=0, concat_axis=0, tiled=True)
 
 
-def on_device(shard_of, offsets, table, weight_one, gain_one, weight_two, gain_two, grad_out):
+def padded_plan(shard_of, offsets, table, weight_one, gain_one, weight_two, gain_two, grad_out):
     sessions, length, _ = shard_of.shape
     width = table.shape[2]
     rows_dev = table.shape[1]
@@ -154,6 +160,454 @@
     )
 
 
+VMEM = pl.BlockSpec(memory_space=pltpu.VMEM)
+
+
+def columns_fit(items_shape, table_shape, groups, shards):
+    sessions, length, _ = items_shape
+    _, rows_dev, width = table_shape
+    run = 2 * length
+    return (
+        2 * width == groups * LANES
+        and groups % 2 == 0
+        and shards % 2 == 0
+        and shards >= 4
+        and sessions % 4 == 0
+        and run % 16 == 0
+        and (groups * sessions * length // 2) % (CHAINS * UNROLL) == 0
+        and rows_dev % 32 == 0
+        and CHAINS * shards * rows_dev * LANES * 4 <= 40 * MIB
+    )
+
+
+def low_lanes(rows):
+    return lax.broadcasted_iota(jnp.int32, (rows, LANES), 1) < LANES // 2
+
+
+def swap_halves(values):
+    return pltpu.roll(values, LANES // 2, 1)
+
+
+def own_columns(me, table):
+    tables, rows_dev, _ = table.shape
+    half = rows_dev // 2
+
+    def kernel(me_ref, table_ref, *out_refs):
+        odd = me_ref[0] % 2 == 1
+        low = low_lanes(half)
+        for t, out_ref in enumerate(out_refs):
+            top = table_ref[t, :half, :].astype(jnp.float32)
+            bottom = table_ref[t, half:, :].astype(jnp.float32)
+            in_low = jnp.where(odd, swap_halves(top), top)
+            in_high = jnp.where(odd, bottom, swap_halves(bottom))
+            out_ref[...] = jnp.where(low, in_low, in_high).astype(jnp.bfloat16)
+
+    return pl.pallas_call(
+        kernel,
+        grid_spec=pltpu.PrefetchScalarGridSpec(
+            num_scalar_prefetch=1,
+            grid=(1,),
+            in_specs=[pl.BlockSpec((tables, rows_dev, LANES), lambda i, m: (0, 0, m[0] // 2))],
+            out_specs=[pl.BlockSpec((half, LANES), lambda i, m: (0, 0))] * tables,
+        ),
+        out_shape=[jax.ShapeDtypeStruct((half, LANES), jnp.bfloat16)] * tables,
+        compiler_params=pltpu.CompilerParams(vmem_limit_bytes=24 * MIB),
+        name="own_columns",
+    )(me, table)
+
+
+def look_up(codes, slots, total, last):
+    count = codes[0].shape[0]
+    half = slots[0].shape[0]
+
+    def kernel(low_ref, high_ref, *refs):
+        slot_refs, refs = refs[: len(slots)], refs[len(slots) :]
+        total_ref = None if total is None else refs[0]
+        out_ref, rows, found = refs[-3:]
+        for s, slot_ref in enumerate(slot_refs):
+            values = slot_ref[...].astype(jnp.float32)
+            rows[pl.ds(2 * s * half, half), :] = values
+            rows[pl.ds((2 * s + 1) * half, half), :] = swap_halves(values)
+        low = low_lanes(1)
+
+        def some(step, carry):
+            for j in range(16):
+                i = step * 16 + j
+                for_low = rows[pl.ds(low_ref[i], 1), :]
+                for_high = rows[pl.ds(high_ref[i], 1), :]
+                found[pl.ds(i, 1), :] = jnp.where(low, for_low, for_high)
+            return carry
+
+        lax.fori_loop(0, count // 16, some, 0)
+        result = found[...]
+        if total_ref is not None:
+            result = result + total_ref[...]
+        out_ref[...] = result.astype(out_ref.dtype)
+
+    operands = list(slots) + ([] if total is None else [total])
+    return pl.pallas_call(
+        kernel,
+        grid_spec=pltpu.PrefetchScalarGridSpec(
+            num_scalar_prefetch=2,
+            grid=(),
+            in_specs=[VMEM] * len(operands),
+            out_specs=VMEM,
+            scratch_shapes=[
+                pltpu.VMEM((2 * len(slots) * half, LANES), jnp.float32),
+                pltpu.VMEM((count, LANES), jnp.float32),
+            ],
+        ),
+        out_shape=jax.ShapeDtypeStruct((count, LANES), jnp.bfloat16 if last else jnp.float32),
+        compiler_params=pltpu.CompilerParams(vmem_limit_bytes=32 * MIB),
+        cost_estimate=pl.CostEstimate(
+            flops=0, bytes_accessed=8 * 3 * count * LANES * 4, transcendentals=0
+        ),
+        name="look_up",
+    )(*codes, *operands)
+
+
+def add_rows(codes, blocks, shards, half):
+    count = codes[0].shape[0]
+    per = blocks[0].shape[0]
+    planes = shards // 2
+    share = count // CHAINS
+
+    def kernel(low_ref, high_ref, *refs):
+        block_refs, refs = refs[: len(blocks)], refs[len(blocks) :]
+        near_ref, far_ref, values, *sums = refs
+        for k, block_ref in enumerate(block_refs):
+            values[pl.ds(k * per, per), :] = block_ref[...].astype(jnp.float32)
+        for part in sums:
+            part[...] = jnp.zeros_like(part)
+        low = low_lanes(1)
+        high = jnp.logical_not(low)
+
+        def some(step, carry):
+            for j in range(UNROLL):
+                ready = []
+                for k, part in enumerate(sums):
+                    i = k * share + step * UNROLL + j
+                    value = values[pl.ds(i, 1), :]
+                    to_low, to_high = pl.ds(low_ref[i], 1), pl.ds(high_ref[i], 1)
+                    ready.append((to_low, part[to_low, :] + value, to_high, part[to_high, :] + value))
+                for part, (to_low, in_low, to_high, in_high) in zip(sums, ready):
+                    pltpu.store(part.at[to_low, :], in_low, mask=low)
+                    pltpu.store(part.at[to_high, :], in_high, mask=high)
+            return carry
+
+        lax.fori_loop(0, share // UNROLL, some, 0)
+        for s in range(shards):
+            straight = sum(part[pl.ds(2 * s * half, half), :] for part in sums)
+            crossed = sum(part[pl.ds((2 * s + 1) * half, half), :] for part in sums)
+            result = (straight + swap_halves(crossed)).astype(jnp.bfloat16)
+            if s < planes:
+                near_ref[s] = result
+            else:
+                far_ref[s - planes] = result
+
+    return pl.pallas_call(
+        kernel,
+        grid_spec=pltpu.PrefetchScalarGridSpec(
+            num_scalar_prefetch=2,
+            grid=(),
+            in_specs=[VMEM] * len(blocks),
+            out_specs=[VMEM] * 2,
+            scratch_shapes=[pltpu.VMEM((count, LANES), jnp.float32)]
+            + [pltpu.VMEM((2 * shards * half, LANES), jnp.float32)] * CHAINS,
+        ),
+        out_shape=[jax.ShapeDtypeStruct((planes, half, LANES), jnp.bfloat16)] * 2,
+        compiler_params=pltpu.CompilerParams(vmem_limit_bytes=56 * MIB),
+        cost_estimate=pl.CostEstimate(
+            flops=0, bytes_accessed=12 * 3 * count * LANES * 4, transcendentals=0
+        ),
+        name="add_rows",
+    )(*codes, *blocks)
+
+
+def both_layers(me, blocks, weight_one, gain_one, weight_two, gain_two, grad_out, length):
+    groups = len(blocks)
+    items, width = grad_out.shape
+    run = 2 * length
+    steps = items // (2 * run)
+    tall = weight_one.shape[0]
+    chunk = -(-(2 * tall + 16) // (32 * groups)) * 32
+
+    def kernel(me_ref, *refs):
+        block_refs, refs = refs[:groups], refs[groups:]
+        w_one_ref, g_one_ref, w_two_ref, g_two_ref, top_ref, out_ref, *refs = refs
+        grad_refs, weight_refs, refs = refs[:groups], refs[groups : 2 * groups], refs[2 * groups :]
+        held, packed, sum_one, sum_two, sum_gains, flat = refs
+        step = pl.program_id(0)
+        me_at = me_ref[0]
+        low = low_lanes(run)
+        place = lax.broadcasted_iota(jnp.int32, (run, width), 0)
+        place = jnp.where(place >= length, place - length, place)
+
+        @pl.when(step == 0)
+        def _():
+            sum_one[...] = jnp.zeros_like(sum_one)
+            sum_two[...] = jnp.zeros_like(sum_two)
+            sum_gains[...] = jnp.zeros_like(sum_gains)
+
+        def taps(values, gap):
+            one = jnp.where(place >= gap, pltpu.roll(values, gap, 0), 0.0)
+            two = jnp.where(place >= 2 * gap, pltpu.roll(values, 2 * gap, 0), 0.0)
+            return jnp.concatenate([x.astype(jnp.bfloat16) for x in (values, one, two)], axis=1)
+
+        def untaps(values, gap):
+            one = jnp.where(place < length - gap, pltpu.roll(values, run - gap, 0), 0.0)
+            two = jnp.where(place < length - 2 * gap, pltpu.roll(values, run - 2 * gap, 0), 0.0)
+            return [x.astype(jnp.bfloat16) for x in (values, one, two)]
+
+        def forward(values, weight_ref, gain, gap):
+            before = jnp.dot(taps(values, gap), weight_ref[...], preferred_element_type=jnp.float32)
+            centred = before - jnp.mean(before, axis=-1, keepdims=True)
+            inv_std = lax.rsqrt(jnp.mean(centred * centred, axis=-1, keepdims=True) + 1e-05)
+            normal = centred * inv_std
+            output, slope = gelu_parts(normal * gain)
+            return output, (normal, inv_std, slope)
+
+        def backward(grad, values, weight_ref, gain, saved, gap, total, row):
+            normal, inv_std, slope = saved
+            scaled = grad * slope
+            sum_gains[pl.ds(row, 1), :] += jnp.sum(scaled * normal, axis=0, keepdims=True)
+            back = scaled * gain
+            before = inv_std * (
+                back
+                - jnp.mean(back, axis=-1, keepdims=True)
+                - normal * jnp.mean(back * normal, axis=-1, keepdims=True)
+            )
+            parts = untaps(before.astype(jnp.bfloat16).astype(jnp.float32), gap)
+            total[...] += lax.dot_general(
+                values.astype(jnp.bfloat16),
+                jnp.concatenate(parts, axis=1),
+                (((0,), (0,)), ((), ())),
+                preferred_element_type=jnp.float32,
+            )
+            return sum(
+                lax.dot_general(
+                    part,
+                    weight_ref[k * width : (k + 1) * width, :],
+                    (((1,), (1,)), ((), ())),
+                    preferred_element_type=jnp.float32,
+                )
+                for k, part in enumerate(parts)
+            )
+
+        for k in range(groups):
+            held[k] = block_refs[k][...].astype(jnp.float32)
+        gain_one_at, gain_two_at = g_one_ref[...], g_two_ref[...]
+        back_to = []
+        for side in range(2):
+            columns = []
+            for q in range(0, groups, 2):
+                left = held[(q - me_at + groups) % groups]
+                right = held[(q + 1 - me_at + groups) % groups]
+                if side == 0:
+                    columns.append(jnp.where(low, left, swap_halves(right)))
+                else:
+                    columns.append(jnp.where(low, swap_halves(left), right))
+            embedded = jnp.concatenate(columns, axis=1)
+            rows = pl.ds(side * run, run)
+            top = top_ref[rows, :].astype(jnp.float32)
+            act_one, saved_one = forward(embedded, w_one_ref, gain_one_at, 1)
+            hidden = act_one.astype(jnp.bfloat16).astype(jnp.float32)
+            act_two, saved_two = forward(hidden, w_two_ref, gain_two_at, 2)
+            out_ref[rows, :] = (embedded + act_two).astype(jnp.bfloat16)
+            grad_hidden = backward(top, hidden, w_two_ref, gain_two_at, saved_two, 2, sum_two, 1)
+            grad_inner = backward(grad_hidden, embedded, w_one_ref, gain_one_at, saved_one, 1, sum_one, 0)
+            back_to.append(top + grad_inner)
+        for q in range(groups):
+            at = slice((q // 2) * LANES, (q // 2 + 1) * LANES)
+            first, second = back_to[0][:, at], back_to[1][:, at]
+            if q % 2 == 0:
+                pair = jnp.where(low, first, swap_halves(second))
+            else:
+                pair = jnp.where(low, swap_halves(first), second)
+            packed[(q - me_at + groups) % groups] = pair
+        for k in range(groups):
+            grad_refs[k][...] = packed[k].astype(jnp.bfloat16)
+
+        @pl.when(step == steps - 1)
+        def _():
+            for n, total in enumerate((sum_one, sum_two)):
+                for k in range(tall // width):
+                    flat[n * tall + k * width : n * tall + (k + 1) * width, :] = total[
+                        :, k * width : (k + 1) * width
+                    ].astype(jnp.bfloat16)
+            flat[2 * tall : 2 * tall + 16, :] = jnp.concatenate(
+                [sum_gains[...], jnp.zeros_like(sum_gains)], axis=0
+            ).astype(jnp.bfloat16)
+            if groups * chunk > 2 * tall + 16:
+                flat[2 * tall + 16 :, :] = jnp.zeros(
+                    (groups * chunk - 2 * tall - 16, width), jnp.bfloat16
+                )
+            for k in range(groups):
+                begin = pl.multiple_of(((me_at + k) % groups) * chunk, 32)
+                weight_refs[k][...] = flat[pl.ds(begin, chunk), :]
+
+    def whole(shape):
+        return pl.BlockSpec(shape, lambda j, m: (0, 0))
+
+    def by_step(rows, columns):
+        return pl.BlockSpec((rows, columns), lambda j, m: (j, 0))
+
+    return pl.pallas_call(
+        kernel,
+        grid_spec=pltpu.PrefetchScalarGridSpec(
+            num_scalar_prefetch=1,
+            grid=(steps,),
+            in_specs=[by_step(run, LANES)] * groups
+            + [whole((tall, width)), whole((1, width))] * 2
+            + [by_step(2 * run, width)],
+            out_specs=[by_step(2 * run, width)]
+            + [by_step(run, LANES)] * groups
+            + [whole((chunk, width))] * groups,
+            scratch_shapes=[
+                pltpu.VMEM((groups, run, LANES), jnp.float32),
+                pltpu.VMEM((groups, run, LANES), jnp.float32),
+                pltpu.VMEM((width, tall), jnp.float32),
+                pltpu.VMEM((width, tall), jnp.float32),
+                pltpu.VMEM((8, width), jnp.float32),
+                pltpu.VMEM((groups * chunk, width), jnp.bfloat16),
+            ],
+        ),
+        out_shape=[jax.ShapeDtypeStruct((items, width), jnp.bfloat16)]
+        + [jax.ShapeDtypeStruct((items // 2, LANES), jnp.bfloat16)] * groups
+        + [jax.ShapeDtypeStruct((chunk, width), jnp.bfloat16)] * groups,
+        compiler_params=pltpu.CompilerParams(vmem_limit_bytes=48 * MIB),
+        name="both_layers",
+    )(
+        me,
+        *blocks,
+        weight_one,
+        gain_one.reshape(1, width),
+        weight_two,
+        gain_two.reshape(1, width),
+        grad_out,
+    )
+
+
+def column_plan(shard_of, offsets, table, weight_one, gain_one, weight_two, gain_two, grad_out):
+    sessions, length, _ = shard_of.shape
+    tables, rows_dev, width = table.shape
+    items = sessions * length
+    groups = lax.axis_size("dp")
+    shards = lax.axis_size("table")
+    planes = shards // 2
+    half = rows_dev // 2
+    run = 2 * length
+    me = lax.axis_index("dp")
+    plane, core = lax.axis_index("table") // 2, lax.axis_index("table") % 2
+    me_at = me.astype(jnp.int32).reshape(1)
+
+    def dp_shift(values, k):
+        return lax.ppermute(values, "dp", [(i, (i + k) % groups) for i in range(groups)])
+
+    def up(values):
+        return lax.ppermute(values, "table", [(i, (i + 2) % shards) for i in range(shards)])
+
+    def down(values):
+        return lax.ppermute(values, "table", [(i, (i - 2) % shards) for i in range(shards)])
+
+    def across(values):
+        return lax.ppermute(values, "table", [(i, i ^ 1) for i in range(shards)])
+
+    slot = (shard_of + core) % 2 * planes + (shard_of // 2 - plane + planes) % planes
+    places = jnp.stack(
+        [slot * rows_dev + offsets, slot * rows_dev + (offsets + half) % rows_dev], axis=0
+    ).astype(jnp.int32)
+    places = places.reshape(2, items // (2 * run), 2, run, tables)
+    mine = jnp.stack([places[0, :, 0], places[1, :, 1]], axis=0)
+    mine = jnp.transpose(mine, (3, 0, 1, 2)).reshape(tables, 2, items // 2)
+    all_codes = jnp.concatenate([mine] + [dp_shift(mine, k) for k in range(1, groups)], axis=2)
+    codes = [(all_codes[t, 0], all_codes[t, 1]) for t in range(tables)]
+
+    total = None
+    for t, own in enumerate(own_columns(me_at, table)):
+        near = [None] * planes
+        near[0] = rising = falling = own
+        for k in range(1, planes // 2 + 1):
+            near[planes - k] = rising = up(rising)
+            if k <= (planes - 1) // 2:
+                near[k] = falling = down(falling)
+        far = [across(values) for values in near]
+        total = look_up(codes[t], near + far, total, t == tables - 1)
+
+    pieces = total.reshape(groups, items // 2, LANES)
+    arrived = [pieces[0]] + [dp_shift(pieces[k], -k) for k in range(1, groups)]
+    done = both_layers(
+        me_at, arrived, weight_one, gain_one, weight_two, gain_two, grad_out.reshape(items, width), length
+    )
+    block_out = done[0].reshape(sessions, length, width)
+    sent, sums = done[1 : 1 + groups], done[1 + groups :]
+    blocks = [sent[0]] + [dp_shift(sent[k], k) for k in range(1, groups)]
+
+    grads = []
+    for t in range(tables):
+        near, far = add_rows(codes[t], blocks, shards, half)
+        got = across(far)
+
+        def both(r):
+            return near[r].astype(jnp.float32) + got[r].astype(jnp.float32)
+
+        result = both(0)
+        for move, order in (
+            (up, list(range(planes // 2, 0, -1))),
+            (down, list(range(planes // 2 + 1, planes))),
+        ):
+            moving = None
+            for r in order:
+                term = both(r)
+                if moving is not None:
+                    term = term + moving.astype(jnp.float32)
+                moving = move(term.astype(jnp.bfloat16))
+            if moving is not None:
+                result = result + moving.astype(jnp.float32)
+        grads.append(jnp.concatenate([result[:, : LANES // 2], result[:, LANES // 2 :]], axis=0))
+    table_grad = jnp.stack(grads, axis=0)
+
+    def add_up(parts):
+        return sum(part.astype(jnp.float32) for part in parts)
+
+    chunk = sums[0].shape[0]
+    mid = add_up([sums[0]] + [dp_shift(sums[k], k) for k in range(1, groups)]).astype(jnp.bfloat16)
+    kept = lax.dynamic_slice_in_dim(mid, core * (chunk // 2), chunk // 2, 0)
+    given = lax.dynamic_slice_in_dim(mid, (1 - core) * (chunk // 2), chunk // 2, 0)
+    by_plane = [None] * planes
+    by_plane[0] = rising = falling = add_up([kept, across(given)]).astype(jnp.bfloat16)
+    for k in range(1, planes // 2 + 1):
+        by_plane[planes - k] = rising = up(rising)
+        if k <= (planes - 1) // 2:
+            by_plane[k] = falling = down(falling)
+    stacked = jnp.stack(by_plane, axis=0)
+    kept = add_up(
+        [
+            lax.dynamic_index_in_dim(stacked, (a - plane + planes) % planes, 0, keepdims=False)
+            for a in range(planes)
+        ]
+    ).astype(jnp.bfloat16)
+    given = across(kept)
+    mid = jnp.where(core == 0, jnp.concatenate([kept, given]), jnp.concatenate([given, kept]))
+    stacked = jnp.stack([mid] + [dp_shift(mid, k) for k in range(1, groups)], axis=0)
+    sums = jnp.concatenate(
+        [
+            lax.dynamic_index_in_dim(stacked, (me - a + groups) % groups, 0, keepdims=False)
+            for a in range(groups)
+        ],
+        axis=0,
+    ).astype(jnp.float32) * (1.0 / math.sqrt(items * groups * shards))
+    tall = weight_one.shape[0]
+    return (
+        block_out,
+        sums[:tall],
+        sums[tall : 2 * tall],
+        sums[2 * tall],
+        sums[2 * tall + 1],
+        table_grad,
+    )
+
+
 def solution(mesh):
     placed = (
         P(("dp", "table"), None, None),
@@ -165,6 +619,12 @@
         P(),
         P(("dp", "table"), None, None),
     )
+
+    def on_device(shard_of, offsets, table, *rest):
+        fits = columns_fit(shard_of.shape, table.shape, mesh.shape["dp"], mesh.shape["table"])
+        plan = column_plan if fits else padded_plan
+        return plan(shard_of, offsets, table, *rest)
+
     return jax.shard_map(
         on_device,
         mesh=mesh,

time: 563 us -> 257 us (0.46); the launches traced: 557 us -> 256 us
  local copies, waits for them, and re-layouts: 133 us -> 13 us
  waiting for transfers between devices: 223 us -> 103 us
  other arithmetic: 114 us -> 2.36 us
  Pallas kernels: 0 us -> 74.8 us
  starting transfers between devices: 9.88 us -> 62 us
  blocking collectives: 51.9 us -> 0 us
  between operations: 16.4 us -> 1.39 us
  matrix products: 8.87 us -> 0 us
    all_to_all x2 -> x0, waiting for transfers between devices: 222 us -> none  [the longest x1 114 us: to_owners(): lax.all_to_all(outgoing, 'table', split_axis=0, concat_axis=0, tiled=True)]
    ppermute x0 -> x53, waiting for transfers between devices: none -> 103 us  [the longest x14 55.9 us: up(): lax.ppermute(values, 'table', [(i, (i + 2) % shards) for i in range(shard...]
    pallas_call x0 -> x8, Pallas kernels: none -> 74.8 us  [the longest x3 38.7 us: add_rows(): pl.pallas_call(kernel, grid_spec=pltpu.PrefetchScalarGridSpec(num_scalar_...]
    scatter-add x1 -> x0, other arithmetic: 64.6 us -> none  [on_device(): dense_grad = jnp.zeros((3 * rows_dev, width), jnp.float32).at[jnp.maximum...]
    ppermute x0 -> x53, starting transfers between devices: none -> 62 us  [the longest x7 25.8 us: down(): lax.ppermute(values, 'table', [(i, (i - 2) % shards) for i in range(shard...]
    scatter x2 -> x0, local copies, waits for them, and re-layouts: 51.3 us -> none  [the longest x1 28.4 us: to_owners(): outgoing = jnp.zeros((shards * slot_count, width), jnp.bfloat16).at[slot_...]
    gather x3 -> x0, local copies, waits for them, and re-layouts: 45.3 us -> none  [the longest x1 27.7 us: on_device(): found_rows = jnp.take(table_flat, jnp.maximum(asked_rows, 0), axis=0)]
    psum x1 -> x0, blocking collectives: 40 us -> none  [on_device(): lax.psum((first_weights, second_weights, first_gains, second_gains), ('dp...]
  transfers between devices with their start and end apart: 4 -> 53, of which waited for: 3 -> 24; matrix products, arithmetic and copies ran while one was open for 15% -> 2% of each run, Pallas kernels for 0% -> 21%
where the time goes in v1:
time: 257 us; the launch traced here: 256 us
  waiting for transfers between devices  103 us (40%)
  Pallas kernels  74.8 us (29%)
  starting transfers between devices  62 us (24%)
  local copies, waits for them, and re-layouts  13 us (5%)
    ppermute x14, waiting for transfers between devices, up(): lax.ppermute(values, 'table', [(i, (i + 2) % shards) for i in range(shard...  55.9 us
    pallas_call x3, Pallas kernels, add_rows(): pl.pallas_call(kernel, grid_spec=pltpu.PrefetchScalarGridSpec(num_scalar_...  38.7 us
    ppermute x15, waiting for transfers between devices, dp_shift(): lax.ppermute(values, 'dp', [(i, (i + k) % groups) for i in range(groups)])  29.4 us
    ppermute x7, starting transfers between devices, down(): lax.ppermute(values, 'table', [(i, (i - 2) % shards) for i in range(shard...  25.8 us
    pallas_call x3, Pallas kernels, look_up(): pl.pallas_call(kernel, grid_spec=pltpu.PrefetchScalarGridSpec(num_scalar_...  22.5 us
    ppermute x15, starting transfers between devices, dp_shift(): lax.ppermute(values, 'dp', [(i, (i + k) % groups) for i in range(groups)])  19.2 us
    ppermute x7, waiting for transfers between devices, down(): lax.ppermute(values, 'table', [(i, (i - 2) % shards) for i in range(shard...  16.2 us
    ppermute x14, starting transfers between devices, up(): lax.ppermute(values, 'table', [(i, (i + 2) % shards) for i in range(shard...  14.6 us
  transfers between devices with their start and end apart: 53, of which 24 were waited for; matrix products, arithmetic and copies ran while one was open for 2% of the time, Pallas kernels for 21%

profile of v1, /device:TPU:0, one launch (start us, length us, event | category | flops | bytes accessed | tf_op | source)
XLA Modules:
  0.0 256.4 jit_solution(7743382930242956238)
XLA Ops:
  3.3 3.1 %collective-permute-start.18 = (bf16[1024,128]{1,0:T(8,128)(2,1)S(1)}, bf16[1024,128]{1,0:T(8,128)(2,1)S(1)}, u32[]{:S(2)}, u32[]{:S(2)}) collective-permute-start(bf16[1024,128]{1,0:T(8,128)(2,1)S(1)} %get-tuple-element.26.refs_0_), channel_id=1, source_target_pairs={{0,2},{1,3},{2,4},{3,5},{4,6},{5,7},{6,0},{7,1},{8,10},{9,11},{10,... | collective-permute-start | bytes 786440 | tf_op jit(solution)/shard_map/ppermute | solution.py:508
  13.7 3.7 %collective-permute-start.10 = (bf16[1024,128]{1,0:T(8,128)(2,1)S(1)}, bf16[1024,128]{1,0:T(8,128)(2,1)S(1)}, u32[]{:S(2)}, u32[]{:S(2)}) collective-permute-start(bf16[1024,128]{1,0:T(8,128)(2,1)S(1)} %get-tuple-element.25.refs_0_), channel_id=1, source_target_pairs={{0,6},{1,7},{2,0},{3,1},{4,2},{5,3},{6,4},{7,5},{8,14},{9,15},{10,... | collective-permute-start | bytes 786440 | tf_op jit(solution)/shard_map/ppermute | solution.py:511
  17.4 6.9 %collective-permute-done.17.refs_1_ = bf16[1024,128]{1,0:T(8,128)(2,1)S(1)} collective-permute-done((bf16[1024,128]{1,0:T(8,128)(2,1)S(1)}, bf16[1024,128]{1,0:T(8,128)(2,1)S(1)}, u32[]{:S(2)}, u32[]{:S(2)}) %collective-permute-start.17) | collective-permute-done | bytes 262176 | tf_op jit(solution)/shard_map/ppermute | solution.py:511
  29.2 4.5 %collective-permute-done.10.refs_1_ = bf16[1024,128]{1,0:T(8,128)(2,1)S(1)} collective-permute-done((bf16[1024,128]{1,0:T(8,128)(2,1)S(1)}, bf16[1024,128]{1,0:T(8,128)(2,1)S(1)}, u32[]{:S(2)}, u32[]{:S(2)}) %collective-permute-start.10) | collective-permute-done | bytes 262176 | tf_op jit(solution)/shard_map/ppermute | solution.py:511
  34.9 4.1 %collective-permute-done.4.refs_3_ = bf16[1024,128]{1,0:T(8,128)(2,1)S(1)} collective-permute-done((bf16[1024,128]{1,0:T(8,128)(2,1)S(1)}, bf16[1024,128]{1,0:T(8,128)(2,1)S(1)}, u32[]{:S(2)}, u32[]{:S(2)}) %collective-permute-start.4) | collective-permute-done | bytes 262176 | tf_op jit(solution)/shard_map/ppermute | solution.py:508
  39.7 4.8 %collective-permute-done.3.refs_1_ = bf16[1024,128]{1,0:T(8,128)(2,1)S(1)} collective-permute-done((bf16[1024,128]{1,0:T(8,128)(2,1)S(1)}, bf16[1024,128]{1,0:T(8,128)(2,1)S(1)}, u32[]{:S(2)}, u32[]{:S(2)}) %collective-permute-start.3) | collective-permute-done | bytes 262176 | tf_op jit(solution)/shard_map/ppermute | solution.py:511
  45.2 5.1 %collective-permute-done.19.refs_2_ = bf16[1024,128]{1,0:T(8,128)(2,1)S(1)} collective-permute-done((bf16[1024,128]{1,0:T(8,128)(2,1)S(1)}, bf16[1024,128]{1,0:T(8,128)(2,1)S(1)}, u32[]{:S(2)}, u32[]{:S(2)}) %collective-permute-start.19) | collective-permute-done | bytes 262176 | tf_op jit(solution)/shard_map/ppermute | solution.py:508
  56.1 5.4 %collective-permute-done.5.refs_2_ = bf16[1024,128]{1,0:T(8,128)(2,1)S(1)} collective-permute-done((bf16[1024,128]{1,0:T(8,128)(2,1)S(1)}, bf16[1024,128]{1,0:T(8,128)(2,1)S(1)}, u32[]{:S(2)}, u32[]{:S(2)}) %collective-permute-start.5) | collective-permute-done | bytes 262176 | tf_op jit(solution)/shard_map/ppermute | solution.py:508
  63.3 6.8 %look_up.3.refs_8_ = f32[3200,128]{1,0:T(8,128)S(1)} custom-call(s32[3200]{0:T(1024)S(1)} %get-tuple-element.55.low_ref, s32[3200]{0:T(1024)S(1)} %get-tuple-element.54.high_ref, bf16[1024,128]{1,0:T(8,128)(2,1)S(1)} %get-tuple-element.26.refs_0_, bf16[1024,128]{1,0:T(8,128)(2,1)S(1)} %collective-permute-done.17.refs_1_, ...), custom_call_target="tpu_custom_call" | custom-call | bytes 39321600 | tf_op jit(solution)/shard_map/look_up/pallas_call | solution.py:248
  70.1 7.8 %look_up.4.refs_8_ = f32[3200,128]{1,0:T(8,128)S(1)} custom-call(s32[3200]{0:T(1024)S(1)} %get-tuple-element.57.low_ref, s32[3200]{0:T(1024)S(1)} %get-tuple-element.56.high_ref, bf16[1024,128]{1,0:T(8,128)(2,1)S(1)} %copy-done.6, bf16[1024,128]{1,0:T(8,128)(2,1)S(1)} %copy-done.10, bf16[1024,128]{1,0:T(8,128)(2,1)} %collective-permute-done.12.refs_2_, ...), custom_call_target="tpu_custom_call" | custom-call | bytes 39321600 | tf_op jit(solution)/shard_map/look_up/pallas_call | solution.py:248
  78.1 7.9 %look_up.5 = bf16[3200,128]{1,0:T(8,128)(2,1)S(1)} custom-call(s32[3200]{0:T(1024)S(1)} %get-tuple-element.59.low_ref, s32[3200]{0:T(1024)S(1)} %get-tuple-element.58.high_ref, bf16[1024,128]{1,0:T(8,128)(2,1)S(1)} %get-tuple-element.24.refs_0_, bf16[1024,128]{1,0:T(8,128)(2,1)S(1)} %collective-permute-done.3.refs_1_, ...), custom_call_target="tpu_custom_call" | custom-call | bytes 39321600 | tf_op jit(solution)/shard_map/look_up/pallas_call | solution.py:248
  89.1 4.9 %collective-permute-done.24.refs_1_ = bf16[800,128]{1,0:T(8,128)(2,1)S(1)} collective-permute-done((bf16[800,128]{1,0:T(8,128)(2,1)S(1)}, bf16[800,128]{1,0:T(8,128)(2,1)S(1)}, u32[]{:S(2)}, u32[]{:S(2)}) %collective-permute-start.24) | collective-permute-done | bytes 204832 | tf_op jit(solution)/shard_map/ppermute | solution.py:505
  94.1 4.9 %collective-permute-done.25.refs_2_ = bf16[800,128]{1,0:T(8,128)(2,1)S(1)} collective-permute-done((bf16[800,128]{1,0:T(8,128)(2,1)S(1)}, bf16[800,128]{1,0:T(8,128)(2,1)S(1)}, u32[]{:S(2)}, u32[]{:S(2)}) %collective-permute-start.25) | collective-permute-done | bytes 204832 | tf_op jit(solution)/shard_map/ppermute | solution.py:505
  99.0 12.9 %both_layers.1 = (bf16[1600,256]{1,0:T(8,128)(2,1)}, bf16[800,128]{1,0:T(8,128)(2,1)S(1)}, bf16[800,128]{1,0:T(8,128)(2,1)S(1)}, bf16[800,128]{1,0:T(8,128)(2,1)...) custom-call(s32[1]{0:T(128)} %bitcast.me_ref, ...), custom_call_target="tpu_custom_call" | custom-call | tf_op jit(solution)/shard_map/both_layers/pallas_call | solution.py:455
  116.3 4.9 %collective-permute-done.27 = bf16[416,256]{1,0:T(8,128)(2,1)S(1)} collective-permute-done((bf16[416,256]{1,0:T(8,128)(2,1)S(1)}, bf16[416,256]{1,0:T(8,128)(2,1)S(1)}, u32[]{:S(2)}, u32[]{:S(2)}) %collective-permute-start.27) | collective-permute-done | bytes 213024 | tf_op jit(solution)/shard_map/ppermute | solution.py:505
  125.0 3.8 %collective-permute-start.31 = (bf16[208,256]{1,0:T(8,128)(2,1)S(1)}, bf16[208,256]{1,0:T(8,128)(2,1)S(1)}, u32[]{:S(2)}, u32[]{:S(2)}) collective-permute-start(bf16[208,256]{1,0:T(8,128)(2,1)S(1)} %add_convert_fusion.8), channel_id=1, source_target_pairs={{0,6},{1,7},{2,0},{3,1},{4,2},{5,3},{6,4},{7,5},{8,14},{9,15},{10,... | collective-permute-start | bytes 319496 | tf_op jit(solution)/shard_map/ppermute | solution.py:511
  128.8 3.8 %collective-permute-done.32 = bf16[208,256]{1,0:T(8,128)(2,1)S(1)} collective-permute-done((bf16[208,256]{1,0:T(8,128)(2,1)S(1)}, bf16[208,256]{1,0:T(8,128)(2,1)S(1)}, u32[]{:S(2)}, u32[]{:S(2)}) %collective-permute-start.32) | collective-permute-done | bytes 106528 | tf_op jit(solution)/shard_map/ppermute | solution.py:508
  144.1 13.0 %add_rows.3 = (bf16[4,1024,128]{2,1,0:T(8,128)(2,1)}, bf16[4,1024,128]{2,1,0:T(8,128)(2,1)}) custom-call(s32[3200]{0:T(1024)} %copy-done.22, s32[3200]{0:T(1024)} %copy-done.21, bf16[800,128]{1,0:T(8,128)(2,1)} %copy-done.1, bf16[800,128]{1,0:T(8,128)(2,1)} %copy-done.25, bf16[800,128]{1,0:T(8,128)(2,1)} %copy-done.26, bf16[800,128]{1,0:T(8,128)(2,1)} %copy-done.27), custom_call_target="tpu_custom_call" | custom-call | bytes 58982400 | tf_op jit(solution)/shard_map/add_rows/pallas_call | solution.py:308
  157.2 12.8 %add_rows.4 = (bf16[4,1024,128]{2,1,0:T(8,128)(2,1)}, bf16[4,1024,128]{2,1,0:T(8,128)(2,1)}) custom-call(s32[3200]{0:T(1024)} %copy-done.20, s32[3200]{0:T(1024)} %copy-done.19, bf16[800,128]{1,0:T(8,128)(2,1)} %copy-done.1, bf16[800,128]{1,0:T(8,128)(2,1)} %copy-done.25, bf16[800,128]{1,0:T(8,128)(2,1)} %copy-done.26, bf16[800,128]{1,0:T(8,128)(2,1)} %copy-done.27), custom_call_target="tpu_custom_call" | custom-call | bytes 58982400 | tf_op jit(solution)/shard_map/add_rows/pallas_call | solution.py:308
  170.5 12.8 %add_rows.5 = (bf16[4,1024,128]{2,1,0:T(8,128)(2,1)}, bf16[4,1024,128]{2,1,0:T(8,128)(2,1)}) custom-call(s32[3200]{0:T(1024)} %copy-done.18, s32[3200]{0:T(1024)} %copy-done.17, bf16[800,128]{1,0:T(8,128)(2,1)} %copy-done.1, bf16[800,128]{1,0:T(8,128)(2,1)} %copy-done.25, bf16[800,128]{1,0:T(8,128)(2,1)} %copy-done.26, bf16[800,128]{1,0:T(8,128)(2,1)} %copy-done.27), custom_call_target="tpu_custom_call" | custom-call | bytes 58982400 | tf_op jit(solution)/shard_map/add_rows/pallas_call | solution.py:308
  187.6 4.9 %collective-permute-done.35 = bf16[416,256]{1,0:T(8,128)(2,1)S(1)} collective-permute-done((bf16[416,256]{1,0:T(8,128)(2,1)S(1)}, bf16[416,256]{1,0:T(8,128)(2,1)S(1)}, u32[]{:S(2)}, u32[]{:S(2)}) %collective-permute-start.35) | collective-permute-done | bytes 213024 | tf_op jit(solution)/shard_map/ppermute | solution.py:505
  192.6 3.6 %collective-permute-done.36 = bf16[416,256]{1,0:T(8,128)(2,1)S(1)} collective-permute-done((bf16[416,256]{1,0:T(8,128)(2,1)S(1)}, bf16[416,256]{1,0:T(8,128)(2,1)S(1)}, u32[]{:S(2)}, u32[]{:S(2)}) %collective-permute-start.36) | collective-permute-done | bytes 213024 | tf_op jit(solution)/shard_map/ppermute | solution.py:505
  198.5 3.8 %collective-permute-start.44 = (bf16[1024,128]{1,0:T(8,128)(2,1)S(1)}, bf16[1024,128]{1,0:T(8,128)(2,1)S(1)}, u32[]{:S(2)}, u32[]{:S(2)}) collective-permute-start(bf16[1024,128]{1,0:T(8,128)(2,1)S(1)} %get-tuple-element.63), channel_id=1, source_target_pairs={{0,6},{1,7},{2,0},{3,1},{4,2},{5,3},{6,4},{7,5},{8,14},{9,15},{10,... | collective-permute-start | bytes 786440 | tf_op jit(solution)/shard_map/ppermute | solution.py:511
  202.5 3.8 %collective-permute-start.48 = (bf16[1024,128]{1,0:T(8,128)(2,1)S(1)}, bf16[1024,128]{1,0:T(8,128)(2,1)S(1)}, u32[]{:S(2)}, u32[]{:S(2)}) collective-permute-start(bf16[1024,128]{1,0:T(8,128)(2,1)S(1)} %get-tuple-element.65), channel_id=1, source_target_pairs={{0,6},{1,7},{2,0},{3,1},{4,2},{5,3},{6,4},{7,5},{8,14},{9,15},{10,... | collective-permute-start | bytes 786440 | tf_op jit(solution)/shard_map/ppermute | solution.py:511
  206.6 2.9 %collective-permute-done.42 = bf16[1024,128]{1,0:T(8,128)(2,1)S(1)} collective-permute-done((bf16[1024,128]{1,0:T(8,128)(2,1)S(1)}, bf16[1024,128]{1,0:T(8,128)(2,1)S(1)}, u32[]{:S(2)}, u32[]{:S(2)}) %collective-permute-start.42) | collective-permute-done | bytes 262176 | tf_op jit(solution)/shard_map/ppermute | solution.py:508
  209.5 7.3 %collective-permute-start.52 = (bf16[1024,128]{1,0:T(8,128)(2,1)S(1)}, bf16[1024,128]{1,0:T(8,128)(2,1)S(1)}, u32[]{:S(2)}, u32[]{:S(2)}) collective-permute-start(bf16[1024,128]{1,0:T(8,128)(2,1)S(1)} %get-tuple-element.67), channel_id=1, source_target_pairs={{0,6},{1,7},{2,0},{3,1},{4,2},{5,3},{6,4},{7,5},{8,14},{9,15},{10,... | collective-permute-start | bytes 786440 | tf_op jit(solution)/shard_map/ppermute | solution.py:511
  216.9 3.9 %collective-permute-done.46 = bf16[1024,128]{1,0:T(8,128)(2,1)S(1)} collective-permute-done((bf16[1024,128]{1,0:T(8,128)(2,1)S(1)}, bf16[1024,128]{1,0:T(8,128)(2,1)S(1)}, u32[]{:S(2)}, u32[]{:S(2)}) %collective-permute-start.46) | collective-permute-done | bytes 262176 | tf_op jit(solution)/shard_map/ppermute | solution.py:508
  220.9 11.2 %collective-permute-done.50 = bf16[1024,128]{1,0:T(8,128)(2,1)S(1)} collective-permute-done((bf16[1024,128]{1,0:T(8,128)(2,1)S(1)}, bf16[1024,128]{1,0:T(8,128)(2,1)S(1)}, u32[]{:S(2)}, u32[]{:S(2)}) %collective-permute-start.50) | collective-permute-done | bytes 262176 | tf_op jit(solution)/shard_map/ppermute | solution.py:508
  232.2 5.9 %collective-permute-start.51 = (bf16[1024,128]{1,0:T(8,128)(2,1)S(1)}, bf16[1024,128]{1,0:T(8,128)(2,1)S(1)}, u32[]{:S(2)}, u32[]{:S(2)}) collective-permute-start(bf16[1024,128]{1,0:T(8,128)(2,1)S(1)} %fusion), channel_id=1, source_target_pairs={{0,2},{1,3},{2,4},{3,5},{4,6},{5,7},{6,0},{7,1},{8,10},{9,11},{10,... | collective-permute-start | bytes 786440 | tf_op jit(solution)/shard_map/ppermute | solution.py:508
  238.1 5.2 %collective-permute-done.43 = bf16[1024,128]{1,0:T(8,128)(2,1)S(1)} collective-permute-done((bf16[1024,128]{1,0:T(8,128)(2,1)S(1)}, bf16[1024,128]{1,0:T(8,128)(2,1)S(1)}, u32[]{:S(2)}, u32[]{:S(2)}) %collective-permute-start.43) | collective-permute-done | bytes 262176 | tf_op jit(solution)/shard_map/ppermute | solution.py:508
  243.7 5.3 %collective-permute-done.47 = bf16[1024,128]{1,0:T(8,128)(2,1)S(1)} collective-permute-done((bf16[1024,128]{1,0:T(8,128)(2,1)S(1)}, bf16[1024,128]{1,0:T(8,128)(2,1)S(1)}, u32[]{:S(2)}, u32[]{:S(2)}) %collective-permute-start.47) | collective-permute-done | bytes 262176 | tf_op jit(solution)/shard_map/ppermute | solution.py:508
  249.3 4.3 %collective-permute-done.51 = bf16[1024,128]{1,0:T(8,128)(2,1)S(1)} collective-permute-done((bf16[1024,128]{1,0:T(8,128)(2,1)S(1)}, bf16[1024,128]{1,0:T(8,128)(2,1)S(1)}, u32[]{:S(2)}, u32[]{:S(2)}) %collective-permute-start.51) | collective-permute-done | bytes 262176 | tf_op jit(solution)/shard_map/ppermute | solution.py:508
  (194 shorter events, 58.9 us)
Async XLA Ops:
  3.3 14.2 %collective-permute-start.18 = (bf16[1024,128]{1,0:T(8,128)(2,1)S(1)}, bf16[1024,128]{1,0:T(8,128)(2,1)S(1)}, u32[]{:S(2)}, u32[]{:S(2)}) collective-permute-start(bf16[1024,128]{1,0:T(8,128)(2,1)S(1)} %get-tuple-element.26.refs_0_), channel_id=1, source_target_pairs={{0,2},{1,3},{2,4},{3,5},{4,6},{5,7},{6,0},{7,1},{8,10},{9,11},{10,... | collective-permute-start | bytes 786440 | tf_op jit(solution)/shard_map/ppermute | solution.py:508
  11.3 13.1 %collective-permute-start.17 = (bf16[1024,128]{1,0:T(8,128)(2,1)S(1)}, bf16[1024,128]{1,0:T(8,128)(2,1)S(1)}, u32[]{:S(2)}, u32[]{:S(2)}) collective-permute-start(bf16[1024,128]{1,0:T(8,128)(2,1)S(1)} %get-tuple-element.26.refs_0_), channel_id=1, source_target_pairs={{0,6},{1,7},{2,0},{3,1},{4,2},{5,3},{6,4},{7,5},{8,14},{9,15},{10,... | collective-permute-start | bytes 786440 | tf_op jit(solution)/shard_map/ppermute | solution.py:511
  13.5 13.6 %collective-permute-start.20 = (bf16[1024,128]{1,0:T(8,128)(2,1)S(1)}, bf16[1024,128]{1,0:T(8,128)(2,1)S(1)}, u32[]{:S(2)}, u32[]{:S(2)}) collective-permute-start(bf16[1024,128]{1,0:T(8,128)(2,1)S(1)} %get-tuple-element.26.refs_0_), channel_id=1, source_target_pairs={{0,1},{1,0},{2,3},{3,2},{4,5},{5,4},{6,7},{7,6},{8,9},{9,8},{10,11... | collective-permute-start | bytes 786440 | tf_op jit(solution)/shard_map/ppermute | solution.py:514
  13.6 14.6 %collective-permute-start.11 = (bf16[1024,128]{1,0:T(8,128)(2,1)S(1)}, bf16[1024,128]{1,0:T(8,128)(2,1)S(1)}, u32[]{:S(2)}, u32[]{:S(2)}) collective-permute-start(bf16[1024,128]{1,0:T(8,128)(2,1)S(1)} %get-tuple-element.25.refs_0_), channel_id=1, source_target_pairs={{0,2},{1,3},{2,4},{3,5},{4,6},{5,7},{6,0},{7,1},{8,10},{9,11},{10,... | collective-permute-start | bytes 786440 | tf_op jit(solution)/shard_map/ppermute | solution.py:508
  13.7 20.0 %collective-permute-start.10 = (bf16[1024,128]{1,0:T(8,128)(2,1)S(1)}, bf16[1024,128]{1,0:T(8,128)(2,1)S(1)}, u32[]{:S(2)}, u32[]{:S(2)}) collective-permute-start(bf16[1024,128]{1,0:T(8,128)(2,1)S(1)} %get-tuple-element.25.refs_0_), channel_id=1, source_target_pairs={{0,6},{1,7},{2,0},{3,1},{4,2},{5,3},{6,4},{7,5},{8,14},{9,15},{10,... | collective-permute-start | bytes 786440 | tf_op jit(solution)/shard_map/ppermute | solution.py:511
  17.4 16.3 %collective-permute-start.13 = (bf16[1024,128]{1,0:T(8,128)(2,1)S(1)}, bf16[1024,128]{1,0:T(8,128)(2,1)S(1)}, u32[]{:S(2)}, u32[]{:S(2)}) collective-permute-start(bf16[1024,128]{1,0:T(8,128)(2,1)S(1)} %get-tuple-element.25.refs_0_), channel_id=1, source_target_pairs={{0,1},{1,0},{2,3},{3,2},{4,5},{5,4},{6,7},{7,6},{8,9},{9,8},{10,11... | collective-permute-start | bytes 786440 | tf_op jit(solution)/shard_map/ppermute | solution.py:514
  24.3 14.7 %collective-permute-start.4 = (bf16[1024,128]{1,0:T(8,128)(2,1)S(1)}, bf16[1024,128]{1,0:T(8,128)(2,1)S(1)}, u32[]{:S(2)}, u32[]{:S(2)}) collective-permute-start(bf16[1024,128]{1,0:T(8,128)(2,1)S(1)} %get-tuple-element.24.refs_0_), channel_id=1, source_target_pairs={{0,2},{1,3},{2,4},{3,5},{4,6},{5,7},{6,0},{7,1},{8,10},{9,11},{10,... | collective-permute-start | bytes 786440 | tf_op jit(solution)/shard_map/ppermute | solution.py:508
  27.1 17.3 %collective-permute-start.3 = (bf16[1024,128]{1,0:T(8,128)(2,1)S(1)}, bf16[1024,128]{1,0:T(8,128)(2,1)S(1)}, u32[]{:S(2)}, u32[]{:S(2)}) collective-permute-start(bf16[1024,128]{1,0:T(8,128)(2,1)S(1)} %get-tuple-element.24.refs_0_), channel_id=1, source_target_pairs={{0,6},{1,7},{2,0},{3,1},{4,2},{5,3},{6,4},{7,5},{8,14},{9,15},{10,... | collective-permute-start | bytes 786440 | tf_op jit(solution)/shard_map/ppermute | solution.py:511
  28.2 22.1 %collective-permute-start.19 = (bf16[1024,128]{1,0:T(8,128)(2,1)S(1)}, bf16[1024,128]{1,0:T(8,128)(2,1)S(1)}, u32[]{:S(2)}, u32[]{:S(2)}) collective-permute-start(bf16[1024,128]{1,0:T(8,128)(2,1)S(1)} %collective-permute-done.18.refs_3_), channel_id=1, source_target_pairs={{0,2},{1,3},{2,4},{3,5},{4,6},{5,7},{6,0},{7,1},{8,10},{9,11},{10,... | collective-permute-start | bytes 786440 | tf_op jit(solution)/shard_map/ppermute | solution.py:508
  33.7 17.3 %collective-permute-start.23 = (bf16[1024,128]{1,0:T(8,128)(2,1)S(1)}, bf16[1024,128]{1,0:T(8,128)(2,1)S(1)}, u32[]{:S(2)}, u32[]{:S(2)}) collective-permute-start(bf16[1024,128]{1,0:T(8,128)(2,1)S(1)} %collective-permute-done.18.refs_3_), channel_id=1, source_target_pairs={{0,1},{1,0},{2,3},{3,2},{4,5},{5,4},{6,7},{7,6},{8,9},{9,8},{10,11... | collective-permute-start | bytes 786440 | tf_op jit(solution)/shard_map/ppermute | solution.py:514
  34.4 17.3 %collective-permute-start.21 = (bf16[1024,128]{1,0:T(8,128)(2,1)S(1)}, bf16[1024,128]{1,0:T(8,128)(2,1)S(1)}, u32[]{:S(2)}, u32[]{:S(2)}) collective-permute-start(bf16[1024,128]{1,0:T(8,128)(2,1)S(1)} %collective-permute-done.17.refs_1_), channel_id=1, source_target_pairs={{0,1},{1,0},{2,3},{3,2},{4,5},{5,4},{6,7},{7,6},{8,9},{9,8},{10,11... | collective-permute-start | bytes 786440 | tf_op jit(solution)/shard_map/ppermute | solution.py:514
  39.0 15.2 %collective-permute-start.12 = (bf16[1024,128]{1,0:T(8,128)(2,1)S(1)}, bf16[1024,128]{1,0:T(8,128)(2,1)}, u32[]{:S(2)}, u32[]{:S(2)}) collective-permute-start(bf16[1024,128]{1,0:T(8,128)(2,1)S(1)} %collective-permute-done.11.refs_3_), channel_id=1, source_target_pairs={{0,2},{1,3},{2,4},{3,5},{4,6},{5,7},{6,0},{7,1},{8,10},{9,11},{10,... | collective-permute-start | bytes 786440 | tf_op jit(solution)/shard_map/ppermute | solution.py:508
  54.2 15.9 %collective-permute-start.15 = (bf16[1024,128]{1,0:T(8,128)(2,1)}, bf16[1024,128]{1,0:T(8,128)(2,1)}, u32[]{:S(2)}, u32[]{:S(2)}) collective-permute-start(bf16[1024,128]{1,0:T(8,128)(2,1)} %collective-permute-done.12.refs_2_), channel_id=1, source_target_pairs={{0,1},{1,0},{2,3},{3,2},{4,5},{5,4},{6,7},{7,6},{8,9},{9,8},{10,11... | collective-permute-start | bytes 786440 | tf_op jit(solution)/shard_map/ppermute | solution.py:514
  54.9 23.1 %collective-permute-start.6 = (bf16[1024,128]{1,0:T(8,128)(2,1)S(1)}, bf16[1024,128]{1,0:T(8,128)(2,1)S(1)}, u32[]{:S(2)}, u32[]{:S(2)}) collective-permute-start(bf16[1024,128]{1,0:T(8,128)(2,1)S(1)} %get-tuple-element.24.refs_0_), channel_id=1, source_target_pairs={{0,1},{1,0},{2,3},{3,2},{4,5},{5,4},{6,7},{7,6},{8,9},{9,8},{10,11... | collective-permute-start | bytes 786440 | tf_op jit(solution)/shard_map/ppermute | solution.py:514
  56.1 21.9 %collective-permute-start.9 = (bf16[1024,128]{1,0:T(8,128)(2,1)S(1)}, bf16[1024,128]{1,0:T(8,128)(2,1)}, u32[]{:S(2)}, u32[]{:S(2)}) collective-permute-start(bf16[1024,128]{1,0:T(8,128)(2,1)S(1)} %collective-permute-done.4.refs_3_), channel_id=1, source_target_pairs={{0,1},{1,0},{2,3},{3,2},{4,5},{5,4},{6,7},{7,6},{8,9},{9,8},{10,11... | collective-permute-start | bytes 786440 | tf_op jit(solution)/shard_map/ppermute | solution.py:514
  61.5 16.5 %collective-permute-start.7 = (bf16[1024,128]{1,0:T(8,128)(2,1)S(1)}, bf16[1024,128]{1,0:T(8,128)(2,1)}, u32[]{:S(2)}, u32[]{:S(2)}) collective-permute-start(bf16[1024,128]{1,0:T(8,128)(2,1)S(1)} %collective-permute-done.3.refs_1_), channel_id=1, source_target_pairs={{0,1},{1,0},{2,3},{3,2},{4,5},{5,4},{6,7},{7,6},{8,9},{9,8},{10,11... | collective-permute-start | bytes 786440 | tf_op jit(solution)/shard_map/ppermute | solution.py:514
  61.5 16.5 %collective-permute-start.8 = (bf16[1024,128]{1,0:T(8,128)(2,1)S(1)}, bf16[1024,128]{1,0:T(8,128)(2,1)}, u32[]{:S(2)}, u32[]{:S(2)}) collective-permute-start(bf16[1024,128]{1,0:T(8,128)(2,1)S(1)} %collective-permute-done.5.refs_2_), channel_id=1, source_target_pairs={{0,1},{1,0},{2,3},{3,2},{4,5},{5,4},{6,7},{7,6},{8,9},{9,8},{10,11... | collective-permute-start | bytes 786440 | tf_op jit(solution)/shard_map/ppermute | solution.py:514
  87.9 11.1 %collective-permute-start.25 = (bf16[800,128]{1,0:T(8,128)(2,1)S(1)}, bf16[800,128]{1,0:T(8,128)(2,1)S(1)}, u32[]{:S(2)}, u32[]{:S(2)}) collective-permute-start(bf16[800,128]{1,0:T(8,128)(2,1)S(1)} %get-tuple-element.77), channel_id=1, source_target_pairs={{0,16},{8,24},{16,0},{24,8},{1,17},{9,25},{17,1},{25,9},{2,18},{10... | collective-permute-start | bytes 614408 | tf_op jit(solution)/shard_map/ppermute | solution.py:505
  125.0 11.6 %collective-permute-start.31 = (bf16[208,256]{1,0:T(8,128)(2,1)S(1)}, bf16[208,256]{1,0:T(8,128)(2,1)S(1)}, u32[]{:S(2)}, u32[]{:S(2)}) collective-permute-start(bf16[208,256]{1,0:T(8,128)(2,1)S(1)} %add_convert_fusion.8), channel_id=1, source_target_pairs={{0,6},{1,7},{2,0},{3,1},{4,2},{5,3},{6,4},{7,5},{8,14},{9,15},{10,... | collective-permute-start | bytes 319496 | tf_op jit(solution)/shard_map/ppermute | solution.py:511
  139.2 44.2 %collective-permute-start.34 = (bf16[208,256]{1,0:T(8,128)(2,1)S(1)}, bf16[208,256]{1,0:T(8,128)(2,1)S(1)}, u32[]{:S(2)}, u32[]{:S(2)}) collective-permute-start(bf16[208,256]{1,0:T(8,128)(2,1)S(1)} %fusion.32), channel_id=1, source_target_pairs={{0,1},{1,0},{2,3},{3,2},{4,5},{5,4},{6,7},{7,6},{8,9},{9,8},{10,11... | collective-permute-start | bytes 319496 | tf_op jit(solution)/shard_map/ppermute | solution.py:514
  157.2 41.1 %collective-permute-start.41 = (bf16[4,1024,128]{2,1,0:T(8,128)(2,1)}, bf16[4,1024,128]{2,1,0:T(8,128)(2,1)S(1)}, u32[]{:S(2)}, u32[]{:S(2)}) collective-permute-start(bf16[4,1024,128]{2,1,0:T(8,128)(2,1)} %get-tuple-element.37), channel_id=1, source_target_pairs={{0,1},{1,0},{2,3},{3,2},{4,5},{5,4},{6,7},{7,6},{8,9},{9,8},{10,11... | collective-permute-start | bytes 3145736 | tf_op jit(solution)/shard_map/ppermute | solution.py:514
  170.0 32.3 %collective-permute-start.45 = (bf16[4,1024,128]{2,1,0:T(8,128)(2,1)}, bf16[4,1024,128]{2,1,0:T(8,128)(2,1)S(1)}, u32[]{:S(2)}, u32[]{:S(2)}) collective-permute-start(bf16[4,1024,128]{2,1,0:T(8,128)(2,1)} %get-tuple-element.39), channel_id=1, source_target_pairs={{0,1},{1,0},{2,3},{3,2},{4,5},{5,4},{6,7},{7,6},{8,9},{9,8},{10,11... | collective-permute-start | bytes 3145736 | tf_op jit(solution)/shard_map/ppermute | solution.py:514
  192.6 13.8 %collective-permute-start.49 = (bf16[4,1024,128]{2,1,0:T(8,128)(2,1)}, bf16[4,1024,128]{2,1,0:T(8,128)(2,1)S(1)}, u32[]{:S(2)}, u32[]{:S(2)}) collective-permute-start(bf16[4,1024,128]{2,1,0:T(8,128)(2,1)} %get-tuple-element.41), channel_id=1, source_target_pairs={{0,1},{1,0},{2,3},{3,2},{4,5},{5,4},{6,7},{7,6},{8,9},{9,8},{10,11... | collective-permute-start | bytes 3145736 | tf_op jit(solution)/shard_map/ppermute | solution.py:514
  198.5 11.1 %collective-permute-start.42 = (bf16[1024,128]{1,0:T(8,128)(2,1)S(1)}, bf16[1024,128]{1,0:T(8,128)(2,1)S(1)}, u32[]{:S(2)}, u32[]{:S(2)}) collective-permute-start(bf16[1024,128]{1,0:T(8,128)(2,1)S(1)} %get-tuple-element.62), channel_id=1, source_target_pairs={{0,2},{1,3},{2,4},{3,5},{4,6},{5,7},{6,0},{7,1},{8,10},{9,11},{10,... | collective-permute-start | bytes 786440 | tf_op jit(solution)/shard_map/ppermute | solution.py:508
  198.5 33.7 %collective-permute-start.44 = (bf16[1024,128]{1,0:T(8,128)(2,1)S(1)}, bf16[1024,128]{1,0:T(8,128)(2,1)S(1)}, u32[]{:S(2)}, u32[]{:S(2)}) collective-permute-start(bf16[1024,128]{1,0:T(8,128)(2,1)S(1)} %get-tuple-element.63), channel_id=1, source_target_pairs={{0,6},{1,7},{2,0},{3,1},{4,2},{5,3},{6,4},{7,5},{8,14},{9,15},{10,... | collective-permute-start | bytes 786440 | tf_op jit(solution)/shard_map/ppermute | solution.py:511
  202.5 18.3 %collective-permute-start.46 = (bf16[1024,128]{1,0:T(8,128)(2,1)S(1)}, bf16[1024,128]{1,0:T(8,128)(2,1)S(1)}, u32[]{:S(2)}, u32[]{:S(2)}) collective-permute-start(bf16[1024,128]{1,0:T(8,128)(2,1)S(1)} %get-tuple-element.64), channel_id=1, source_target_pairs={{0,2},{1,3},{2,4},{3,5},{4,6},{5,7},{6,0},{7,1},{8,10},{9,11},{10,... | collective-permute-start | bytes 786440 | tf_op jit(solution)/shard_map/ppermute | solution.py:508
  202.5 41.1 %collective-permute-start.48 = (bf16[1024,128]{1,0:T(8,128)(2,1)S(1)}, bf16[1024,128]{1,0:T(8,128)(2,1)S(1)}, u32[]{:S(2)}, u32[]{:S(2)}) collective-permute-start(bf16[1024,128]{1,0:T(8,128)(2,1)S(1)} %get-tuple-element.65), channel_id=1, source_target_pairs={{0,6},{1,7},{2,0},{3,1},{4,2},{5,3},{6,4},{7,5},{8,14},{9,15},{10,... | collective-permute-start | bytes 786440 | tf_op jit(solution)/shard_map/ppermute | solution.py:511
  206.5 25.6 %collective-permute-start.50 = (bf16[1024,128]{1,0:T(8,128)(2,1)S(1)}, bf16[1024,128]{1,0:T(8,128)(2,1)S(1)}, u32[]{:S(2)}, u32[]{:S(2)}) collective-permute-start(bf16[1024,128]{1,0:T(8,128)(2,1)S(1)} %get-tuple-element.66), channel_id=1, source_target_pairs={{0,2},{1,3},{2,4},{3,5},{4,6},{5,7},{6,0},{7,1},{8,10},{9,11},{10,... | collective-permute-start | bytes 786440 | tf_op jit(solution)/shard_map/ppermute | solution.py:508
  209.5 39.7 %collective-permute-start.52 = (bf16[1024,128]{1,0:T(8,128)(2,1)S(1)}, bf16[1024,128]{1,0:T(8,128)(2,1)S(1)}, u32[]{:S(2)}, u32[]{:S(2)}) collective-permute-start(bf16[1024,128]{1,0:T(8,128)(2,1)S(1)} %get-tuple-element.67), channel_id=1, source_target_pairs={{0,6},{1,7},{2,0},{3,1},{4,2},{5,3},{6,4},{7,5},{8,14},{9,15},{10,... | collective-permute-start | bytes 786440 | tf_op jit(solution)/shard_map/ppermute | solution.py:511
  220.8 22.5 %collective-permute-start.43 = (bf16[1024,128]{1,0:T(8,128)(2,1)S(1)}, bf16[1024,128]{1,0:T(8,128)(2,1)S(1)}, u32[]{:S(2)}, u32[]{:S(2)}) collective-permute-start(bf16[1024,128]{1,0:T(8,128)(2,1)S(1)} %fusion.4), channel_id=1, source_target_pairs={{0,2},{1,3},{2,4},{3,5},{4,6},{5,7},{6,0},{7,1},{8,10},{9,11},{10,... | collective-permute-start | bytes 786440 | tf_op jit(solution)/shard_map/ppermute | solution.py:508
  232.1 16.8 %collective-permute-start.47 = (bf16[1024,128]{1,0:T(8,128)(2,1)S(1)}, bf16[1024,128]{1,0:T(8,128)(2,1)S(1)}, u32[]{:S(2)}, u32[]{:S(2)}) collective-permute-start(bf16[1024,128]{1,0:T(8,128)(2,1)S(1)} %fusion.2), channel_id=1, source_target_pairs={{0,2},{1,3},{2,4},{3,5},{4,6},{5,7},{6,0},{7,1},{8,10},{9,11},{10,... | collective-permute-start | bytes 786440 | tf_op jit(solution)/shard_map/ppermute | solution.py:508
  232.2 21.4 %collective-permute-start.51 = (bf16[1024,128]{1,0:T(8,128)(2,1)S(1)}, bf16[1024,128]{1,0:T(8,128)(2,1)S(1)}, u32[]{:S(2)}, u32[]{:S(2)}) collective-permute-start(bf16[1024,128]{1,0:T(8,128)(2,1)S(1)} %fusion), channel_id=1, source_target_pairs={{0,2},{1,3},{2,4},{3,5},{4,6},{5,7},{6,0},{7,1},{8,10},{9,11},{10,... | collective-permute-start | bytes 786440 | tf_op jit(solution)/shard_map/ppermute | solution.py:508
  (56 other events, 432.8 us)

commit v2 on v1

--- a/solution.py
+++ b/solution.py
@@ -11,7 +11,7 @@
 GELU_K = 0.044715
 LANES = 128
 MIB = 2**20
-CHAINS = 4
+
 UNROLL = 4
 
 
@@ -170,13 +170,13 @@
     return (
         2 * width == groups * LANES
         and groups % 2 == 0
-        and shards % 2 == 0
         and shards >= 4
+        and (shards & (shards - 1)) == 0
         and sessions % 4 == 0
         and run % 16 == 0
-        and (groups * sessions * length // 2) % (CHAINS * UNROLL) == 0
+        and (groups * sessions * length // 2) % (16) == 0
         and rows_dev % 32 == 0
-        and CHAINS * shards * rows_dev * LANES * 4 <= 40 * MIB
+        and table_shape[0] * shards * rows_dev * LANES * 4 <= 32 * MIB
     )
 
 
@@ -188,19 +188,27 @@
     return pltpu.roll(values, LANES // 2, 1)
 
 
-def own_columns(me, table):
+def own_columns(at, table):
     tables, rows_dev, _ = table.shape
     half = rows_dev // 2
 
-    def kernel(me_ref, table_ref, *out_refs):
-        odd = me_ref[0] % 2 == 1
+    def kernel(at_ref, table_ref, first_ref, last_ref, all_ref):
+        odd = at_ref[0] % 2 == 1
         low = low_lanes(half)
-        for t, out_ref in enumerate(out_refs):
+        for t in range(tables):
             top = table_ref[t, :half, :].astype(jnp.float32)
             bottom = table_ref[t, half:, :].astype(jnp.float32)
             in_low = jnp.where(odd, swap_halves(top), top)
             in_high = jnp.where(odd, bottom, swap_halves(bottom))
-            out_ref[...] = jnp.where(low, in_low, in_high).astype(jnp.bfloat16)
+            values = jnp.where(low, in_low, in_high).astype(jnp.bfloat16)
+            if t < tables - 1:
+                first_ref[t] = values
+            else:
+                last_ref[0] = values
+            all_ref[t] = values
+
+    def whole(count):
+        return pl.BlockSpec((count, half, LANES), lambda i, m: (0, 0, 0))
 
     return pl.pallas_call(
         kernel,
@@ -208,24 +216,27 @@
             num_scalar_prefetch=1,
             grid=(1,),
             in_specs=[pl.BlockSpec((tables, rows_dev, LANES), lambda i, m: (0, 0, m[0] // 2))],
-            out_specs=[pl.BlockSpec((half, LANES), lambda i, m: (0, 0))] * tables,
+            out_specs=[whole(tables - 1), whole(1), whole(tables)],
         ),
-        out_shape=[jax.ShapeDtypeStruct((half, LANES), jnp.bfloat16)] * tables,
+        out_shape=[
+            jax.ShapeDtypeStruct((count, half, LANES), jnp.bfloat16)
+            for count in (tables - 1, 1, tables)
+        ],
         compiler_params=pltpu.CompilerParams(vmem_limit_bytes=24 * MIB),
         name="own_columns",
-    )(me, table)
+    )(at, table)
 
 
 def look_up(codes, slots, total, last):
     count = codes[0].shape[0]
-    half = slots[0].shape[0]
+    half = slots[0][0].shape[1]
 
     def kernel(low_ref, high_ref, *refs):
         slot_refs, refs = refs[: len(slots)], refs[len(slots) :]
         total_ref = None if total is None else refs[0]
         out_ref, rows, found = refs[-3:]
         for s, slot_ref in enumerate(slot_refs):
-            values = slot_ref[...].astype(jnp.float32)
+            values = slot_ref[0].astype(jnp.float32)
             rows[pl.ds(2 * s * half, half), :] = values
             rows[pl.ds((2 * s + 1) * half, half), :] = swap_halves(values)
         low = low_lanes(1)
@@ -244,14 +255,18 @@
             result = result + total_ref[...]
         out_ref[...] = result.astype(out_ref.dtype)
 
-    operands = list(slots) + ([] if total is None else [total])
+    def part(at):
+        return pl.BlockSpec((1, half, LANES), lambda i, *codes: (at, 0, 0))
+
+    operands = [slot[0] for slot in slots] + ([] if total is None else [total])
+    whole = pl.BlockSpec((count, LANES), lambda i, *codes: (0, 0))
     return pl.pallas_call(
         kernel,
         grid_spec=pltpu.PrefetchScalarGridSpec(
             num_scalar_prefetch=2,
-            grid=(),
-            in_specs=[VMEM] * len(operands),
-            out_specs=VMEM,
+            grid=(1,),
+            in_specs=[part(slot[1]) for slot in slots] + ([] if total is None else [whole]),
+            out_specs=whole,
             scratch_shapes=[
                 pltpu.VMEM((2 * len(slots) * half, LANES), jnp.float32),
                 pltpu.VMEM((count, LANES), jnp.float32),
@@ -267,14 +282,15 @@
 
 
 def add_rows(codes, blocks, shards, half):
-    count = codes[0].shape[0]
+    tables = len(codes)
+    count = codes[0][0].shape[0]
     per = blocks[0].shape[0]
     planes = shards // 2
-    share = count // CHAINS
-
-    def kernel(low_ref, high_ref, *refs):
+
+    def kernel(*refs):
+        code_refs, refs = refs[: 2 * tables], refs[2 * tables :]
         block_refs, refs = refs[: len(blocks)], refs[len(blocks) :]
-        near_ref, far_ref, values, *sums = refs
+        out_refs, values, sums = refs[: 2 * tables], refs[2 * tables], refs[2 * tables + 1 :]
         for k, block_ref in enumerate(block_refs):
             values[pl.ds(k * per, per), :] = block_ref[...].astype(jnp.float32)
         for part in sums:
@@ -284,44 +300,77 @@
 
         def some(step, carry):
             for j in range(UNROLL):
+                i = step * UNROLL + j
+                value = values[pl.ds(i, 1), :]
                 ready = []
-                for k, part in enumerate(sums):
-                    i = k * share + step * UNROLL + j
-                    value = values[pl.ds(i, 1), :]
-                    to_low, to_high = pl.ds(low_ref[i], 1), pl.ds(high_ref[i], 1)
+                for t, part in enumerate(sums):
+                    to_low, to_high = pl.ds(code_refs[2 * t][i], 1), pl.ds(code_refs[2 * t + 1][i], 1)
                     ready.append((to_low, part[to_low, :] + value, to_high, part[to_high, :] + value))
                 for part, (to_low, in_low, to_high, in_high) in zip(sums, ready):
                     pltpu.store(part.at[to_low, :], in_low, mask=low)
                     pltpu.store(part.at[to_high, :], in_high, mask=high)
             return carry
 
-        lax.fori_loop(0, share // UNROLL, some, 0)
-        for s in range(shards):
-            straight = sum(part[pl.ds(2 * s * half, half), :] for part in sums)
-            crossed = sum(part[pl.ds((2 * s + 1) * half, half), :] for part in sums)
-            result = (straight + swap_halves(crossed)).astype(jnp.bfloat16)
-            if s < planes:
-                near_ref[s] = result
-            else:
-                far_ref[s - planes] = result
+        lax.fori_loop(0, count // UNROLL, some, 0)
+        for t, part in enumerate(sums):
+            for s in range(shards):
+                straight = part[pl.ds(2 * s * half, half), :]
+                crossed = part[pl.ds((2 * s + 1) * half, half), :]
+                result = (straight + swap_halves(crossed)).astype(jnp.bfloat16)
+                out_refs[2 * t + s // planes][s % planes] = result
+
+    results = pl.pallas_call(
+        kernel,
+        grid_spec=pltpu.PrefetchScalarGridSpec(
+            num_scalar_prefetch=2 * tables,
+            grid=(),
+            in_specs=[VMEM] * len(blocks),
+            out_specs=[VMEM] * (2 * tables),
+            scratch_shapes=[pltpu.VMEM((count, LANES), jnp.float32)]
+            + [pltpu.VMEM((2 * shards * half, LANES), jnp.float32)] * tables,
+        ),
+        out_shape=[jax.ShapeDtypeStruct((planes, half, LANES), jnp.bfloat16)] * (2 * tables),
+        compiler_params=pltpu.CompilerParams(vmem_limit_bytes=48 * MIB),
+        cost_estimate=pl.CostEstimate(
+            flops=0, bytes_accessed=100 * MIB, transcendentals=0
+        ),
+        name="add_rows",
+    )(*[part for pair in codes for part in pair], *blocks)
+    return list(zip(results[::2], results[1::2]))
+
+
+def weight_chunk(tall, groups):
+    return -(-(2 * tall + 16) // (32 * groups)) * 16
+
+
+def scaled_sums(at, near, far, tall, scale):
+    groups, chunk, width = near.shape
+
+    def kernel(at_ref, near_ref, far_ref, one_ref, two_ref, gain_one_ref, gain_two_ref, flat):
+        me, core = at_ref[0], at_ref[1]
+        for k in range(groups):
+            for part_ref, side in ((near_ref, core), (far_ref, 1 - core)):
+                begin = pl.multiple_of((side * groups + (me - k + groups) % groups) * chunk, 16)
+                flat[pl.ds(begin, chunk), :] = part_ref[k].astype(jnp.float32) * scale
+        one_ref[...] = flat[:tall, :]
+        two_ref[...] = flat[tall : 2 * tall, :]
+        gain_one_ref[...] = flat[2 * tall : 2 * tall + 1, :]
+        gain_two_ref[...] = flat[2 * tall + 1 : 2 * tall + 2, :]
 
     return pl.pallas_call(
         kernel,
         grid_spec=pltpu.PrefetchScalarGridSpec(
-            num_scalar_prefetch=2,
+            num_scalar_prefetch=1,
             grid=(),
-            in_specs=[VMEM] * len(blocks),
-            out_specs=[VMEM] * 2,
-            scratch_shapes=[pltpu.VMEM((count, LANES), jnp.float32)]
-            + [pltpu.VMEM((2 * shards * half, LANES), jnp.float32)] * CHAINS,
+            in_specs=[VMEM] * 2,
+            out_specs=[VMEM] * 4,
+            scratch_shapes=[pltpu.VMEM((2 * groups * chunk, width), jnp.float32)],
         ),
-        out_shape=[jax.ShapeDtypeStruct((planes, half, LANES), jnp.bfloat16)] * 2,
-        compiler_params=pltpu.CompilerParams(vmem_limit_bytes=56 * MIB),
-        cost_estimate=pl.CostEstimate(
-            flops=0, bytes_accessed=12 * 3 * count * LANES * 4, transcendentals=0
-        ),
-        name="add_rows",
-    )(*codes, *blocks)
+        out_shape=[jax.ShapeDtypeStruct((tall, width), jnp.float32)] * 2
+        + [jax.ShapeDtypeStruct((1, width), jnp.float32)] * 2,
+        compiler_params=pltpu.CompilerParams(vmem_limit_bytes=16 * MIB),
+        name="scaled_sums",
+    )(at, near, far)
 
 
 def both_layers(me, blocks, weight_one, gain_one, weight_two, gain_two, grad_out, length):
@@ -330,15 +379,15 @@
     run = 2 * length
     steps = items // (2 * run)
     tall = weight_one.shape[0]
-    chunk = -(-(2 * tall + 16) // (32 * groups)) * 32
+    chunk = weight_chunk(tall, groups)
 
     def kernel(me_ref, *refs):
         block_refs, refs = refs[:groups], refs[groups:]
         w_one_ref, g_one_ref, w_two_ref, g_two_ref, top_ref, out_ref, *refs = refs
-        grad_refs, weight_refs, refs = refs[:groups], refs[groups : 2 * groups], refs[2 * groups :]
-        held, packed, sum_one, sum_two, sum_gains, flat = refs
+        grad_refs, refs = refs[:groups], refs[groups:]
+        kept_ref, given_ref, held, packed, sum_one, sum_two, sum_gains, flat = refs
         step = pl.program_id(0)
-        me_at = me_ref[0]
+        me_at, core = me_ref[0], me_ref[1]
         low = low_lanes(run)
         place = lax.broadcasted_iota(jnp.int32, (run, width), 0)
         place = jnp.where(place >= length, place - length, place)
@@ -438,13 +487,14 @@
             flat[2 * tall : 2 * tall + 16, :] = jnp.concatenate(
                 [sum_gains[...], jnp.zeros_like(sum_gains)], axis=0
             ).astype(jnp.bfloat16)
-            if groups * chunk > 2 * tall + 16:
+            if 2 * groups * chunk > 2 * tall + 16:
                 flat[2 * tall + 16 :, :] = jnp.zeros(
-                    (groups * chunk - 2 * tall - 16, width), jnp.bfloat16
+                    (2 * groups * chunk - 2 * tall - 16, width), jnp.bfloat16
                 )
             for k in range(groups):
-                begin = pl.multiple_of(((me_at + k) % groups) * chunk, 32)
-                weight_refs[k][...] = flat[pl.ds(begin, chunk), :]
+                for part_ref, side in ((kept_ref, core), (given_ref, 1 - core)):
+                    begin = pl.multiple_of((side * groups + (me_at + k) % groups) * chunk, 16)
+                    part_ref[k] = flat[pl.ds(begin, chunk), :]
 
     def whole(shape):
         return pl.BlockSpec(shape, lambda j, m: (0, 0))
@@ -462,19 +512,19 @@
             + [by_step(2 * run, width)],
             out_specs=[by_step(2 * run, width)]
             + [by_step(run, LANES)] * groups
-            + [whole((chunk, width))] * groups,
+            + [pl.BlockSpec((groups, chunk, width), lambda j, m: (0, 0, 0))] * 2,
             scratch_shapes=[
                 pltpu.VMEM((groups, run, LANES), jnp.float32),
                 pltpu.VMEM((groups, run, LANES), jnp.float32),
                 pltpu.VMEM((width, tall), jnp.float32),
                 pltpu.VMEM((width, tall), jnp.float32),
                 pltpu.VMEM((8, width), jnp.float32),
-                pltpu.VMEM((groups * chunk, width), jnp.bfloat16),
+                pltpu.VMEM((2 * groups * chunk, width), jnp.bfloat16),
             ],
         ),
         out_shape=[jax.ShapeDtypeStruct((items, width), jnp.bfloat16)]
         + [jax.ShapeDtypeStruct((items // 2, LANES), jnp.bfloat16)] * groups
-        + [jax.ShapeDtypeStruct((chunk, width), jnp.bfloat16)] * groups,
+        + [jax.ShapeDtypeStruct((groups, chunk, width), jnp.bfloat16)] * 2,
         compiler_params=pltpu.CompilerParams(vmem_limit_bytes=48 * MIB),
         name="both_layers",
     )(
@@ -486,6 +536,10 @@
         gain_two.reshape(1, width),
         grad_out,
     )
+
+
+def after(values, *first):
+    return lax.optimization_barrier((values, *first))[0]
 
 
 def column_plan(shard_of, offsets, table, weight_one, gain_one, weight_two, gain_two, grad_out):
@@ -499,16 +553,22 @@
     run = 2 * length
     me = lax.axis_index("dp")
     plane, core = lax.axis_index("table") // 2, lax.axis_index("table") % 2
-    me_at = me.astype(jnp.int32).reshape(1)
+    at = jnp.stack([me, core]).astype(jnp.int32)
 
     def dp_shift(values, k):
         return lax.ppermute(values, "dp", [(i, (i + k) % groups) for i in range(groups)])
 
+    def table_shift(values, k):
+        return lax.ppermute(values, "table", [(i, (i + k) % shards) for i in range(shards)])
+
     def up(values):
-        return lax.ppermute(values, "table", [(i, (i + 2) % shards) for i in range(shards)])
+        return table_shift(values, 2)
 
     def down(values):
-        return lax.ppermute(values, "table", [(i, (i - 2) % shards) for i in range(shards)])
+        return table_shift(values, -2)
+
+    def plane_flip(values, k):
+        return lax.ppermute(values, "table", [(i, i ^ (2 * k)) for i in range(shards)])
 
     def across(values):
         return lax.ppermute(values, "table", [(i, i ^ 1) for i in range(shards)])
@@ -520,92 +580,105 @@
     places = places.reshape(2, items // (2 * run), 2, run, tables)
     mine = jnp.stack([places[0, :, 0], places[1, :, 1]], axis=0)
     mine = jnp.transpose(mine, (3, 0, 1, 2)).reshape(tables, 2, items // 2)
+
+    first, last, own = own_columns(at, table)
+    mine = after(mine, own)
     all_codes = jnp.concatenate([mine] + [dp_shift(mine, k) for k in range(1, groups)], axis=2)
     codes = [(all_codes[t, 0], all_codes[t, 1]) for t in range(tables)]
 
-    total = None
-    for t, own in enumerate(own_columns(me_at, table)):
+    def from_planes(own, first=None):
         near = [None] * planes
-        near[0] = rising = falling = own
+        rising = falling = own
         for k in range(1, planes // 2 + 1):
+            if first is not None and k == planes // 2:
+                rising = after(rising, first)
             near[planes - k] = rising = up(rising)
             if k <= (planes - 1) // 2:
                 near[k] = falling = down(falling)
-        far = [across(values) for values in near]
-        total = look_up(codes[t], near + far, total, t == tables - 1)
+        return near[1:]
+
+    near_first = from_planes(first)
+    swapped = across(after(own, all_codes))
+    last = after(last, swapped, near_first[0], near_first[-1])
+    far_first = [across(values) for values in near_first]
+
+    def slots(t, near, far, place):
+        return [(own, t), *((v, place) for v in near), (swapped, t), *((v, place) for v in far)]
+
+    total = look_up(codes[0], slots(0, near_first, far_first, 0), None, False)
+    near_last = from_planes(last, total)
+    for t in range(1, tables - 1):
+        total = look_up(codes[t], slots(t, near_first, far_first, t), total, False)
+    near_last[planes // 2 - 1] = after(near_last[planes // 2 - 1], total)
+    far_last = [across(values) for values in near_last]
+    total = look_up(codes[tables - 1], slots(tables - 1, near_last, far_last, 0), total, True)
 
     pieces = total.reshape(groups, items // 2, LANES)
     arrived = [pieces[0]] + [dp_shift(pieces[k], -k) for k in range(1, groups)]
     done = both_layers(
-        me_at, arrived, weight_one, gain_one, weight_two, gain_two, grad_out.reshape(items, width), length
+        at, arrived, weight_one, gain_one, weight_two, gain_two, grad_out.reshape(items, width), length
     )
     block_out = done[0].reshape(sessions, length, width)
-    sent, sums = done[1 : 1 + groups], done[1 + groups :]
+    sent, kept, given = done[1 : 1 + groups], done[1 + groups], done[2 + groups]
     blocks = [sent[0]] + [dp_shift(sent[k], k) for k in range(1, groups)]
-
-    grads = []
-    for t in range(tables):
-        near, far = add_rows(codes[t], blocks, shards, half)
-        got = across(far)
-
-        def both(r):
-            return near[r].astype(jnp.float32) + got[r].astype(jnp.float32)
-
-        result = both(0)
-        for move, order in (
-            (up, list(range(planes // 2, 0, -1))),
-            (down, list(range(planes // 2 + 1, planes))),
-        ):
-            moving = None
-            for r in order:
-                term = both(r)
-                if moving is not None:
-                    term = term + moving.astype(jnp.float32)
-                moving = move(term.astype(jnp.bfloat16))
-            if moving is not None:
-                result = result + moving.astype(jnp.float32)
-        grads.append(jnp.concatenate([result[:, : LANES // 2], result[:, LANES // 2 :]], axis=0))
-    table_grad = jnp.stack(grads, axis=0)
 
     def add_up(parts):
         return sum(part.astype(jnp.float32) for part in parts)
 
-    chunk = sums[0].shape[0]
-    mid = add_up([sums[0]] + [dp_shift(sums[k], k) for k in range(1, groups)]).astype(jnp.bfloat16)
-    kept = lax.dynamic_slice_in_dim(mid, core * (chunk // 2), chunk // 2, 0)
-    given = lax.dynamic_slice_in_dim(mid, (1 - core) * (chunk // 2), chunk // 2, 0)
-    by_plane = [None] * planes
-    by_plane[0] = rising = falling = add_up([kept, across(given)]).astype(jnp.bfloat16)
-    for k in range(1, planes // 2 + 1):
-        by_plane[planes - k] = rising = up(rising)
-        if k <= (planes - 1) // 2:
-            by_plane[k] = falling = down(falling)
-    stacked = jnp.stack(by_plane, axis=0)
-    kept = add_up(
-        [
-            lax.dynamic_index_in_dim(stacked, (a - plane + planes) % planes, 0, keepdims=False)
-            for a in range(planes)
-        ]
-    ).astype(jnp.bfloat16)
-    given = across(kept)
-    mid = jnp.where(core == 0, jnp.concatenate([kept, given]), jnp.concatenate([given, kept]))
-    stacked = jnp.stack([mid] + [dp_shift(mid, k) for k in range(1, groups)], axis=0)
-    sums = jnp.concatenate(
-        [
-            lax.dynamic_index_in_dim(stacked, (me - a + groups) % groups, 0, keepdims=False)
-            for a in range(groups)
-        ],
-        axis=0,
-    ).astype(jnp.float32) * (1.0 / math.sqrt(items * groups * shards))
-    tall = weight_one.shape[0]
-    return (
-        block_out,
-        sums[:tall],
-        sums[tall : 2 * tall],
-        sums[2 * tall],
-        sums[2 * tall + 1],
-        table_grad,
-    )
+    got = across(given)
+    chunks = [kept[k].astype(jnp.float32) + got[k].astype(jnp.float32) for k in range(groups)]
+    chunks = [chunks[0]] + [dp_shift(chunk.astype(jnp.bfloat16), k) for k, chunk in enumerate(chunks[1:], 1)]
+
+    def send_on(state):
+        sent = []
+        for side, move in (("up", up), ("down", down)):
+            terms, came = state[side], state["came"].pop(side, None)
+            if terms:
+                value = terms.pop(0)
+                if came is not None:
+                    value = value + came.astype(jnp.float32)
+                sent.append(value.astype(jnp.bfloat16))
+                state["came"][side] = move(sent[-1])
+            elif came is not None:
+                state["home"] = state["home"] + came.astype(jnp.float32)
+        return sent
+
+    states = []
+    sums = add_rows(codes, blocks, shards, half)
+    chunk = add_up([after(part, sums[0][1]) for part in chunks]).astype(jnp.bfloat16)
+    got = None
+    for near, far in sums:
+        got = across(far) if got is None else across(after(far, got))
+        if not states:
+            got = after(got, chunk)
+        sides = [near[r].astype(jnp.float32) + got[r].astype(jnp.float32) for r in range(planes)]
+        states.append(
+            {
+                "home": sides[0],
+                "up": [sides[r] for r in range(planes // 2, 0, -1)],
+                "down": [sides[r] for r in range(planes // 2 + 1, planes)],
+                "came": {},
+            }
+        )
+        send_on(states[-1])
+    sent = [state["came"]["up"] for state in states]
+    while any(state["came"] for state in states):
+        for state in states:
+            send_on(state)
+    grads = [
+        jnp.concatenate([state["home"][:, : LANES // 2], state["home"][:, LANES // 2 :]], axis=0)
+        for state in states
+    ]
+    table_grad = jnp.stack(grads, axis=0)
+
+    for k in range((planes - 1).bit_length()):
+        chunk = add_up([chunk, after(plane_flip(chunk, 2**k), sent[min(k, tables - 1)])]).astype(jnp.bfloat16)
+    near = jnp.stack([chunk] + [dp_shift(chunk, k) for k in range(1, groups)], axis=0)
+    far = across(near)
+    sums = scaled_sums(
+        at, near, far, weight_one.shape[0], 1.0 / math.sqrt(items * groups * shards)
+    )
+    return (block_out, sums[0], sums[1], sums[2].reshape(width), sums[3].reshape(width), table_grad)
 
 
 def solution(mesh):

time: 257 us -> 222 us (0.86)
  starting transfers between devices: 62 us -> 39 us
  Pallas kernels: 74.8 us -> 65.1 us
  local copies, waits for them, and re-layouts: 13 us -> 5.31 us
  waiting for transfers between devices: 103 us -> 110 us
    ppermute x21 -> x17, starting transfers between devices: 40.3 us -> 18.8 us  [the longest x15 15.3 us: table_shift(): lax.ppermute(values, 'table', [(i, (i + k) % shards) for i in range(shard...]
    pallas_call x3 -> x1, Pallas kernels: 38.7 us -> 28 us  [add_rows(): pl.pallas_call(kernel, grid_spec=pltpu.PrefetchScalarGridSpec(num_scalar_...]
    ppermute x21 -> x17, waiting for transfers between devices: 72.1 us -> 78.4 us  [the longest x15 77 us: table_shift(): lax.ppermute(values, 'table', [(i, (i + k) % shards) for i in range(shard...]
    unnamed x71 -> x19, local copies, waits for them, and re-layouts: 8.99 us -> 3.95 us
    ppermute x17 -> x12, waiting for transfers between devices: 1.33 us -> 4.13 us  [across(): return lax.ppermute(values, 'table', [(i, i ^ 1) for i in range(shards)])]
  transfers between devices with their start and end apart: 53 -> 44, of which waited for: 24 -> 30; matrix products, arithmetic and copies ran while one was open for 2% -> 1% of each run, Pallas kernels for 21% -> 7%
where the time goes in v2:
time: 222 us
  waiting for transfers between devices  110 us (50%)
  Pallas kernels  65.1 us (29%)
  starting transfers between devices  39 us (18%)
  local copies, waits for them, and re-layouts  5.31 us (2%)
    ppermute x15, waiting for transfers between devices, table_shift(): lax.ppermute(values, 'table', [(i, (i + k) % shards) for i in range(shard...  77 us
    pallas_call x1, Pallas kernels, add_rows(): pl.pallas_call(kernel, grid_spec=pltpu.PrefetchScalarGridSpec(num_scalar_...  28 us
    ppermute x15, waiting for transfers between devices, dp_shift(): lax.ppermute(values, 'dp', [(i, (i + k) % groups) for i in range(groups)])  27.3 us
    pallas_call x3, Pallas kernels, look_up(): pl.pallas_call(kernel, grid_spec=pltpu.PrefetchScalarGridSpec(num_scalar_...  20.4 us
    ppermute x15, starting transfers between devices, dp_shift(): lax.ppermute(values, 'dp', [(i, (i + k) % groups) for i in range(groups)])  19.2 us
    ppermute x15, starting transfers between devices, table_shift(): lax.ppermute(values, 'table', [(i, (i + k) % shards) for i in range(shard...  15.3 us
    pallas_call x1, Pallas kernels, both_layers(): pl.pallas_call(kernel, grid_spec=pltpu.PrefetchScalarGridSpec(num_scalar_...  13.5 us
  transfers between devices with their start and end apart: 44, of which 30 were waited for; matrix products, arithmetic and copies ran while one was open for 1% of the time, Pallas kernels for 7%

profile of v2, /device:TPU:0, one launch (start us, length us, event | category | flops | bytes accessed | tf_op | source)
XLA Modules:
  0.0 222.2 jit_solution(16052901999042693026)
XLA Ops:
  0.7 1.9 copy-done
  4.0 3.1 %collective-permute-start.5 = (bf16[2,1024,128]{2,1,0:T(8,128)(2,1)S(1)}, bf16[2,1024,128]{2,1,0:T(8,128)(2,1)S(1)}, u32[]{:S(2)}, u32[]{:S(2)}) collective-permute-start(bf16[2,1024,128]{2,1,0:T(8,128)(2,1)S(1)} %get-tuple-element.44), channel_id=1, source_target_pairs={{0,2},{1,3},{2,4},{3,5},{4,6},{5,7},{6,0},{7,1},{8,10},{9,11},{10,... | collective-permute-start | bytes 1572872 | tf_op jit(solution)/shard_map/ppermute | solution.py:562
  7.5 2.5 %collective-permute-start.2 = (s32[3,2,800]{2,1,0:T(2,128)S(1)}, s32[3,2,800]{2,1,0:T(2,128)S(1)}, u32[]{:S(2)}, u32[]{:S(2)}) collective-permute-start(s32[3,2,800]{2,1,0:T(2,128)S(1)} %reshape.104), channel_id=1, source_target_pairs={{0,24},{8,0},{16,8},{24,16},{1,25},{9,1},{17,9},{25,17},{2,26},{10... | collective-permute-start | bytes 57608 | tf_op jit(solution)/shard_map/ppermute | solution.py:559
  11.1 2.2 %collective-permute-start.4 = (bf16[2,1024,128]{2,1,0:T(8,128)(2,1)S(1)}, bf16[2,1024,128]{2,1,0:T(8,128)(2,1)S(1)}, u32[]{:S(2)}, u32[]{:S(2)}) collective-permute-start(bf16[2,1024,128]{2,1,0:T(8,128)(2,1)S(1)} %get-tuple-element.44), channel_id=1, source_target_pairs={{0,6},{1,7},{2,0},{3,1},{4,2},{5,3},{6,4},{7,5},{8,14},{9,15},{10,... | collective-permute-start | bytes 1572872 | tf_op jit(solution)/shard_map/ppermute | solution.py:562
  15.5 6.4 %collective-permute-done.5.refs_3_ = bf16[2,1024,128]{2,1,0:T(8,128)(2,1)S(1)} collective-permute-done((bf16[2,1024,128]{2,1,0:T(8,128)(2,1)S(1)}, bf16[2,1024,128]{2,1,0:T(8,128)(2,1)S(1)}, u32[]{:S(2)}, u32[]{:S(2)}) %collective-permute-start.5) | collective-permute-done | bytes 524320 | tf_op jit(solution)/shard_map/ppermute | solution.py:562
  21.9 11.1 %collective-permute-done.4.refs_1_ = bf16[2,1024,128]{2,1,0:T(8,128)(2,1)S(1)} collective-permute-done((bf16[2,1024,128]{2,1,0:T(8,128)(2,1)S(1)}, bf16[2,1024,128]{2,1,0:T(8,128)(2,1)S(1)}, u32[]{:S(2)}, u32[]{:S(2)}) %collective-permute-start.4) | collective-permute-done | bytes 524320 | tf_op jit(solution)/shard_map/ppermute | solution.py:562
  33.0 10.5 %collective-permute-done.8.refs_2_ = bf16[2,1024,128]{2,1,0:T(8,128)(2,1)S(1)} collective-permute-done((bf16[2,1024,128]{2,1,0:T(8,128)(2,1)S(1)}, bf16[2,1024,128]{2,1,0:T(8,128)(2,1)S(1)}, u32[]{:S(2)}, u32[]{:S(2)}) %collective-permute-start.8) | collective-permute-done | bytes 524320 | tf_op jit(solution)/shard_map/ppermute | solution.py:562
  43.7 3.9 %collective-permute-start.6 = (bf16[1,1024,128]{2,1,0:T(8,128)(2,1)S(1)}, bf16[1,1024,128]{2,1,0:T(8,128)(2,1)S(1)}, u32[]{:S(2)}, u32[]{:S(2)}) collective-permute-start(bf16[1,1024,128]{2,1,0:T(8,128)(2,1)S(1)} %get-tuple-element.45), channel_id=1, source_target_pairs={{0,6},{1,7},{2,0},{3,1},{4,2},{5,3},{6,4},{7,5},{8,14},{9,15},{10,... | collective-permute-start | bytes 786440 | tf_op jit(solution)/shard_map/ppermute | solution.py:562
  47.6 6.8 %look_up.3.refs_8_ = f32[3200,128]{1,0:T(8,128)S(1)} custom-call(s32[3200]{0:T(1024)S(1)} %get-tuple-element.89.low_ref.refs_0_, s32[3200]{0:T(1024)S(1)} %get-tuple-element.88.high_ref.refs_1_, bf16[3,1024,128]{2,1,0:T(8,128)(2,1)S(1)} %get-tuple-element.43.refs_0_, bf16[2,1024,128]{2,1,0:T(8,128)(2,1)S(1)} %collective-permute-done.4.refs_1_, ...), custom_call_target="tpu_custom_call" | custom-call | bytes 39321600 | tf_op jit(solution)/shard_map/look_up/pallas_call | solution.py:263
  54.5 3.6 %collective-permute-done.6.refs_1_ = bf16[1,1024,128]{2,1,0:T(8,128)(2,1)S(1)} collective-permute-done((bf16[1,1024,128]{2,1,0:T(8,128)(2,1)S(1)}, bf16[1,1024,128]{2,1,0:T(8,128)(2,1)S(1)}, u32[]{:S(2)}, u32[]{:S(2)}) %collective-permute-start.6) | collective-permute-done | bytes 262176 | tf_op jit(solution)/shard_map/ppermute | solution.py:562
  58.1 6.8 %look_up.4.refs_8_ = f32[3200,128]{1,0:T(8,128)S(1)} custom-call(s32[3200]{0:T(1024)S(1)} %get-tuple-element.87.low_ref.refs_2_, s32[3200]{0:T(1024)S(1)} %get-tuple-element.86.high_ref.refs_3_, bf16[3,1024,128]{2,1,0:T(8,128)(2,1)S(1)} %get-tuple-element.43.refs_0_, bf16[2,1024,128]{2,1,0:T(8,128)(2,1)S(1)} %collective-permute-done.4.refs_1_, ...), custom_call_target="tpu_custom_call" | custom-call | bytes 39321600 | tf_op jit(solution)/shard_map/look_up/pallas_call | solution.py:263
  66.9 6.8 %look_up.5 = bf16[3200,128]{1,0:T(8,128)(2,1)S(1)} custom-call(s32[3200]{0:T(1024)S(1)} %get-tuple-element.91.low_ref.refs_4_, s32[3200]{0:T(1024)S(1)} %get-tuple-element.90.high_ref.refs_5_, bf16[3,1024,128]{2,1,0:T(8,128)(2,1)S(1)} %get-tuple-element.43.refs_0_, bf16[1,1024,128]{2,1,0:T(8,128)(2,1)S(1)} %collective-permute-done.6.refs_1_, ...), custom_call_target="tpu_custom_call" | custom-call | bytes 39321600 | tf_op jit(solution)/shard_map/look_up/pallas_call | solution.py:263
  78.2 4.4 %collective-permute-done.18.refs_3_ = bf16[800,128]{1,0:T(8,128)(2,1)S(1)} collective-permute-done((bf16[800,128]{1,0:T(8,128)(2,1)S(1)}, bf16[800,128]{1,0:T(8,128)(2,1)S(1)}, u32[]{:S(2)}, u32[]{:S(2)}) %collective-permute-start.18) | collective-permute-done | bytes 204832 | tf_op jit(solution)/shard_map/ppermute | solution.py:559
  82.7 3.6 %collective-permute-done.17.refs_2_ = bf16[800,128]{1,0:T(8,128)(2,1)S(1)} collective-permute-done((bf16[800,128]{1,0:T(8,128)(2,1)S(1)}, bf16[800,128]{1,0:T(8,128)(2,1)S(1)}, u32[]{:S(2)}, u32[]{:S(2)}) %collective-permute-start.17) | collective-permute-done | bytes 204832 | tf_op jit(solution)/shard_map/ppermute | solution.py:559
  86.4 13.5 %both_layers.1 = (bf16[1600,256]{1,0:T(8,128)(2,1)}, bf16[800,128]{1,0:T(8,128)(2,1)S(1)}, bf16[800,128]{1,0:T(8,128)(2,1)S(1)}, bf16[800,128]{1,0:T(8,128)(2,1)...) custom-call(s32[2]{0:T(128)S(1)} %pad_add_fusion.at_ref.me_ref, ...), custom_call_target="tpu_custom_call" | custom-call | tf_op jit(solution)/shard_map/both_layers/pallas_call | solution.py:505
  102.1 2.1 collective-permute-start.22
  104.3 4.5 %collective-permute-done.20.refs_7_ = bf16[800,128]{1,0:T(8,128)(2,1)S(1)} collective-permute-done((bf16[800,128]{1,0:T(8,128)(2,1)S(1)}, bf16[800,128]{1,0:T(8,128)(2,1)S(1)}, u32[]{:S(2)}, u32[]{:S(2)}) %collective-permute-start.20) | collective-permute-done | bytes 204832 | tf_op jit(solution)/shard_map/ppermute | solution.py:559
  108.8 3.1 %collective-permute-done.21.refs_8_ = bf16[800,128]{1,0:T(8,128)(2,1)S(1)} collective-permute-done((bf16[800,128]{1,0:T(8,128)(2,1)S(1)}, bf16[800,128]{1,0:T(8,128)(2,1)S(1)}, u32[]{:S(2)}, u32[]{:S(2)}) %collective-permute-start.21) | collective-permute-done | bytes 204832 | tf_op jit(solution)/shard_map/ppermute | solution.py:559
  112.2 28.0 %add_rows.1 = (bf16[4,1024,128]{2,1,0:T(8,128)(2,1)S(1)}, bf16[4,1024,128]{2,1,0:T(8,128)(2,1)S(1)}, bf16[4,1024,128]{2,1,0:T(8,128)(2,1)S(1)}, bf16[4,1024,128]...) custom-call(s32[3200]{0:T(1024)S(1)} %get-tuple-element.89.low_ref.refs_0_, ...), custom_call_target="tpu_custom_call" | custom-call | bytes 104857600 | tf_op jit(solution)/shard_map/add_rows/pallas_call | solution.py:322
  140.7 2.8 %collective-permute-done.19 = bf16[4,208,256]{2,1,0:T(8,128)(2,1)S(1)} collective-permute-done((bf16[4,208,256]{2,1,0:T(8,128)(2,1)S(1)}, bf16[4,208,256]{2,1,0:T(8,128)(2,1)S(1)}, u32[]{:S(2)}, u32[]{:S(2)}) %collective-permute-start.19) | collective-permute-done | bytes 426016 | tf_op jit(solution)/shard_map/ppermute | solution.py:574
  148.6 2.7 %collective-permute-done.24 = bf16[208,256]{1,0:T(8,128)(2,1)S(1)} collective-permute-done((bf16[208,256]{1,0:T(8,128)(2,1)S(1)}, bf16[208,256]{1,0:T(8,128)(2,1)S(1)}, u32[]{:S(2)}, u32[]{:S(2)}) %collective-permute-start.24) | collective-permute-done | bytes 106528 | tf_op jit(solution)/shard_map/ppermute | solution.py:559
  153.7 2.1 collective-permute-start.26
  156.8 6.8 %collective-permute-done.28 = bf16[1024,128]{1,0:T(8,128)(2,1)S(1)} collective-permute-done((bf16[1024,128]{1,0:T(8,128)(2,1)S(1)}, bf16[1024,128]{1,0:T(8,128)(2,1)S(1)}, u32[]{:S(2)}, u32[]{:S(2)}) %collective-permute-start.28) | collective-permute-done | bytes 262176 | tf_op jit(solution)/shard_map/ppermute | solution.py:562
  166.6 11.7 %collective-permute-done.36 = bf16[1024,128]{1,0:T(8,128)(2,1)S(1)} collective-permute-done((bf16[1024,128]{1,0:T(8,128)(2,1)S(1)}, bf16[1024,128]{1,0:T(8,128)(2,1)S(1)}, u32[]{:S(2)}, u32[]{:S(2)}) %collective-permute-start.36) | collective-permute-done | bytes 262176 | tf_op jit(solution)/shard_map/ppermute | solution.py:562
  179.1 3.8 %collective-permute-start.38 = (bf16[1024,128]{1,0:T(8,128)(2,1)S(1)}, bf16[1024,128]{1,0:T(8,128)(2,1)S(1)}, u32[]{:S(2)}, u32[]{:S(2)}) collective-permute-start(bf16[1024,128]{1,0:T(8,128)(2,1)S(1)} %get-tuple-element.96), channel_id=1, source_target_pairs={{0,6},{1,7},{2,0},{3,1},{4,2},{5,3},{6,4},{7,5},{8,14},{9,15},{10,... | collective-permute-start | bytes 786440 | tf_op jit(solution)/shard_map/ppermute | solution.py:562
  182.9 6.8 %collective-permute-done.31 = bf16[1024,128]{1,0:T(8,128)(2,1)S(1)} collective-permute-done((bf16[1024,128]{1,0:T(8,128)(2,1)S(1)}, bf16[1024,128]{1,0:T(8,128)(2,1)S(1)}, u32[]{:S(2)}, u32[]{:S(2)}) %collective-permute-start.31) | collective-permute-done | bytes 262176 | tf_op jit(solution)/shard_map/ppermute | solution.py:562
  197.5 5.5 %collective-permute-done.39 = bf16[1024,128]{1,0:T(8,128)(2,1)S(1)} collective-permute-done((bf16[1024,128]{1,0:T(8,128)(2,1)S(1)}, bf16[1024,128]{1,0:T(8,128)(2,1)S(1)}, u32[]{:S(2)}, u32[]{:S(2)}) %collective-permute-start.39) | collective-permute-done | bytes 262176 | tf_op jit(solution)/shard_map/ppermute | solution.py:562
  203.3 5.3 %collective-permute-done.42 = bf16[1024,128]{1,0:T(8,128)(2,1)S(1)} collective-permute-done((bf16[1024,128]{1,0:T(8,128)(2,1)S(1)}, bf16[1024,128]{1,0:T(8,128)(2,1)S(1)}, u32[]{:S(2)}, u32[]{:S(2)}) %collective-permute-start.42) | collective-permute-done | bytes 262176 | tf_op jit(solution)/shard_map/ppermute | solution.py:562
  209.0 1.9 scaled_sums.1
  210.9 3.3 %collective-permute-done.41 = bf16[1024,128]{1,0:T(8,128)(2,1)S(1)} collective-permute-done((bf16[1024,128]{1,0:T(8,128)(2,1)S(1)}, bf16[1024,128]{1,0:T(8,128)(2,1)S(1)}, u32[]{:S(2)}, u32[]{:S(2)}) %collective-permute-start.41) | collective-permute-done | bytes 262176 | tf_op jit(solution)/shard_map/ppermute | solution.py:562
  214.2 5.4 %collective-permute-done.43 = bf16[1024,128]{1,0:T(8,128)(2,1)S(1)} collective-permute-done((bf16[1024,128]{1,0:T(8,128)(2,1)S(1)}, bf16[1024,128]{1,0:T(8,128)(2,1)S(1)}, u32[]{:S(2)}, u32[]{:S(2)}) %collective-permute-start.43) | collective-permute-done | bytes 262176 | tf_op jit(solution)/shard_map/ppermute | solution.py:562
  220.2 2.0 copy.18
  (116 shorter events, 36.2 us)
Async XLA Ops:
  4.0 17.9 %collective-permute-start.5 = (bf16[2,1024,128]{2,1,0:T(8,128)(2,1)S(1)}, bf16[2,1024,128]{2,1,0:T(8,128)(2,1)S(1)}, u32[]{:S(2)}, u32[]{:S(2)}) collective-permute-start(bf16[2,1024,128]{2,1,0:T(8,128)(2,1)S(1)} %get-tuple-element.44), channel_id=1, source_target_pairs={{0,2},{1,3},{2,4},{3,5},{4,6},{5,7},{6,0},{7,1},{8,10},{9,11},{10,... | collective-permute-start | bytes 1572872 | tf_op jit(solution)/shard_map/ppermute | solution.py:562
  11.1 21.9 %collective-permute-start.4 = (bf16[2,1024,128]{2,1,0:T(8,128)(2,1)S(1)}, bf16[2,1024,128]{2,1,0:T(8,128)(2,1)S(1)}, u32[]{:S(2)}, u32[]{:S(2)}) collective-permute-start(bf16[2,1024,128]{2,1,0:T(8,128)(2,1)S(1)} %get-tuple-element.44), channel_id=1, source_target_pairs={{0,6},{1,7},{2,0},{3,1},{4,2},{5,3},{6,4},{7,5},{8,14},{9,15},{10,... | collective-permute-start | bytes 1572872 | tf_op jit(solution)/shard_map/ppermute | solution.py:562
  15.4 28.1 %collective-permute-start.3 = (bf16[3,1024,128]{2,1,0:T(8,128)(2,1)S(1)}, bf16[3,1024,128]{2,1,0:T(8,128)(2,1)S(1)}, u32[]{:S(2)}, u32[]{:S(2)}) collective-permute-start(bf16[3,1024,128]{2,1,0:T(8,128)(2,1)S(1)} %get-tuple-element.43.refs_0_), channel_id=1, source_target_pairs={{0,1},{1,0},{2,3},{3,2},{4,5},{5,4},{6,7},{7,6},{8,9},{9,8},{10,11... | collective-permute-start | bytes 2359304 | tf_op jit(solution)/shard_map/ppermute | solution.py:574
  21.9 21.6 %collective-permute-start.8 = (bf16[2,1024,128]{2,1,0:T(8,128)(2,1)S(1)}, bf16[2,1024,128]{2,1,0:T(8,128)(2,1)S(1)}, u32[]{:S(2)}, u32[]{:S(2)}) collective-permute-start(bf16[2,1024,128]{2,1,0:T(8,128)(2,1)S(1)} %collective-permute-done.5.refs_3_), channel_id=1, source_target_pairs={{0,2},{1,3},{2,4},{3,5},{4,6},{5,7},{6,0},{7,1},{8,10},{9,11},{10,... | collective-permute-start | bytes 1572872 | tf_op jit(solution)/shard_map/ppermute | solution.py:562
  21.9 25.7 %collective-permute-start.11 = (bf16[2,1024,128]{2,1,0:T(8,128)(2,1)S(1)}, bf16[2,1024,128]{2,1,0:T(8,128)(2,1)S(1)}, u32[]{:S(2)}, u32[]{:S(2)}) collective-permute-start(bf16[2,1024,128]{2,1,0:T(8,128)(2,1)S(1)} %collective-permute-done.5.refs_3_), channel_id=1, source_target_pairs={{0,1},{1,0},{2,3},{3,2},{4,5},{5,4},{6,7},{7,6},{8,9},{9,8},{10,11... | collective-permute-start | bytes 1572872 | tf_op jit(solution)/shard_map/ppermute | solution.py:574
  33.0 14.6 %collective-permute-start.9 = (bf16[2,1024,128]{2,1,0:T(8,128)(2,1)S(1)}, bf16[2,1024,128]{2,1,0:T(8,128)(2,1)S(1)}, u32[]{:S(2)}, u32[]{:S(2)}) collective-permute-start(bf16[2,1024,128]{2,1,0:T(8,128)(2,1)S(1)} %collective-permute-done.4.refs_1_), channel_id=1, source_target_pairs={{0,1},{1,0},{2,3},{3,2},{4,5},{5,4},{6,7},{7,6},{8,9},{9,8},{10,11... | collective-permute-start | bytes 1572872 | tf_op jit(solution)/shard_map/ppermute | solution.py:574
  43.5 11.0 %collective-permute-start.7 = (bf16[1,1024,128]{2,1,0:T(8,128)(2,1)S(1)}, bf16[1,1024,128]{2,1,0:T(8,128)(2,1)S(1)}, u32[]{:S(2)}, u32[]{:S(2)}) collective-permute-start(bf16[1,1024,128]{2,1,0:T(8,128)(2,1)S(1)} %get-tuple-element.45), channel_id=1, source_target_pairs={{0,2},{1,3},{2,4},{3,5},{4,6},{5,7},{6,0},{7,1},{8,10},{9,11},{10,... | collective-permute-start | bytes 786440 | tf_op jit(solution)/shard_map/ppermute | solution.py:562
  43.7 14.4 %collective-permute-start.6 = (bf16[1,1024,128]{2,1,0:T(8,128)(2,1)S(1)}, bf16[1,1024,128]{2,1,0:T(8,128)(2,1)S(1)}, u32[]{:S(2)}, u32[]{:S(2)}) collective-permute-start(bf16[1,1024,128]{2,1,0:T(8,128)(2,1)S(1)} %get-tuple-element.45), channel_id=1, source_target_pairs={{0,6},{1,7},{2,0},{3,1},{4,2},{5,3},{6,4},{7,5},{8,14},{9,15},{10,... | collective-permute-start | bytes 786440 | tf_op jit(solution)/shard_map/ppermute | solution.py:562
  54.5 10.8 %collective-permute-start.12 = (bf16[1,1024,128]{2,1,0:T(8,128)(2,1)S(1)}, bf16[1,1024,128]{2,1,0:T(8,128)(2,1)S(1)}, u32[]{:S(2)}, u32[]{:S(2)}) collective-permute-start(bf16[1,1024,128]{2,1,0:T(8,128)(2,1)S(1)} %collective-permute-done.7.refs_3_), channel_id=1, source_target_pairs={{0,2},{1,3},{2,4},{3,5},{4,6},{5,7},{6,0},{7,1},{8,10},{9,11},{10,... | collective-permute-start | bytes 786440 | tf_op jit(solution)/shard_map/ppermute | solution.py:562
  54.5 11.0 %collective-permute-start.15 = (bf16[1,1024,128]{2,1,0:T(8,128)(2,1)S(1)}, bf16[1,1024,128]{2,1,0:T(8,128)(2,1)S(1)}, u32[]{:S(2)}, u32[]{:S(2)}) collective-permute-start(bf16[1,1024,128]{2,1,0:T(8,128)(2,1)S(1)} %collective-permute-done.7.refs_3_), channel_id=1, source_target_pairs={{0,1},{1,0},{2,3},{3,2},{4,5},{5,4},{6,7},{7,6},{8,9},{9,8},{10,11... | collective-permute-start | bytes 786440 | tf_op jit(solution)/shard_map/ppermute | solution.py:574
  58.1 7.4 %collective-permute-start.13 = (bf16[1,1024,128]{2,1,0:T(8,128)(2,1)S(1)}, bf16[1,1024,128]{2,1,0:T(8,128)(2,1)S(1)}, u32[]{:S(2)}, u32[]{:S(2)}) collective-permute-start(bf16[1,1024,128]{2,1,0:T(8,128)(2,1)S(1)} %collective-permute-done.6.refs_1_), channel_id=1, source_target_pairs={{0,1},{1,0},{2,3},{3,2},{4,5},{5,4},{6,7},{7,6},{8,9},{9,8},{10,11... | collective-permute-start | bytes 786440 | tf_op jit(solution)/shard_map/ppermute | solution.py:574
  73.7 8.9 %collective-permute-start.18 = (bf16[800,128]{1,0:T(8,128)(2,1)S(1)}, bf16[800,128]{1,0:T(8,128)(2,1)S(1)}, u32[]{:S(2)}, u32[]{:S(2)}) collective-permute-start(bf16[800,128]{1,0:T(8,128)(2,1)S(1)} %get-tuple-element.104), channel_id=1, source_target_pairs={{0,8},{8,16},{16,24},{24,0},{1,9},{9,17},{17,25},{25,1},{2,10},{10... | collective-permute-start | bytes 614408 | tf_op jit(solution)/shard_map/ppermute | solution.py:559
  75.3 11.0 %collective-permute-start.17 = (bf16[800,128]{1,0:T(8,128)(2,1)S(1)}, bf16[800,128]{1,0:T(8,128)(2,1)S(1)}, u32[]{:S(2)}, u32[]{:S(2)}) collective-permute-start(bf16[800,128]{1,0:T(8,128)(2,1)S(1)} %get-tuple-element.105), channel_id=1, source_target_pairs={{0,16},{8,24},{16,0},{24,8},{1,17},{9,25},{17,1},{25,9},{2,18},{10... | collective-permute-start | bytes 614408 | tf_op jit(solution)/shard_map/ppermute | solution.py:559
  76.8 9.5 %collective-permute-start.16 = (bf16[800,128]{1,0:T(8,128)(2,1)S(1)}, bf16[800,128]{1,0:T(8,128)(2,1)S(1)}, u32[]{:S(2)}, u32[]{:S(2)}) collective-permute-start(bf16[800,128]{1,0:T(8,128)(2,1)S(1)} %get-tuple-element.106), channel_id=1, source_target_pairs={{0,24},{8,0},{16,8},{24,16},{1,25},{9,1},{17,9},{25,17},{2,26},{10... | collective-permute-start | bytes 614408 | tf_op jit(solution)/shard_map/ppermute | solution.py:559
  99.9 8.9 %collective-permute-start.20 = (bf16[800,128]{1,0:T(8,128)(2,1)S(1)}, bf16[800,128]{1,0:T(8,128)(2,1)S(1)}, u32[]{:S(2)}, u32[]{:S(2)}) collective-permute-start(bf16[800,128]{1,0:T(8,128)(2,1)S(1)} %get-tuple-element.52), channel_id=1, source_target_pairs={{0,8},{8,16},{16,24},{24,0},{1,9},{9,17},{17,25},{25,1},{2,10},{10... | collective-permute-start | bytes 614408 | tf_op jit(solution)/shard_map/ppermute | solution.py:559
  101.6 10.2 %collective-permute-start.21 = (bf16[800,128]{1,0:T(8,128)(2,1)S(1)}, bf16[800,128]{1,0:T(8,128)(2,1)S(1)}, u32[]{:S(2)}, u32[]{:S(2)}) collective-permute-start(bf16[800,128]{1,0:T(8,128)(2,1)S(1)} %get-tuple-element.53), channel_id=1, source_target_pairs={{0,16},{8,24},{16,0},{24,8},{1,17},{9,25},{17,1},{25,9},{2,18},{10... | collective-permute-start | bytes 614408 | tf_op jit(solution)/shard_map/ppermute | solution.py:559
  102.1 10.1 %collective-permute-start.22 = (bf16[800,128]{1,0:T(8,128)(2,1)S(1)}, bf16[800,128]{1,0:T(8,128)(2,1)S(1)}, u32[]{:S(2)}, u32[]{:S(2)}) collective-permute-start(bf16[800,128]{1,0:T(8,128)(2,1)S(1)} %get-tuple-element.54), channel_id=1, source_target_pairs={{0,24},{8,0},{16,8},{24,16},{1,25},{9,1},{17,9},{25,17},{2,26},{10... | collective-permute-start | bytes 614408 | tf_op jit(solution)/shard_map/ppermute | solution.py:559
  140.2 12.3 %collective-permute-start.27 = (bf16[4,1024,128]{2,1,0:T(8,128)(2,1)S(1)}, bf16[4,1024,128]{2,1,0:T(8,128)(2,1)S(1)}, u32[]{:S(2)}, u32[]{:S(2)}) collective-permute-start(bf16[4,1024,128]{2,1,0:T(8,128)(2,1)S(1)} %get-tuple-element.55), channel_id=1, source_target_pairs={{0,1},{1,0},{2,3},{3,2},{4,5},{5,4},{6,7},{7,6},{8,9},{9,8},{10,11... | collective-permute-start | bytes 3145736 | tf_op jit(solution)/shard_map/ppermute | solution.py:574
  152.5 26.0 %collective-permute-start.30 = (bf16[4,1024,128]{2,1,0:T(8,128)(2,1)S(1)}, bf16[4,1024,128]{2,1,0:T(8,128)(2,1)S(1)}, u32[]{:S(2)}, u32[]{:S(2)}) collective-permute-start(bf16[4,1024,128]{2,1,0:T(8,128)(2,1)S(1)} %get-tuple-element.65), channel_id=1, source_target_pairs={{0,1},{1,0},{2,3},{3,2},{4,5},{5,4},{6,7},{7,6},{8,9},{9,8},{10,11... | collective-permute-start | bytes 3145736 | tf_op jit(solution)/shard_map/ppermute | solution.py:574
  152.7 11.0 %collective-permute-start.28 = (bf16[1024,128]{1,0:T(8,128)(2,1)S(1)}, bf16[1024,128]{1,0:T(8,128)(2,1)S(1)}, u32[]{:S(2)}, u32[]{:S(2)}) collective-permute-start(bf16[1024,128]{1,0:T(8,128)(2,1)S(1)} %get-tuple-element.95), channel_id=1, source_target_pairs={{0,2},{1,3},{2,4},{3,5},{4,6},{5,7},{6,0},{7,1},{8,10},{9,11},{10,... | collective-permute-start | bytes 786440 | tf_op jit(solution)/shard_map/ppermute | solution.py:562
  153.7 11.5 %collective-permute-start.26 = (bf16[208,256]{1,0:T(8,128)(2,1)S(1)}, bf16[208,256]{1,0:T(8,128)(2,1)S(1)}, u32[]{:S(2)}, u32[]{:S(2)}) collective-permute-start(bf16[208,256]{1,0:T(8,128)(2,1)S(1)} %add_convert_fusion.8), channel_id=1, source_target_pairs={{0,2},{1,3},{2,0},{3,1},{4,6},{5,7},{6,4},{7,5},{8,10},{9,11},{10,... | collective-permute-start | bytes 319496 | tf_op jit(solution)/shard_map/ppermute | solution.py:571
  155.9 22.5 %collective-permute-start.36 = (bf16[1024,128]{1,0:T(8,128)(2,1)S(1)}, bf16[1024,128]{1,0:T(8,128)(2,1)S(1)}, u32[]{:S(2)}, u32[]{:S(2)}) collective-permute-start(bf16[1024,128]{1,0:T(8,128)(2,1)S(1)} %get-tuple-element.94), channel_id=1, source_target_pairs={{0,6},{1,7},{2,0},{3,1},{4,2},{5,3},{6,4},{7,5},{8,14},{9,15},{10,... | collective-permute-start | bytes 786440 | tf_op jit(solution)/shard_map/ppermute | solution.py:562
  163.8 14.5 %collective-permute-start.37 = (bf16[1024,128]{1,0:T(8,128)(2,1)S(1)}, bf16[1024,128]{1,0:T(8,128)(2,1)S(1)}, u32[]{:S(2)}, u32[]{:S(2)}) collective-permute-start(bf16[1024,128]{1,0:T(8,128)(2,1)S(1)} %fusion.4), channel_id=1, source_target_pairs={{0,2},{1,3},{2,4},{3,5},{4,6},{5,7},{6,0},{7,1},{8,10},{9,11},{10,... | collective-permute-start | bytes 786440 | tf_op jit(solution)/shard_map/ppermute | solution.py:562
  165.3 17.6 %collective-permute-start.29 = (bf16[208,256]{1,0:T(8,128)(2,1)S(1)}, bf16[208,256]{1,0:T(8,128)(2,1)S(1)}, u32[]{:S(2)}, u32[]{:S(2)}) collective-permute-start(bf16[208,256]{1,0:T(8,128)(2,1)S(1)} %add_convert_fusion.7), channel_id=1, source_target_pairs={{0,4},{1,5},{2,6},{3,7},{4,0},{5,1},{6,2},{7,3},{8,12},{9,13},{10,... | collective-permute-start | bytes 319496 | tf_op jit(solution)/shard_map/ppermute | solution.py:571
  178.6 11.1 %collective-permute-start.31 = (bf16[1024,128]{1,0:T(8,128)(2,1)S(1)}, bf16[1024,128]{1,0:T(8,128)(2,1)S(1)}, u32[]{:S(2)}, u32[]{:S(2)}) collective-permute-start(bf16[1024,128]{1,0:T(8,128)(2,1)S(1)} %get-tuple-element.97), channel_id=1, source_target_pairs={{0,2},{1,3},{2,4},{3,5},{4,6},{5,7},{6,0},{7,1},{8,10},{9,11},{10,... | collective-permute-start | bytes 786440 | tf_op jit(solution)/shard_map/ppermute | solution.py:562
  178.7 18.6 %collective-permute-start.40 = (bf16[4,1024,128]{2,1,0:T(8,128)(2,1)S(1)}, bf16[4,1024,128]{2,1,0:T(8,128)(2,1)S(1)}, u32[]{:S(2)}, u32[]{:S(2)}) collective-permute-start(bf16[4,1024,128]{2,1,0:T(8,128)(2,1)S(1)} %copy-done.8), channel_id=1, source_target_pairs={{0,1},{1,0},{2,3},{3,2},{4,5},{5,4},{6,7},{7,6},{8,9},{9,8},{10,11... | collective-permute-start | bytes 3145736 | tf_op jit(solution)/shard_map/ppermute | solution.py:574
  179.1 18.5 %collective-permute-start.38 = (bf16[1024,128]{1,0:T(8,128)(2,1)S(1)}, bf16[1024,128]{1,0:T(8,128)(2,1)S(1)}, u32[]{:S(2)}, u32[]{:S(2)}) collective-permute-start(bf16[1024,128]{1,0:T(8,128)(2,1)S(1)} %get-tuple-element.96), channel_id=1, source_target_pairs={{0,6},{1,7},{2,0},{3,1},{4,2},{5,3},{6,4},{7,5},{8,14},{9,15},{10,... | collective-permute-start | bytes 786440 | tf_op jit(solution)/shard_map/ppermute | solution.py:562
  194.5 8.6 %collective-permute-start.39 = (bf16[1024,128]{1,0:T(8,128)(2,1)S(1)}, bf16[1024,128]{1,0:T(8,128)(2,1)S(1)}, u32[]{:S(2)}, u32[]{:S(2)}) collective-permute-start(bf16[1024,128]{1,0:T(8,128)(2,1)S(1)} %fusion.2), channel_id=1, source_target_pairs={{0,2},{1,3},{2,4},{3,5},{4,6},{5,7},{6,0},{7,1},{8,10},{9,11},{10,... | collective-permute-start | bytes 786440 | tf_op jit(solution)/shard_map/ppermute | solution.py:562
  197.2 11.8 %collective-permute-start.35 = (bf16[4,208,256]{2,1,0:T(8,128)(2,1)S(1)}, bf16[4,208,256]{2,1,0:T(8,128)(2,1)S(1)}, u32[]{:S(2)}, u32[]{:S(2)}) collective-permute-start(bf16[4,208,256]{2,1,0:T(8,128)(2,1)S(1)} %pad_maximum_fusion.1.near_ref), channel_id=1, source_target_pairs={{0,1},{1,0},{2,3},{3,2},{4,5},{5,4},{6,7},{7,6},{8,9},{9,8},{10,11... | collective-permute-start | bytes 1277960 | tf_op jit(solution)/shard_map/ppermute | solution.py:574
  197.5 11.1 %collective-permute-start.42 = (bf16[1024,128]{1,0:T(8,128)(2,1)S(1)}, bf16[1024,128]{1,0:T(8,128)(2,1)S(1)}, u32[]{:S(2)}, u32[]{:S(2)}) collective-permute-start(bf16[1024,128]{1,0:T(8,128)(2,1)S(1)} %get-tuple-element.99), channel_id=1, source_target_pairs={{0,2},{1,3},{2,4},{3,5},{4,6},{5,7},{6,0},{7,1},{8,10},{9,11},{10,... | collective-permute-start | bytes 786440 | tf_op jit(solution)/shard_map/ppermute | solution.py:562
  203.2 11.0 %collective-permute-start.41 = (bf16[1024,128]{1,0:T(8,128)(2,1)S(1)}, bf16[1024,128]{1,0:T(8,128)(2,1)S(1)}, u32[]{:S(2)}, u32[]{:S(2)}) collective-permute-start(bf16[1024,128]{1,0:T(8,128)(2,1)S(1)} %get-tuple-element.98), channel_id=1, source_target_pairs={{0,6},{1,7},{2,0},{3,1},{4,2},{5,3},{6,4},{7,5},{8,14},{9,15},{10,... | collective-permute-start | bytes 786440 | tf_op jit(solution)/shard_map/ppermute | solution.py:562
  208.7 10.9 %collective-permute-start.43 = (bf16[1024,128]{1,0:T(8,128)(2,1)S(1)}, bf16[1024,128]{1,0:T(8,128)(2,1)S(1)}, u32[]{:S(2)}, u32[]{:S(2)}) collective-permute-start(bf16[1024,128]{1,0:T(8,128)(2,1)S(1)} %fusion), channel_id=1, source_target_pairs={{0,2},{1,3},{2,4},{3,5},{4,6},{5,7},{6,0},{7,1},{8,10},{9,11},{10,... | collective-permute-start | bytes 786440 | tf_op jit(solution)/shard_map/ppermute | solution.py:562
  (21 other events, 191.5 us)

commit v3 on v2

--- a/solution.py
+++ b/solution.py
@@ -12,7 +12,8 @@
 LANES = 128
 MIB = 2**20
 
-UNROLL = 4
+UNROLL = 16
+ROWS = 40
 
 
 def shifted(values, spacing):
@@ -169,14 +170,16 @@
     run = 2 * length
     return (
         2 * width == groups * LANES
-        and groups % 2 == 0
-        and shards >= 4
-        and (shards & (shards - 1)) == 0
+        and groups > 1
+        and (groups & (groups - 1)) == 0
         and sessions % 4 == 0
         and run % 16 == 0
-        and (groups * sessions * length // 2) % (16) == 0
+        and run % ROWS == 0
+        and (groups * sessions * length // 2) % (4 * UNROLL) == 0
         and rows_dev % 32 == 0
-        and table_shape[0] * shards * rows_dev * LANES * 4 <= 32 * MIB
+        and 4 * shards * rows_dev * LANES * 4 <= 40 * MIB
+        and table_shape[0] == 3
+        and shards == 8
     )
 
 
@@ -281,7 +284,7 @@
     )(*codes, *operands)
 
 
-def add_rows(codes, blocks, shards, half):
+def add_rows(codes, blocks, shards, half, chains):
     tables = len(codes)
     count = codes[0][0].shape[0]
     per = blocks[0].shape[0]
@@ -290,32 +293,37 @@
     def kernel(*refs):
         code_refs, refs = refs[: 2 * tables], refs[2 * tables :]
         block_refs, refs = refs[: len(blocks)], refs[len(blocks) :]
-        out_refs, values, sums = refs[: 2 * tables], refs[2 * tables], refs[2 * tables + 1 :]
+        out_refs, values, refs = refs[: 2 * tables], refs[2 * tables], refs[2 * tables + 1 :]
+        sums = [refs[t * chains : (t + 1) * chains] for t in range(tables)]
         for k, block_ref in enumerate(block_refs):
             values[pl.ds(k * per, per), :] = block_ref[...].astype(jnp.float32)
-        for part in sums:
+        for part in refs:
             part[...] = jnp.zeros_like(part)
         low = low_lanes(1)
         high = jnp.logical_not(low)
 
         def some(step, carry):
             for j in range(UNROLL):
-                i = step * UNROLL + j
-                value = values[pl.ds(i, 1), :]
                 ready = []
-                for t, part in enumerate(sums):
-                    to_low, to_high = pl.ds(code_refs[2 * t][i], 1), pl.ds(code_refs[2 * t + 1][i], 1)
-                    ready.append((to_low, part[to_low, :] + value, to_high, part[to_high, :] + value))
-                for part, (to_low, in_low, to_high, in_high) in zip(sums, ready):
+                for c in range(chains):
+                    i = c * (count // chains) + step * UNROLL + j
+                    value = values[pl.ds(i, 1), :]
+                    for t in range(tables):
+                        part = sums[t][c]
+                        to_low, to_high = pl.ds(code_refs[2 * t][i], 1), pl.ds(code_refs[2 * t + 1][i], 1)
+                        ready.append(
+                            (part, to_low, part[to_low, :] + value, to_high, part[to_high, :] + value)
+                        )
+                for part, to_low, in_low, to_high, in_high in ready:
                     pltpu.store(part.at[to_low, :], in_low, mask=low)
                     pltpu.store(part.at[to_high, :], in_high, mask=high)
             return carry
 
-        lax.fori_loop(0, count // UNROLL, some, 0)
-        for t, part in enumerate(sums):
+        lax.fori_loop(0, count // (chains * UNROLL), some, 0)
+        for t in range(tables):
             for s in range(shards):
-                straight = part[pl.ds(2 * s * half, half), :]
-                crossed = part[pl.ds((2 * s + 1) * half, half), :]
+                straight = sum(part[pl.ds(2 * s * half, half), :] for part in sums[t])
+                crossed = sum(part[pl.ds((2 * s + 1) * half, half), :] for part in sums[t])
                 result = (straight + swap_halves(crossed)).astype(jnp.bfloat16)
                 out_refs[2 * t + s // planes][s % planes] = result
 
@@ -327,18 +335,55 @@
             in_specs=[VMEM] * len(blocks),
             out_specs=[VMEM] * (2 * tables),
             scratch_shapes=[pltpu.VMEM((count, LANES), jnp.float32)]
-            + [pltpu.VMEM((2 * shards * half, LANES), jnp.float32)] * tables,
+            + [pltpu.VMEM((2 * shards * half, LANES), jnp.float32)] * (tables * chains),
         ),
         out_shape=[jax.ShapeDtypeStruct((planes, half, LANES), jnp.bfloat16)] * (2 * tables),
-        compiler_params=pltpu.CompilerParams(vmem_limit_bytes=48 * MIB),
+        compiler_params=pltpu.CompilerParams(vmem_limit_bytes=56 * MIB),
         cost_estimate=pl.CostEstimate(
-            flops=0, bytes_accessed=100 * MIB, transcendentals=0
+            flops=0, bytes_accessed=tables * 40 * MIB, transcendentals=0
         ),
         name="add_rows",
     )(*[part for pair in codes for part in pair], *blocks)
     return list(zip(results[::2], results[1::2]))
 
 
+def finished(parts, tables, earlier):
+    _, half, lanes = parts[0][0].shape
+    count = len(parts)
+    begin = 0 if earlier is None else tables - count
+
+    def kernel(*refs):
+        refs, out_ref = refs[:-1], refs[-1]
+        for t in range(count):
+            total = sum(ref[...].reshape(half, lanes).astype(jnp.float32) for ref in refs[4 * t : 4 * t + 4])
+            turned = total.T
+            out_ref[t, :, :half] = turned[: lanes // 2]
+            out_ref[t, :, half:] = turned[lanes // 2 :]
+
+    own = pl.BlockSpec((1, half, lanes), lambda i: (0, 0, 0))
+
+    def row_block(n):
+        return pl.BlockSpec((half, lanes), lambda i: (n, 0))
+
+    operands, specs = [], []
+    for near, got, down, last, n in parts:
+        operands += [near, got, down, last]
+        specs += [own, own, row_block(0), row_block(n)]
+    if earlier is not None:
+        operands.append(earlier)
+        specs.append(pl.BlockSpec(memory_space=pl.ANY))
+    return pl.pallas_call(
+        kernel,
+        grid=(1,),
+        in_specs=specs,
+        out_specs=pl.BlockSpec((count, lanes // 2, 2 * half), lambda i: (begin // count, 0, 0)),
+        out_shape=jax.ShapeDtypeStruct((tables, lanes // 2, 2 * half), jnp.float32),
+        input_output_aliases={} if earlier is None else {len(operands) - 1: 0},
+        compiler_params=pltpu.CompilerParams(vmem_limit_bytes=32 * MIB),
+        name="finished",
+    )(*operands)
+
+
 def weight_chunk(tall, groups):
     return -(-(2 * tall + 16) // (32 * groups)) * 16
 
@@ -350,7 +395,7 @@
         me, core = at_ref[0], at_ref[1]
         for k in range(groups):
             for part_ref, side in ((near_ref, core), (far_ref, 1 - core)):
-                begin = pl.multiple_of((side * groups + (me - k + groups) % groups) * chunk, 16)
+                begin = pl.multiple_of((side * groups + (me ^ k)) * chunk, 16)
                 flat[pl.ds(begin, chunk), :] = part_ref[k].astype(jnp.float32) * scale
         one_ref[...] = flat[:tall, :]
         two_ref[...] = flat[tall : 2 * tall, :]
@@ -385,7 +430,7 @@
         block_refs, refs = refs[:groups], refs[groups:]
         w_one_ref, g_one_ref, w_two_ref, g_two_ref, top_ref, out_ref, *refs = refs
         grad_refs, refs = refs[:groups], refs[groups:]
-        kept_ref, given_ref, held, packed, sum_one, sum_two, sum_gains, flat = refs
+        kept_ref, given_ref, held, packed, sum_one, sum_two, sum_gains, flat, turned_one, turned_two = refs
         step = pl.program_id(0)
         me_at, core = me_ref[0], me_ref[1]
         low = low_lanes(run)
@@ -397,6 +442,10 @@
             sum_one[...] = jnp.zeros_like(sum_one)
             sum_two[...] = jnp.zeros_like(sum_two)
             sum_gains[...] = jnp.zeros_like(sum_gains)
+            for weight_ref, turned_ref in ((w_one_ref, turned_one), (w_two_ref, turned_two)):
+                for k in range(tall // width):
+                    at = slice(k * width, (k + 1) * width)
+                    turned_ref[at, :] = weight_ref[at, :].T
 
         def taps(values, gap):
             one = jnp.where(place >= gap, pltpu.roll(values, gap, 0), 0.0)
@@ -408,50 +457,53 @@
             two = jnp.where(place < length - 2 * gap, pltpu.roll(values, run - 2 * gap, 0), 0.0)
             return [x.astype(jnp.bfloat16) for x in (values, one, two)]
 
-        def forward(values, weight_ref, gain, gap):
-            before = jnp.dot(taps(values, gap), weight_ref[...], preferred_element_type=jnp.float32)
+        def by_rows(work, *arrays):
+            parts = [work(*(a[r : r + ROWS] for a in arrays)) for r in range(0, run, ROWS)]
+            return [jnp.concatenate(values, axis=0) for values in zip(*parts)]
+
+        def activate(before, gain):
             centred = before - jnp.mean(before, axis=-1, keepdims=True)
             inv_std = lax.rsqrt(jnp.mean(centred * centred, axis=-1, keepdims=True) + 1e-05)
             normal = centred * inv_std
-            output, slope = gelu_parts(normal * gain)
-            return output, (normal, inv_std, slope)
-
-        def backward(grad, values, weight_ref, gain, saved, gap, total, row):
-            normal, inv_std, slope = saved
+            inputs = normal * gain
+            square = inputs * inputs
+            part = 0.5 + 0.5 * jnp.tanh(inputs * (GELU_C + GELU_C * GELU_K * square))
+            slope = part + inputs * (part - part * part) * (
+                2.0 * GELU_C + 6.0 * GELU_C * GELU_K * square
+            )
+            return normal, inv_std, inputs * part, slope
+
+        def unwind(grad, normal, inv_std, slope, gain, row):
             scaled = grad * slope
-            sum_gains[pl.ds(row, 1), :] += jnp.sum(scaled * normal, axis=0, keepdims=True)
+            sum_gains[row] += jnp.sum((scaled * normal).reshape(-1, 8, width), axis=0)
             back = scaled * gain
             before = inv_std * (
                 back
                 - jnp.mean(back, axis=-1, keepdims=True)
                 - normal * jnp.mean(back * normal, axis=-1, keepdims=True)
             )
-            parts = untaps(before.astype(jnp.bfloat16).astype(jnp.float32), gap)
+            return before.astype(jnp.bfloat16).astype(jnp.float32)
+
+        def products(before, values, turned_ref, gap, total):
+            stacked = jnp.concatenate(untaps(before, gap), axis=1)
             total[...] += lax.dot_general(
                 values.astype(jnp.bfloat16),
-                jnp.concatenate(parts, axis=1),
+                stacked,
                 (((0,), (0,)), ((), ())),
                 preferred_element_type=jnp.float32,
             )
-            return sum(
-                lax.dot_general(
-                    part,
-                    weight_ref[k * width : (k + 1) * width, :],
-                    (((1,), (1,)), ((), ())),
-                    preferred_element_type=jnp.float32,
-                )
-                for k, part in enumerate(parts)
-            )
+            return jnp.dot(stacked, turned_ref[...], preferred_element_type=jnp.float32)
 
         for k in range(groups):
             held[k] = block_refs[k][...].astype(jnp.float32)
         gain_one_at, gain_two_at = g_one_ref[...], g_two_ref[...]
-        back_to = []
-        for side in range(2):
+        back_to = [None, None]
+
+        def one_side(side):
             columns = []
             for q in range(0, groups, 2):
-                left = held[(q - me_at + groups) % groups]
-                right = held[(q + 1 - me_at + groups) % groups]
+                left = held[q ^ me_at]
+                right = held[(q + 1) ^ me_at]
                 if side == 0:
                     columns.append(jnp.where(low, left, swap_halves(right)))
                 else:
@@ -459,13 +511,45 @@
             embedded = jnp.concatenate(columns, axis=1)
             rows = pl.ds(side * run, run)
             top = top_ref[rows, :].astype(jnp.float32)
-            act_one, saved_one = forward(embedded, w_one_ref, gain_one_at, 1)
-            hidden = act_one.astype(jnp.bfloat16).astype(jnp.float32)
-            act_two, saved_two = forward(hidden, w_two_ref, gain_two_at, 2)
-            out_ref[rows, :] = (embedded + act_two).astype(jnp.bfloat16)
-            grad_hidden = backward(top, hidden, w_two_ref, gain_two_at, saved_two, 2, sum_two, 1)
-            grad_inner = backward(grad_hidden, embedded, w_one_ref, gain_one_at, saved_one, 1, sum_one, 0)
-            back_to.append(top + grad_inner)
+            stacked = taps(embedded, 1)
+            yield
+            before = jnp.dot(stacked, w_one_ref[...], preferred_element_type=jnp.float32)
+            yield
+
+            def first(before):
+                normal, inv_std, output, slope = activate(before, gain_one_at)
+                return normal, inv_std, output.astype(jnp.bfloat16).astype(jnp.float32), slope
+
+            normal, inv_std, hidden, slope = by_rows(first, before)
+            stacked = taps(hidden, 2)
+            yield
+            before = jnp.dot(stacked, w_two_ref[...], preferred_element_type=jnp.float32)
+            yield
+
+            def second(before, values, grad):
+                normal, inv_std, output, slope = activate(before, gain_two_at)
+                return values + output, unwind(grad, normal, inv_std, slope, gain_two_at, 1)
+
+            output, before = by_rows(second, before, embedded, top)
+            out_ref[rows, :] = output.astype(jnp.bfloat16)
+            yield
+            grad = products(before, hidden, turned_two, 2, sum_two)
+            yield
+
+            def third(grad, normal, inv_std, slope):
+                return (unwind(grad, normal, inv_std, slope, gain_one_at, 0),)
+
+            (before,) = by_rows(third, grad, normal, inv_std, slope)
+            yield
+            back_to[side] = top + products(before, embedded, turned_one, 1, sum_one)
+
+        sides = [one_side(0), one_side(1)]
+        next(sides[0])
+        while sides:
+            for one in sides[::-1]:
+                if next(one, "done") == "done":
+                    sides.remove(one)
+
         for q in range(groups):
             at = slice((q // 2) * LANES, (q // 2 + 1) * LANES)
             first, second = back_to[0][:, at], back_to[1][:, at]
@@ -473,7 +557,7 @@
                 pair = jnp.where(low, first, swap_halves(second))
             else:
                 pair = jnp.where(low, swap_halves(first), second)
-            packed[(q - me_at + groups) % groups] = pair
+            packed[q ^ me_at] = pair
         for k in range(groups):
             grad_refs[k][...] = packed[k].astype(jnp.bfloat16)
 
@@ -484,8 +568,9 @@
                     flat[n * tall + k * width : n * tall + (k + 1) * width, :] = total[
                         :, k * width : (k + 1) * width
                     ].astype(jnp.bfloat16)
+            gains = [jnp.sum(sum_gains[n], axis=0, keepdims=True) for n in range(2)]
             flat[2 * tall : 2 * tall + 16, :] = jnp.concatenate(
-                [sum_gains[...], jnp.zeros_like(sum_gains)], axis=0
+                gains + [jnp.zeros((14, width), jnp.float32)], axis=0
             ).astype(jnp.bfloat16)
             if 2 * groups * chunk > 2 * tall + 16:
                 flat[2 * tall + 16 :, :] = jnp.zeros(
@@ -493,7 +578,7 @@
                 )
             for k in range(groups):
                 for part_ref, side in ((kept_ref, core), (given_ref, 1 - core)):
-                    begin = pl.multiple_of((side * groups + (me_at + k) % groups) * chunk, 16)
+                    begin = pl.multiple_of((side * groups + (me_at ^ k)) * chunk, 16)
                     part_ref[k] = flat[pl.ds(begin, chunk), :]
 
     def whole(shape):
@@ -518,8 +603,10 @@
                 pltpu.VMEM((groups, run, LANES), jnp.float32),
                 pltpu.VMEM((width, tall), jnp.float32),
                 pltpu.VMEM((width, tall), jnp.float32),
-                pltpu.VMEM((8, width), jnp.float32),
+                pltpu.VMEM((2, 8, width), jnp.float32),
                 pltpu.VMEM((2 * groups * chunk, width), jnp.bfloat16),
+                pltpu.VMEM((tall, width), jnp.bfloat16),
+                pltpu.VMEM((tall, width), jnp.bfloat16),
             ],
         ),
         out_shape=[jax.ShapeDtypeStruct((items, width), jnp.bfloat16)]
@@ -538,6 +625,10 @@
     )
 
 
+def together(*values):
+    return lax.optimization_barrier(values)
+
+
 def after(values, *first):
     return lax.optimization_barrier((values, *first))[0]
 
@@ -555,8 +646,8 @@
     plane, core = lax.axis_index("table") // 2, lax.axis_index("table") % 2
     at = jnp.stack([me, core]).astype(jnp.int32)
 
-    def dp_shift(values, k):
-        return lax.ppermute(values, "dp", [(i, (i + k) % groups) for i in range(groups)])
+    def dp_flip(values, k):
+        return lax.ppermute(values, "dp", [(i, i ^ k) for i in range(groups)])
 
     def table_shift(values, k):
         return lax.ppermute(values, "table", [(i, (i + k) % shards) for i in range(shards)])
@@ -583,7 +674,9 @@
 
     first, last, own = own_columns(at, table)
     mine = after(mine, own)
-    all_codes = jnp.concatenate([mine] + [dp_shift(mine, k) for k in range(1, groups)], axis=2)
+    all_codes = mine
+    for k in range((groups - 1).bit_length()):
+        all_codes = jnp.concatenate([all_codes, dp_flip(all_codes, 2**k)], axis=2)
     codes = [(all_codes[t, 0], all_codes[t, 1]) for t in range(tables)]
 
     def from_planes(own, first=None):
@@ -599,8 +692,8 @@
 
     near_first = from_planes(first)
     swapped = across(after(own, all_codes))
-    last = after(last, swapped, near_first[0], near_first[-1])
     far_first = [across(values) for values in near_first]
+    last = after(last, swapped, far_first[0], far_first[-1])
 
     def slots(t, near, far, place):
         return [(own, t), *((v, place) for v in near), (swapped, t), *((v, place) for v in far)]
@@ -609,75 +702,70 @@
     near_last = from_planes(last, total)
     for t in range(1, tables - 1):
         total = look_up(codes[t], slots(t, near_first, far_first, t), total, False)
-    near_last[planes // 2 - 1] = after(near_last[planes // 2 - 1], total)
-    far_last = [across(values) for values in near_last]
+    far_last = [across(after(values, total)) for values in near_last]
     total = look_up(codes[tables - 1], slots(tables - 1, near_last, far_last, 0), total, True)
 
     pieces = total.reshape(groups, items // 2, LANES)
-    arrived = [pieces[0]] + [dp_shift(pieces[k], -k) for k in range(1, groups)]
+    arrived = [pieces[0]] + [dp_flip(pieces[k], k) for k in range(1, groups)]
     done = both_layers(
         at, arrived, weight_one, gain_one, weight_two, gain_two, grad_out.reshape(items, width), length
     )
     block_out = done[0].reshape(sessions, length, width)
     sent, kept, given = done[1 : 1 + groups], done[1 + groups], done[2 + groups]
-    blocks = [sent[0]] + [dp_shift(sent[k], k) for k in range(1, groups)]
+    blocks = [sent[0]] + [dp_flip(sent[k], k) for k in range(1, groups)]
 
     def add_up(parts):
         return sum(part.astype(jnp.float32) for part in parts)
 
     got = across(given)
     chunks = [kept[k].astype(jnp.float32) + got[k].astype(jnp.float32) for k in range(groups)]
-    chunks = [chunks[0]] + [dp_shift(chunk.astype(jnp.bfloat16), k) for k, chunk in enumerate(chunks[1:], 1)]
-
-    def send_on(state):
-        sent = []
-        for side, move in (("up", up), ("down", down)):
-            terms, came = state[side], state["came"].pop(side, None)
-            if terms:
-                value = terms.pop(0)
-                if came is not None:
-                    value = value + came.astype(jnp.float32)
-                sent.append(value.astype(jnp.bfloat16))
-                state["came"][side] = move(sent[-1])
-            elif came is not None:
-                state["home"] = state["home"] + came.astype(jnp.float32)
-        return sent
-
-    states = []
-    sums = add_rows(codes, blocks, shards, half)
-    chunk = add_up([after(part, sums[0][1]) for part in chunks]).astype(jnp.bfloat16)
-    got = None
-    for near, far in sums:
-        got = across(far) if got is None else across(after(far, got))
-        if not states:
-            got = after(got, chunk)
-        sides = [near[r].astype(jnp.float32) + got[r].astype(jnp.float32) for r in range(planes)]
-        states.append(
-            {
-                "home": sides[0],
-                "up": [sides[r] for r in range(planes // 2, 0, -1)],
-                "down": [sides[r] for r in range(planes // 2 + 1, planes)],
-                "came": {},
-            }
-        )
-        send_on(states[-1])
-    sent = [state["came"]["up"] for state in states]
-    while any(state["came"] for state in states):
-        for state in states:
-            send_on(state)
-    grads = [
-        jnp.concatenate([state["home"][:, : LANES // 2], state["home"][:, LANES // 2 :]], axis=0)
-        for state in states
+    chunks = [chunks[0]] + [chunk.astype(jnp.bfloat16) for chunk in chunks[1:]]
+    blocks = [after(block, *chunks) for block in blocks]
+    chunks = [chunks[0]] + [dp_flip(chunk, k) for k, chunk in enumerate(chunks[1:], 1)]
+
+    def side(near, got, r):
+        return near[r].astype(jnp.float32) + got[r].astype(jnp.float32)
+
+    def packed(*values):
+        return jnp.concatenate([value.astype(jnp.bfloat16) for value in values], axis=0)
+
+    (near_0, far_0), (near_1, far_1) = add_rows(codes[:2], blocks, shards, half, 2)
+    far_0, *chunks = together(far_0, *chunks)
+    chunk = add_up(chunks).astype(jnp.bfloat16)
+    got_0 = across(far_0)
+    got_1 = across(after(far_1, got_0))
+    going = [
+        packed(side(near_0, got_0, 2)),
+        packed(side(near_0, got_0, 3)),
+        packed(side(near_1, got_1, 2)),
+        packed(side(near_1, got_1, 3)),
     ]
-    table_grad = jnp.stack(grads, axis=0)
-
-    for k in range((planes - 1).bit_length()):
-        chunk = add_up([chunk, after(plane_flip(chunk, 2**k), sent[min(k, tables - 1)])]).astype(jnp.bfloat16)
-    near = jnp.stack([chunk] + [dp_shift(chunk, k) for k in range(1, groups)], axis=0)
+    came = [up(going[0]), down(going[1]), up(going[2]), down(going[3]), plane_flip(chunk, 1)]
+    blocks = [after(block, *going, chunk) for block in blocks]
+    ((near_2, far_2),) = add_rows(codes[2:], blocks, shards, half, 4)
+    far_2, up_0, down_0, up_1, down_1, other = together(far_2, *came)
+    got_2 = across(far_2)
+    chunk = add_up([chunk, other]).astype(jnp.bfloat16)
+    going = packed(
+        side(near_0, got_0, 1) + up_0.astype(jnp.float32),
+        side(near_1, got_1, 1) + up_1.astype(jnp.float32),
+        side(near_2, got_2, 2),
+    )
+    last_01, down_2, other = together(
+        up(going), down(packed(side(near_2, got_2, 3))), plane_flip(chunk, 2)
+    )
+    chunk = add_up([chunk, other]).astype(jnp.bfloat16)
+    going = packed(side(near_2, got_2, 1) + last_01[2 * half :].astype(jnp.float32))
+    last_2, *chunks = together(up(going), *(dp_flip(chunk, k) for k in range(1, groups)))
+    near = jnp.stack([chunk, *chunks], axis=0)
     far = across(near)
-    sums = scaled_sums(
-        at, near, far, weight_one.shape[0], 1.0 / math.sqrt(items * groups * shards)
-    )
+    sums = scaled_sums(at, near, far, weight_one.shape[0], 1.0 / math.sqrt(items * groups * shards))
+
+    grads = finished(
+        [(near_0, got_0, down_0, last_01, 0), (near_1, got_1, down_1, last_01, 1)], tables, None
+    )
+    grads = finished([(near_2, got_2, down_2, last_2, 0)], tables, grads)
+    table_grad = jnp.transpose(grads, (0, 2, 1))
     return (block_out, sums[0], sums[1], sums[2].reshape(width), sums[3].reshape(width), table_grad)
 
 

time: 222 us -> 211 us (0.950)
  waiting for transfers between devices: 110 us -> 99.8 us
    ppermute x15 -> x13, waiting for transfers between devices: 77 us -> 32 us  [table_shift(): lax.ppermute(values, 'table', [(i, (i + k) % shards) for i in range(shard...]
    ppermute x2, waiting for transfers between devices: 1.36 us -> 37 us  [plane_flip(): lax.ppermute(values, 'table', [(i, i ^ 2 * k) for i in range(shards)])]
    ppermute x15 -> x14, waiting for transfers between devices: 27.3 us -> 23.7 us  [dp_flip(): return lax.ppermute(values, 'dp', [(i, i ^ k) for i in range(groups)])]
    ppermute x2, starting transfers between devices: 3.51 us -> 0.14 us  [plane_flip(): lax.ppermute(values, 'table', [(i, i ^ 2 * k) for i in range(shards)])]
    pallas_call x1, Pallas kernels: 13.5 us -> 10.3 us  [both_layers(): pl.pallas_call(kernel, grid_spec=pltpu.PrefetchScalarGridSpec(num_scalar_...]
    ppermute x12, waiting for transfers between devices: 4.13 us -> 7.02 us  [across(): return lax.ppermute(values, 'table', [(i, i ^ 1) for i in range(shards)])]
    ppermute x15 -> x13, starting transfers between devices: 15.3 us -> 18.2 us  [table_shift(): lax.ppermute(values, 'table', [(i, (i + k) % shards) for i in range(shard...]
    pallas_call x0 -> x2, Pallas kernels: none -> 2.32 us  [finished(): pl.pallas_call(kernel, grid=(1,), in_specs=specs, out_specs=pl.BlockSpec(...]
  transfers between devices with their start and end apart: 44 -> 41, of which waited for: 30 -> 19; matrix products, arithmetic and copies ran while one was open for 1% -> 1% of each run, Pallas kernels for 7% -> 22%
where the time goes in v3:
time: 211 us
  waiting for transfers between devices  99.8 us (47%)
  Pallas kernels  66.3 us (31%)
  starting transfers between devices  36.8 us (17%)
  local copies, waits for them, and re-layouts  4.15 us (2%)
  other arithmetic  2.33 us (1%)
    ppermute x2, waiting for transfers between devices, plane_flip(): lax.ppermute(values, 'table', [(i, i ^ 2 * k) for i in range(shards)])  37 us
    ppermute x13, waiting for transfers between devices, table_shift(): lax.ppermute(values, 'table', [(i, (i + k) % shards) for i in range(shard...  32 us
    pallas_call x2, Pallas kernels, add_rows(): pl.pallas_call(kernel, grid_spec=pltpu.PrefetchScalarGridSpec(num_scalar_...  30.1 us
    ppermute x14, waiting for transfers between devices, dp_flip(): return lax.ppermute(values, 'dp', [(i, i ^ k) for i in range(groups)])  23.7 us
    pallas_call x3, Pallas kernels, look_up(): pl.pallas_call(kernel, grid_spec=pltpu.PrefetchScalarGridSpec(num_scalar_...  20.3 us
    ppermute x13, starting transfers between devices, table_shift(): lax.ppermute(values, 'table', [(i, (i + k) % shards) for i in range(shard...  18.2 us
    ppermute x14, starting transfers between devices, dp_flip(): return lax.ppermute(values, 'dp', [(i, i ^ k) for i in range(groups)])  17.5 us
    pallas_call x1, Pallas kernels, both_layers(): pl.pallas_call(kernel, grid_spec=pltpu.PrefetchScalarGridSpec(num_scalar_...  10.3 us
  transfers between devices with their start and end apart: 41, of which 19 were waited for; matrix products, arithmetic and copies ran while one was open for 1% of the time, Pallas kernels for 22%

profile of v3, /device:TPU:0, one launch (start us, length us, event | category | flops | bytes accessed | tf_op | source)
XLA Modules:
  0.0 210.6 jit_solution(17595403072119595905)
XLA Ops:
  0.7 1.9 copy-done.3
  4.0 3.1 %collective-permute-start.5 = (bf16[2,1024,128]{2,1,0:T(8,128)(2,1)S(1)}, bf16[2,1024,128]{2,1,0:T(8,128)(2,1)S(1)}, u32[]{:S(2)}, u32[]{:S(2)}) collective-permute-start(bf16[2,1024,128]{2,1,0:T(8,128)(2,1)S(1)} %get-tuple-element.64), channel_id=1, source_target_pairs={{0,2},{1,3},{2,4},{3,5},{4,6},{5,7},{6,0},{7,1},{8,10},{9,11},{10,... | collective-permute-start | bytes 1572872 | tf_op jit(solution)/shard_map/ppermute | solution.py:653
  7.5 1.6 collective-permute-start
  9.0 2.2 %collective-permute-start.3 = (bf16[2,1024,128]{2,1,0:T(8,128)(2,1)S(1)}, bf16[2,1024,128]{2,1,0:T(8,128)(2,1)S(1)}, u32[]{:S(2)}, u32[]{:S(2)}) collective-permute-start(bf16[2,1024,128]{2,1,0:T(8,128)(2,1)S(1)} %get-tuple-element.64), channel_id=1, source_target_pairs={{0,6},{1,7},{2,0},{3,1},{4,2},{5,3},{6,4},{7,5},{8,14},{9,15},{10,... | collective-permute-start | bytes 1572872 | tf_op jit(solution)/shard_map/ppermute | solution.py:653
  11.4 1.6 collective-permute-start.1
  13.0 2.5 %collective-permute-done.1 = s32[3,2,1600]{2,1,0:T(2,128)S(1)} collective-permute-done((s32[3,2,1600]{2,1,0:T(2,128)S(1)}, s32[3,2,1600]{2,1,0:T(2,128)S(1)}, u32[]{:S(2)}, u32[]{:S(2)}) %collective-permute-start.1) | collective-permute-done | bytes 38432 | tf_op jit(solution)/shard_map/ppermute | solution.py:650
  15.8 6.1 %collective-permute-done.5.refs_3_ = bf16[2,1024,128]{2,1,0:T(8,128)(2,1)S(1)} collective-permute-done((bf16[2,1024,128]{2,1,0:T(8,128)(2,1)S(1)}, bf16[2,1024,128]{2,1,0:T(8,128)(2,1)S(1)}, u32[]{:S(2)}, u32[]{:S(2)}) %collective-permute-start.5) | collective-permute-done | bytes 524320 | tf_op jit(solution)/shard_map/ppermute | solution.py:653
  21.9 11.1 %collective-permute-done.3.refs_1_ = bf16[2,1024,128]{2,1,0:T(8,128)(2,1)S(1)} collective-permute-done((bf16[2,1024,128]{2,1,0:T(8,128)(2,1)S(1)}, bf16[2,1024,128]{2,1,0:T(8,128)(2,1)S(1)}, u32[]{:S(2)}, u32[]{:S(2)}) %collective-permute-start.3) | collective-permute-done | bytes 524320 | tf_op jit(solution)/shard_map/ppermute | solution.py:653
  33.0 10.5 %collective-permute-done.9.refs_2_ = bf16[2,1024,128]{2,1,0:T(8,128)(2,1)S(1)} collective-permute-done((bf16[2,1024,128]{2,1,0:T(8,128)(2,1)S(1)}, bf16[2,1024,128]{2,1,0:T(8,128)(2,1)S(1)}, u32[]{:S(2)}, u32[]{:S(2)}) %collective-permute-start.9) | collective-permute-done | bytes 524320 | tf_op jit(solution)/shard_map/ppermute | solution.py:653
  43.9 3.9 %collective-permute-start.7 = (bf16[1,1024,128]{2,1,0:T(8,128)(2,1)S(1)}, bf16[1,1024,128]{2,1,0:T(8,128)(2,1)S(1)}, u32[]{:S(2)}, u32[]{:S(2)}) collective-permute-start(bf16[1,1024,128]{2,1,0:T(8,128)(2,1)S(1)} %get-tuple-element.65), channel_id=1, source_target_pairs={{0,6},{1,7},{2,0},{3,1},{4,2},{5,3},{6,4},{7,5},{8,14},{9,15},{10,... | collective-permute-start | bytes 786440 | tf_op jit(solution)/shard_map/ppermute | solution.py:653
  47.7 6.8 %look_up.3.refs_8_ = f32[3200,128]{1,0:T(8,128)S(1)} custom-call(s32[3200]{0:T(1024)S(1)} %get-tuple-element.117.low_ref.refs_0_, s32[3200]{0:T(1024)S(1)} %get-tuple-element.116.high_ref.refs_1_, bf16[3,1024,128]{2,1,0:T(8,128)(2,1)S(1)} %get-tuple-element.63.refs_0_, bf16[2,1024,128]{2,1,0:T(8,128)(2,1)S(1)} %collective-permute-done.3.refs_1_, ...), custom_call_target="tpu_custom_call" | custom-call | bytes 39321600 | tf_op jit(solution)/shard_map/look_up/pallas_call | solution.py:266
  54.8 6.8 %look_up.4.refs_8_ = f32[3200,128]{1,0:T(8,128)S(1)} custom-call(s32[3200]{0:T(1024)S(1)} %get-tuple-element.115.low_ref.refs_2_, s32[3200]{0:T(1024)S(1)} %get-tuple-element.114.high_ref.refs_3_, bf16[3,1024,128]{2,1,0:T(8,128)(2,1)S(1)} %get-tuple-element.63.refs_0_, bf16[2,1024,128]{2,1,0:T(8,128)(2,1)S(1)} %collective-permute-done.3.refs_1_, ...), custom_call_target="tpu_custom_call" | custom-call | bytes 39321600 | tf_op jit(solution)/shard_map/look_up/pallas_call | solution.py:266
  62.2 3.2 %collective-permute-done.11.refs_2_ = bf16[1,1024,128]{2,1,0:T(8,128)(2,1)S(1)} collective-permute-done((bf16[1,1024,128]{2,1,0:T(8,128)(2,1)S(1)}, bf16[1,1024,128]{2,1,0:T(8,128)(2,1)S(1)}, u32[]{:S(2)}, u32[]{:S(2)}) %collective-permute-start.11) | collective-permute-done | bytes 262176 | tf_op jit(solution)/shard_map/ppermute | solution.py:653
  66.9 6.8 %look_up.5 = bf16[3200,128]{1,0:T(8,128)(2,1)S(1)} custom-call(s32[3200]{0:T(1024)S(1)} %get-tuple-element.119.low_ref.refs_0_, s32[3200]{0:T(1024)S(1)} %get-tuple-element.118.high_ref.refs_1_, bf16[3,1024,128]{2,1,0:T(8,128)(2,1)S(1)} %get-tuple-element.63.refs_0_, bf16[1,1024,128]{2,1,0:T(8,128)(2,1)S(1)} %collective-permute-done.7.refs_1_, ...), custom_call_target="tpu_custom_call" | custom-call | bytes 39321600 | tf_op jit(solution)/shard_map/look_up/pallas_call | solution.py:266
  73.8 2.5 %collective-permute-start.17 = (bf16[800,128]{1,0:T(8,128)(2,1)S(1)}, bf16[800,128]{1,0:T(8,128)(2,1)S(1)}, u32[]{:S(2)}, u32[]{:S(2)}) collective-permute-start(bf16[800,128]{1,0:T(8,128)(2,1)S(1)} %get-tuple-element.132), channel_id=1, source_target_pairs={{0,24},{8,16},{16,8},{24,0},{1,25},{9,17},{17,9},{25,1},{2,26},{10... | collective-permute-start | bytes 614408 | tf_op jit(solution)/shard_map/ppermute | solution.py:650
  77.4 5.4 %collective-permute-done.17.refs_3_ = bf16[800,128]{1,0:T(8,128)(2,1)S(1)} collective-permute-done((bf16[800,128]{1,0:T(8,128)(2,1)S(1)}, bf16[800,128]{1,0:T(8,128)(2,1)S(1)}, u32[]{:S(2)}, u32[]{:S(2)}) %collective-permute-start.17) | collective-permute-done | bytes 204832 | tf_op jit(solution)/shard_map/ppermute | solution.py:650
  82.8 3.5 %collective-permute-done.16.refs_2_ = bf16[800,128]{1,0:T(8,128)(2,1)S(1)} collective-permute-done((bf16[800,128]{1,0:T(8,128)(2,1)S(1)}, bf16[800,128]{1,0:T(8,128)(2,1)S(1)}, u32[]{:S(2)}, u32[]{:S(2)}) %collective-permute-start.16) | collective-permute-done | bytes 204832 | tf_op jit(solution)/shard_map/ppermute | solution.py:650
  86.4 10.3 %both_layers.1 = (bf16[1600,256]{1,0:T(8,128)(2,1)}, bf16[800,128]{1,0:T(8,128)(2,1)S(1)}, bf16[800,128]{1,0:T(8,128)(2,1)S(1)}, bf16[800,128]{1,0:T(8,128)(2,1)...) custom-call(s32[2]{0:T(128)S(1)} %pad_add_fusion.1.at_ref.me_ref, ...), custom_call_target="tpu_custom_call" | custom-call | tf_op jit(solution)/shard_map/both_layers/pallas_call | solution.py:590
  101.1 1.7 collective-permute-start.24
  104.1 6.6 %collective-permute-done.21.refs_7_.refs_5_ = bf16[800,128]{1,0:T(8,128)(2,1)S(1)} collective-permute-done((bf16[800,128]{1,0:T(8,128)(2,1)S(1)}, bf16[800,128]{1,0:T(8,128)(2,1)S(1)}, u32[]{:S(2)}, u32[]{:S(2)}) %collective-permute-start.21) | collective-permute-done | bytes 204832 | tf_op jit(solution)/shard_map/ppermute | solution.py:650
  111.5 2.1 collective-permute-done.20.refs_6_.refs_4_
  114.3 18.2 %add_rows.2 = (bf16[4,1024,128]{2,1,0:T(8,128)(2,1)}, bf16[4,1024,128]{2,1,0:T(8,128)(2,1)}, bf16[4,1024,128]{2,1,0:T(8,128)(2,1)}, bf16[4,1024,128]{2,1,0:T(8,128)(2,1)}) custom-call(s32[3200]{0:T(1024)} %copy-done.11, s32[3200]{0:T(1024)} %copy-done.10, s32[3200]{0:T(1024)} %copy-done.9, s32[3200]{0:T(1024)} %copy-done.8, bf16[800,128]{1,0:T(8,128)(2,1)} %copy-done.5, ...), custom_call_target="tpu_custom_call" | custom-call | bytes 83886080 | tf_op jit(solution)/shard_map/add_rows/pallas_call | solution.py:330
  132.5 2.9 %collective-permute-done.25.refs_1_ = bf16[4,1024,128]{2,1,0:T(8,128)(2,1)S(1)} collective-permute-done((bf16[4,1024,128]{2,1,0:T(8,128)(2,1)}, bf16[4,1024,128]{2,1,0:T(8,128)(2,1)S(1)}, u32[]{:S(2)}, u32[]{:S(2)}) %collective-permute-start.25) | collective-permute-done | bytes 1048608 | tf_op jit(solution)/shard_map/ppermute | solution.py:665
  138.9 2.7 %collective-permute-start.30 = (bf16[1024,128]{1,0:T(8,128)(2,1)S(1)}, bf16[1024,128]{1,0:T(8,128)(2,1)S(1)}, u32[]{:S(2)}, u32[]{:S(2)}) collective-permute-start(bf16[1024,128]{1,0:T(8,128)(2,1)S(1)} %get-tuple-element.124), channel_id=1, source_target_pairs={{0,6},{1,7},{2,0},{3,1},{4,2},{5,3},{6,4},{7,5},{8,14},{9,15},{10,... | collective-permute-start | bytes 786440 | tf_op jit(solution)/shard_map/ppermute | solution.py:653
  141.8 11.9 %add_rows.3 = (bf16[4,1024,128]{2,1,0:T(8,128)(2,1)}, bf16[4,1024,128]{2,1,0:T(8,128)(2,1)}) custom-call(s32[3200]{0:T(1024)} %copy-done.13, s32[3200]{0:T(1024)} %copy-done.12, bf16[800,128]{1,0:T(8,128)(2,1)} %copy-done.5, bf16[800,128]{1,0:T(8,128)(2,1)} %copy-done.16, bf16[800,128]{1,0:T(8,128)(2,1)} %copy-done.17, bf16[800,128]{1,0:T(8,128)(2,1)} %copy-done.18), custom_call_target="tpu_custom_call" | custom-call | bytes 41943040 | tf_op jit(solution)/shard_map/add_rows/pallas_call | solution.py:330
  153.7 10.8 %collective-permute-done.31 = bf16[208,256]{1,0:T(8,128)(2,1)S(1)} collective-permute-done((bf16[208,256]{1,0:T(8,128)(2,1)S(1)}, bf16[208,256]{1,0:T(8,128)(2,1)S(1)}, u32[]{:S(2)}, u32[]{:S(2)}) %collective-permute-start.31) | collective-permute-done | bytes 106528 | tf_op jit(solution)/shard_map/ppermute | solution.py:662
  164.8 2.6 %collective-permute-done.32.refs_1_ = bf16[4,1024,128]{2,1,0:T(8,128)(2,1)S(1)} collective-permute-done((bf16[4,1024,128]{2,1,0:T(8,128)(2,1)}, bf16[4,1024,128]{2,1,0:T(8,128)(2,1)S(1)}, u32[]{:S(2)}, u32[]{:S(2)}) %collective-permute-start.32) | collective-permute-done | bytes 1048608 | tf_op jit(solution)/shard_map/ppermute | solution.py:665
  168.6 2.9 %collective-permute-start.34 = (bf16[1024,128]{1,0:T(8,128)(2,1)S(1)}, bf16[1024,128]{1,0:T(8,128)(2,1)S(1)}, u32[]{:S(2)}, u32[]{:S(2)}) collective-permute-start(bf16[1024,128]{1,0:T(8,128)(2,1)S(1)} %get-tuple-element.122), channel_id=1, source_target_pairs={{0,6},{1,7},{2,0},{3,1},{4,2},{5,3},{6,4},{7,5},{8,14},{9,15},{10,... | collective-permute-start | bytes 786440 | tf_op jit(solution)/shard_map/ppermute | solution.py:653
  171.6 26.3 %collective-permute-done.35 = bf16[208,256]{1,0:T(8,128)(2,1)S(1)} collective-permute-done((bf16[208,256]{1,0:T(8,128)(2,1)S(1)}, bf16[208,256]{1,0:T(8,128)(2,1)S(1)}, u32[]{:S(2)}, u32[]{:S(2)}) %collective-permute-start.35) | collective-permute-done | bytes 106528 | tf_op jit(solution)/shard_map/ppermute | solution.py:662
  200.1 1.6 collective-permute-start.37
  201.7 2.5 %collective-permute-done.39 = bf16[208,256]{1,0:T(8,128)(2,1)S(1)} collective-permute-done((bf16[208,256]{1,0:T(8,128)(2,1)S(1)}, bf16[208,256]{1,0:T(8,128)(2,1)S(1)}, u32[]{:S(2)}, u32[]{:S(2)}) %collective-permute-start.39) | collective-permute-done | bytes 106528 | tf_op jit(solution)/shard_map/ppermute | solution.py:650
  208.7 1.9 scaled_sums.1
  (128 shorter events, 25.2 us)
Async XLA Ops:
  4.0 17.9 %collective-permute-start.5 = (bf16[2,1024,128]{2,1,0:T(8,128)(2,1)S(1)}, bf16[2,1024,128]{2,1,0:T(8,128)(2,1)S(1)}, u32[]{:S(2)}, u32[]{:S(2)}) collective-permute-start(bf16[2,1024,128]{2,1,0:T(8,128)(2,1)S(1)} %get-tuple-element.64), channel_id=1, source_target_pairs={{0,2},{1,3},{2,4},{3,5},{4,6},{5,7},{6,0},{7,1},{8,10},{9,11},{10,... | collective-permute-start | bytes 1572872 | tf_op jit(solution)/shard_map/ppermute | solution.py:653
  9.0 24.0 %collective-permute-start.3 = (bf16[2,1024,128]{2,1,0:T(8,128)(2,1)S(1)}, bf16[2,1024,128]{2,1,0:T(8,128)(2,1)S(1)}, u32[]{:S(2)}, u32[]{:S(2)}) collective-permute-start(bf16[2,1024,128]{2,1,0:T(8,128)(2,1)S(1)} %get-tuple-element.64), channel_id=1, source_target_pairs={{0,6},{1,7},{2,0},{3,1},{4,2},{5,3},{6,4},{7,5},{8,14},{9,15},{10,... | collective-permute-start | bytes 1572872 | tf_op jit(solution)/shard_map/ppermute | solution.py:653
  11.4 4.1 %collective-permute-start.1 = (s32[3,2,1600]{2,1,0:T(2,128)S(1)}, s32[3,2,1600]{2,1,0:T(2,128)S(1)}, u32[]{:S(2)}, u32[]{:S(2)}) collective-permute-start(s32[3,2,1600]{2,1,0:T(2,128)S(1)} %pad_add_fusion), channel_id=1, source_target_pairs={{0,16},{8,24},{16,0},{24,8},{1,17},{9,25},{17,1},{25,9},{2,18},{10... | collective-permute-start | bytes 115208 | tf_op jit(solution)/shard_map/ppermute | solution.py:650
  15.7 27.8 %collective-permute-start.2 = (bf16[3,1024,128]{2,1,0:T(8,128)(2,1)S(1)}, bf16[3,1024,128]{2,1,0:T(8,128)(2,1)S(1)}, u32[]{:S(2)}, u32[]{:S(2)}) collective-permute-start(bf16[3,1024,128]{2,1,0:T(8,128)(2,1)S(1)} %get-tuple-element.63.refs_0_), channel_id=1, source_target_pairs={{0,1},{1,0},{2,3},{3,2},{4,5},{5,4},{6,7},{7,6},{8,9},{9,8},{10,11... | collective-permute-start | bytes 2359304 | tf_op jit(solution)/shard_map/ppermute | solution.py:665
  21.9 21.6 %collective-permute-start.9 = (bf16[2,1024,128]{2,1,0:T(8,128)(2,1)S(1)}, bf16[2,1024,128]{2,1,0:T(8,128)(2,1)S(1)}, u32[]{:S(2)}, u32[]{:S(2)}) collective-permute-start(bf16[2,1024,128]{2,1,0:T(8,128)(2,1)S(1)} %collective-permute-done.5.refs_3_), channel_id=1, source_target_pairs={{0,2},{1,3},{2,4},{3,5},{4,6},{5,7},{6,0},{7,1},{8,10},{9,11},{10,... | collective-permute-start | bytes 1572872 | tf_op jit(solution)/shard_map/ppermute | solution.py:653
  21.9 21.6 %collective-permute-start.6 = (bf16[2,1024,128]{2,1,0:T(8,128)(2,1)S(1)}, bf16[2,1024,128]{2,1,0:T(8,128)(2,1)S(1)}, u32[]{:S(2)}, u32[]{:S(2)}) collective-permute-start(bf16[2,1024,128]{2,1,0:T(8,128)(2,1)S(1)} %collective-permute-done.5.refs_3_), channel_id=1, source_target_pairs={{0,1},{1,0},{2,3},{3,2},{4,5},{5,4},{6,7},{7,6},{8,9},{9,8},{10,11... | collective-permute-start | bytes 1572872 | tf_op jit(solution)/shard_map/ppermute | solution.py:665
  33.0 10.5 %collective-permute-start.4 = (bf16[2,1024,128]{2,1,0:T(8,128)(2,1)S(1)}, bf16[2,1024,128]{2,1,0:T(8,128)(2,1)S(1)}, u32[]{:S(2)}, u32[]{:S(2)}) collective-permute-start(bf16[2,1024,128]{2,1,0:T(8,128)(2,1)S(1)} %collective-permute-done.3.refs_1_), channel_id=1, source_target_pairs={{0,1},{1,0},{2,3},{3,2},{4,5},{5,4},{6,7},{7,6},{8,9},{9,8},{10,11... | collective-permute-start | bytes 1572872 | tf_op jit(solution)/shard_map/ppermute | solution.py:665
  43.5 4.2 %collective-permute-start.10 = (bf16[2,1024,128]{2,1,0:T(8,128)(2,1)S(1)}, bf16[2,1024,128]{2,1,0:T(8,128)(2,1)S(1)}, u32[]{:S(2)}, u32[]{:S(2)}) collective-permute-start(bf16[2,1024,128]{2,1,0:T(8,128)(2,1)S(1)} %collective-permute-done.9.refs_2_), channel_id=1, source_target_pairs={{0,1},{1,0},{2,3},{3,2},{4,5},{5,4},{6,7},{7,6},{8,9},{9,8},{10,11... | collective-permute-start | bytes 1572872 | tf_op jit(solution)/shard_map/ppermute | solution.py:665
  43.5 11.0 %collective-permute-start.8 = (bf16[1,1024,128]{2,1,0:T(8,128)(2,1)S(1)}, bf16[1,1024,128]{2,1,0:T(8,128)(2,1)S(1)}, u32[]{:S(2)}, u32[]{:S(2)}) collective-permute-start(bf16[1,1024,128]{2,1,0:T(8,128)(2,1)S(1)} %get-tuple-element.65), channel_id=1, source_target_pairs={{0,2},{1,3},{2,4},{3,5},{4,6},{5,7},{6,0},{7,1},{8,10},{9,11},{10,... | collective-permute-start | bytes 786440 | tf_op jit(solution)/shard_map/ppermute | solution.py:653
  43.9 17.7 %collective-permute-start.7 = (bf16[1,1024,128]{2,1,0:T(8,128)(2,1)S(1)}, bf16[1,1024,128]{2,1,0:T(8,128)(2,1)S(1)}, u32[]{:S(2)}, u32[]{:S(2)}) collective-permute-start(bf16[1,1024,128]{2,1,0:T(8,128)(2,1)S(1)} %get-tuple-element.65), channel_id=1, source_target_pairs={{0,6},{1,7},{2,0},{3,1},{4,2},{5,3},{6,4},{7,5},{8,14},{9,15},{10,... | collective-permute-start | bytes 786440 | tf_op jit(solution)/shard_map/ppermute | solution.py:653
  54.5 10.8 %collective-permute-start.11 = (bf16[1,1024,128]{2,1,0:T(8,128)(2,1)S(1)}, bf16[1,1024,128]{2,1,0:T(8,128)(2,1)S(1)}, u32[]{:S(2)}, u32[]{:S(2)}) collective-permute-start(bf16[1,1024,128]{2,1,0:T(8,128)(2,1)S(1)} %collective-permute-done.8.refs_3_), channel_id=1, source_target_pairs={{0,2},{1,3},{2,4},{3,5},{4,6},{5,7},{6,0},{7,1},{8,10},{9,11},{10,... | collective-permute-start | bytes 786440 | tf_op jit(solution)/shard_map/ppermute | solution.py:653
  73.8 8.9 %collective-permute-start.17 = (bf16[800,128]{1,0:T(8,128)(2,1)S(1)}, bf16[800,128]{1,0:T(8,128)(2,1)S(1)}, u32[]{:S(2)}, u32[]{:S(2)}) collective-permute-start(bf16[800,128]{1,0:T(8,128)(2,1)S(1)} %get-tuple-element.132), channel_id=1, source_target_pairs={{0,24},{8,16},{16,8},{24,0},{1,25},{9,17},{17,9},{25,1},{2,26},{10... | collective-permute-start | bytes 614408 | tf_op jit(solution)/shard_map/ppermute | solution.py:650
  76.4 10.0 %collective-permute-start.16 = (bf16[800,128]{1,0:T(8,128)(2,1)S(1)}, bf16[800,128]{1,0:T(8,128)(2,1)S(1)}, u32[]{:S(2)}, u32[]{:S(2)}) collective-permute-start(bf16[800,128]{1,0:T(8,128)(2,1)S(1)} %get-tuple-element.133), channel_id=1, source_target_pairs={{0,16},{8,24},{16,0},{24,8},{1,17},{9,25},{17,1},{25,9},{2,18},{10... | collective-permute-start | bytes 614408 | tf_op jit(solution)/shard_map/ppermute | solution.py:650
  76.9 9.6 %collective-permute-start.15 = (bf16[800,128]{1,0:T(8,128)(2,1)S(1)}, bf16[800,128]{1,0:T(8,128)(2,1)S(1)}, u32[]{:S(2)}, u32[]{:S(2)}) collective-permute-start(bf16[800,128]{1,0:T(8,128)(2,1)S(1)} %get-tuple-element.134), channel_id=1, source_target_pairs={{0,8},{8,0},{16,24},{24,16},{1,9},{9,1},{17,25},{25,17},{2,10},{10... | collective-permute-start | bytes 614408 | tf_op jit(solution)/shard_map/ppermute | solution.py:650
  97.5 16.1 %collective-permute-start.19 = (bf16[800,128]{1,0:T(8,128)(2,1)S(1)}, bf16[800,128]{1,0:T(8,128)(2,1)S(1)}, u32[]{:S(2)}, u32[]{:S(2)}) collective-permute-start(bf16[800,128]{1,0:T(8,128)(2,1)S(1)} %get-tuple-element.75), channel_id=1, source_target_pairs={{0,8},{8,0},{16,24},{24,16},{1,9},{9,1},{17,25},{25,17},{2,10},{10... | collective-permute-start | bytes 614408 | tf_op jit(solution)/shard_map/ppermute | solution.py:650
  98.9 14.6 %collective-permute-start.20 = (bf16[800,128]{1,0:T(8,128)(2,1)S(1)}, bf16[800,128]{1,0:T(8,128)(2,1)S(1)}, u32[]{:S(2)}, u32[]{:S(2)}) collective-permute-start(bf16[800,128]{1,0:T(8,128)(2,1)S(1)} %get-tuple-element.77), channel_id=1, source_target_pairs={{0,16},{8,24},{16,0},{24,8},{1,17},{9,25},{17,1},{25,9},{2,18},{10... | collective-permute-start | bytes 614408 | tf_op jit(solution)/shard_map/ppermute | solution.py:650
  99.7 11.0 %collective-permute-start.21 = (bf16[800,128]{1,0:T(8,128)(2,1)S(1)}, bf16[800,128]{1,0:T(8,128)(2,1)S(1)}, u32[]{:S(2)}, u32[]{:S(2)}) collective-permute-start(bf16[800,128]{1,0:T(8,128)(2,1)S(1)} %get-tuple-element.79), channel_id=1, source_target_pairs={{0,24},{8,16},{16,8},{24,0},{1,25},{9,17},{17,9},{25,1},{2,26},{10... | collective-permute-start | bytes 614408 | tf_op jit(solution)/shard_map/ppermute | solution.py:650
  101.1 31.4 %collective-permute-start.24 = (bf16[208,256]{1,0:T(8,128)(2,1)S(1)}, bf16[208,256]{1,0:T(8,128)(2,1)S(1)}, u32[]{:S(2)}, u32[]{:S(2)}) collective-permute-start(bf16[208,256]{1,0:T(8,128)(2,1)S(1)} %get-tuple-element.128), channel_id=1, source_target_pairs={{0,24},{8,16},{16,8},{24,0},{1,25},{9,17},{17,9},{25,1},{2,26},{10... | collective-permute-start | bytes 319496 | tf_op jit(solution)/shard_map/ppermute | solution.py:650
  102.8 29.7 %collective-permute-start.23 = (bf16[208,256]{1,0:T(8,128)(2,1)S(1)}, bf16[208,256]{1,0:T(8,128)(2,1)S(1)}, u32[]{:S(2)}, u32[]{:S(2)}) collective-permute-start(bf16[208,256]{1,0:T(8,128)(2,1)S(1)} %get-tuple-element.129), channel_id=1, source_target_pairs={{0,16},{8,24},{16,0},{24,8},{1,17},{9,25},{17,1},{25,9},{2,18},{10... | collective-permute-start | bytes 319496 | tf_op jit(solution)/shard_map/ppermute | solution.py:650
  110.7 21.7 %collective-permute-start.22 = (bf16[208,256]{1,0:T(8,128)(2,1)S(1)}, bf16[208,256]{1,0:T(8,128)(2,1)S(1)}, u32[]{:S(2)}, u32[]{:S(2)}) collective-permute-start(bf16[208,256]{1,0:T(8,128)(2,1)S(1)} %get-tuple-element.130), channel_id=1, source_target_pairs={{0,8},{8,0},{16,24},{24,16},{1,9},{9,1},{17,25},{25,17},{2,10},{10... | collective-permute-start | bytes 319496 | tf_op jit(solution)/shard_map/ppermute | solution.py:650
  136.7 27.8 %collective-permute-start.28 = (bf16[1024,128]{1,0:T(8,128)(2,1)S(1)}, bf16[1024,128]{1,0:T(8,128)(2,1)S(1)}, u32[]{:S(2)}, u32[]{:S(2)}) collective-permute-start(bf16[1024,128]{1,0:T(8,128)(2,1)S(1)} %get-tuple-element.126), channel_id=1, source_target_pairs={{0,6},{1,7},{2,0},{3,1},{4,2},{5,3},{6,4},{7,5},{8,14},{9,15},{10,... | collective-permute-start | bytes 786440 | tf_op jit(solution)/shard_map/ppermute | solution.py:653
  137.6 26.9 %collective-permute-start.27 = (bf16[1024,128]{1,0:T(8,128)(2,1)S(1)}, bf16[1024,128]{1,0:T(8,128)(2,1)S(1)}, u32[]{:S(2)}, u32[]{:S(2)}) collective-permute-start(bf16[1024,128]{1,0:T(8,128)(2,1)S(1)} %get-tuple-element.127), channel_id=1, source_target_pairs={{0,2},{1,3},{2,4},{3,5},{4,6},{5,7},{6,0},{7,1},{8,10},{9,11},{10,... | collective-permute-start | bytes 786440 | tf_op jit(solution)/shard_map/ppermute | solution.py:653
  138.9 25.5 %collective-permute-start.30 = (bf16[1024,128]{1,0:T(8,128)(2,1)S(1)}, bf16[1024,128]{1,0:T(8,128)(2,1)S(1)}, u32[]{:S(2)}, u32[]{:S(2)}) collective-permute-start(bf16[1024,128]{1,0:T(8,128)(2,1)S(1)} %get-tuple-element.124), channel_id=1, source_target_pairs={{0,6},{1,7},{2,0},{3,1},{4,2},{5,3},{6,4},{7,5},{8,14},{9,15},{10,... | collective-permute-start | bytes 786440 | tf_op jit(solution)/shard_map/ppermute | solution.py:653
  141.6 22.9 %collective-permute-start.29 = (bf16[1024,128]{1,0:T(8,128)(2,1)S(1)}, bf16[1024,128]{1,0:T(8,128)(2,1)S(1)}, u32[]{:S(2)}, u32[]{:S(2)}) collective-permute-start(bf16[1024,128]{1,0:T(8,128)(2,1)S(1)} %get-tuple-element.125), channel_id=1, source_target_pairs={{0,2},{1,3},{2,4},{3,5},{4,6},{5,7},{6,0},{7,1},{8,10},{9,11},{10,... | collective-permute-start | bytes 786440 | tf_op jit(solution)/shard_map/ppermute | solution.py:653
  141.7 22.8 %collective-permute-start.31 = (bf16[208,256]{1,0:T(8,128)(2,1)S(1)}, bf16[208,256]{1,0:T(8,128)(2,1)S(1)}, u32[]{:S(2)}, u32[]{:S(2)}) collective-permute-start(bf16[208,256]{1,0:T(8,128)(2,1)S(1)} %add_convert_fusion.8), channel_id=1, source_target_pairs={{0,2},{1,3},{2,0},{3,1},{4,6},{5,7},{6,4},{7,5},{8,10},{9,11},{10,... | collective-permute-start | bytes 319496 | tf_op jit(solution)/shard_map/ppermute | solution.py:662
  167.6 30.2 %collective-permute-start.33 = (bf16[3072,128]{1,0:T(8,128)(2,1)S(1)}, bf16[3072,128]{1,0:T(8,128)(2,1)S(1)}, u32[]{:S(2)}, u32[]{:S(2)}) collective-permute-start(bf16[3072,128]{1,0:T(8,128)(2,1)S(1)} %pad_maximum_fusion), channel_id=1, source_target_pairs={{0,2},{1,3},{2,4},{3,5},{4,6},{5,7},{6,0},{7,1},{8,10},{9,11},{10,... | collective-permute-start | bytes 2359304 | tf_op jit(solution)/shard_map/ppermute | solution.py:653
  168.6 29.3 %collective-permute-start.34 = (bf16[1024,128]{1,0:T(8,128)(2,1)S(1)}, bf16[1024,128]{1,0:T(8,128)(2,1)S(1)}, u32[]{:S(2)}, u32[]{:S(2)}) collective-permute-start(bf16[1024,128]{1,0:T(8,128)(2,1)S(1)} %get-tuple-element.122), channel_id=1, source_target_pairs={{0,6},{1,7},{2,0},{3,1},{4,2},{5,3},{6,4},{7,5},{8,14},{9,15},{10,... | collective-permute-start | bytes 786440 | tf_op jit(solution)/shard_map/ppermute | solution.py:653
  171.6 26.3 %collective-permute-start.35 = (bf16[208,256]{1,0:T(8,128)(2,1)S(1)}, bf16[208,256]{1,0:T(8,128)(2,1)S(1)}, u32[]{:S(2)}, u32[]{:S(2)}) collective-permute-start(bf16[208,256]{1,0:T(8,128)(2,1)S(1)} %add_convert_fusion.7), channel_id=1, source_target_pairs={{0,4},{1,5},{2,6},{3,7},{4,0},{5,1},{6,2},{7,3},{8,12},{9,13},{10,... | collective-permute-start | bytes 319496 | tf_op jit(solution)/shard_map/ppermute | solution.py:662
  198.0 8.2 %collective-permute-start.36 = (bf16[1024,128]{1,0:T(8,128)(2,1)S(1)}, bf16[1024,128]{1,0:T(8,128)(2,1)S(1)}, u32[]{:S(2)}, u32[]{:S(2)}) collective-permute-start(bf16[1024,128]{1,0:T(8,128)(2,1)S(1)} %fusion), channel_id=1, source_target_pairs={{0,2},{1,3},{2,4},{3,5},{4,6},{5,7},{6,0},{7,1},{8,10},{9,11},{10,... | collective-permute-start | bytes 786440 | tf_op jit(solution)/shard_map/ppermute | solution.py:653
  198.1 6.0 %collective-permute-start.39 = (bf16[208,256]{1,0:T(8,128)(2,1)S(1)}, bf16[208,256]{1,0:T(8,128)(2,1)S(1)}, u32[]{:S(2)}, u32[]{:S(2)}) collective-permute-start(bf16[208,256]{1,0:T(8,128)(2,1)S(1)} %add_convert_fusion.6), channel_id=1, source_target_pairs={{0,24},{8,16},{16,8},{24,0},{1,25},{9,17},{17,9},{25,1},{2,26},{10... | collective-permute-start | bytes 319496 | tf_op jit(solution)/shard_map/ppermute | solution.py:650
  199.6 5.6 %collective-permute-start.38 = (bf16[208,256]{1,0:T(8,128)(2,1)S(1)}, bf16[208,256]{1,0:T(8,128)(2,1)S(1)}, u32[]{:S(2)}, u32[]{:S(2)}) collective-permute-start(bf16[208,256]{1,0:T(8,128)(2,1)S(1)} %add_convert_fusion.6), channel_id=1, source_target_pairs={{0,16},{8,24},{16,0},{24,8},{1,17},{9,25},{17,1},{25,9},{2,18},{10... | collective-permute-start | bytes 319496 | tf_op jit(solution)/shard_map/ppermute | solution.py:650
  200.1 5.1 %collective-permute-start.37 = (bf16[208,256]{1,0:T(8,128)(2,1)S(1)}, bf16[208,256]{1,0:T(8,128)(2,1)S(1)}, u32[]{:S(2)}, u32[]{:S(2)}) collective-permute-start(bf16[208,256]{1,0:T(8,128)(2,1)S(1)} %add_convert_fusion.6), channel_id=1, source_target_pairs={{0,8},{8,0},{16,24},{24,16},{1,9},{9,1},{17,25},{25,17},{2,10},{10... | collective-permute-start | bytes 319496 | tf_op jit(solution)/shard_map/ppermute | solution.py:650
  (30 other events, 244.6 us)

commit v4 on v3

--- a/solution.py
+++ b/solution.py
@@ -12,6 +12,7 @@
 LANES = 128
 MIB = 2**20
 
+CHAINS = 4
 UNROLL = 16
 ROWS = 40
 
@@ -276,7 +277,7 @@
             ],
         ),
         out_shape=jax.ShapeDtypeStruct((count, LANES), jnp.bfloat16 if last else jnp.float32),
-        compiler_params=pltpu.CompilerParams(vmem_limit_bytes=32 * MIB),
+        compiler_params=pltpu.CompilerParams(vmem_limit_bytes=20 * MIB),
         cost_estimate=pl.CostEstimate(
             flops=0, bytes_accessed=8 * 3 * count * LANES * 4, transcendentals=0
         ),
@@ -338,7 +339,7 @@
             + [pltpu.VMEM((2 * shards * half, LANES), jnp.float32)] * (tables * chains),
         ),
         out_shape=[jax.ShapeDtypeStruct((planes, half, LANES), jnp.bfloat16)] * (2 * tables),
-        compiler_params=pltpu.CompilerParams(vmem_limit_bytes=56 * MIB),
+        compiler_params=pltpu.CompilerParams(vmem_limit_bytes=42 * MIB),
         cost_estimate=pl.CostEstimate(
             flops=0, bytes_accessed=tables * 40 * MIB, transcendentals=0
         ),
@@ -347,10 +348,9 @@
     return list(zip(results[::2], results[1::2]))
 
 
-def finished(parts, tables, earlier):
+def finished(parts, begin, tables, earlier):
     _, half, lanes = parts[0][0].shape
     count = len(parts)
-    begin = 0 if earlier is None else tables - count
 
     def kernel(*refs):
         refs, out_ref = refs[:-1], refs[-1]
@@ -366,9 +366,9 @@
         return pl.BlockSpec((half, lanes), lambda i: (n, 0))
 
     operands, specs = [], []
-    for near, got, down, last, n in parts:
+    for near, got, down, d, last, n in parts:
         operands += [near, got, down, last]
-        specs += [own, own, row_block(0), row_block(n)]
+        specs += [own, own, row_block(d), row_block(n)]
     if earlier is not None:
         operands.append(earlier)
         specs.append(pl.BlockSpec(memory_space=pl.ANY))
@@ -612,7 +612,7 @@
         out_shape=[jax.ShapeDtypeStruct((items, width), jnp.bfloat16)]
         + [jax.ShapeDtypeStruct((items // 2, LANES), jnp.bfloat16)] * groups
         + [jax.ShapeDtypeStruct((groups, chunk, width), jnp.bfloat16)] * 2,
-        compiler_params=pltpu.CompilerParams(vmem_limit_bytes=48 * MIB),
+        compiler_params=pltpu.CompilerParams(vmem_limit_bytes=32 * MIB),
         name="both_layers",
     )(
         me,
@@ -658,9 +658,6 @@
     def down(values):
         return table_shift(values, -2)
 
-    def plane_flip(values, k):
-        return lax.ppermute(values, "table", [(i, i ^ (2 * k)) for i in range(shards)])
-
     def across(values):
         return lax.ppermute(values, "table", [(i, i ^ 1) for i in range(shards)])
 
@@ -729,42 +726,40 @@
     def packed(*values):
         return jnp.concatenate([value.astype(jnp.bfloat16) for value in values], axis=0)
 
+    ((near_2, far_2),) = add_rows(codes[2:], blocks, shards, half, 4)
+    far_2, *chunks[:-1] = together(far_2, *chunks[:-1])
+    chunk = add_up(chunks).astype(jnp.bfloat16)
+    got_2 = across(far_2)
+    going = [packed(side(near_2, got_2, 2)), packed(side(near_2, got_2, 3)), chunk]
+    came = [up(going[0]), down(going[1]), *(table_shift(chunk, k) for k in (shards // 2, 2, -2))]
+    blocks = [after(block, *going) for block in blocks]
     (near_0, far_0), (near_1, far_1) = add_rows(codes[:2], blocks, shards, half, 2)
-    far_0, *chunks = together(far_0, *chunks)
-    chunk = add_up(chunks).astype(jnp.bfloat16)
+    far_0, up_2, down_2, *chunks = together(far_0, *came)
     got_0 = across(far_0)
     got_1 = across(after(far_1, got_0))
-    going = [
-        packed(side(near_0, got_0, 2)),
-        packed(side(near_0, got_0, 3)),
-        packed(side(near_1, got_1, 2)),
-        packed(side(near_1, got_1, 3)),
-    ]
-    came = [up(going[0]), down(going[1]), up(going[2]), down(going[3]), plane_flip(chunk, 1)]
-    blocks = [after(block, *going, chunk) for block in blocks]
-    ((near_2, far_2),) = add_rows(codes[2:], blocks, shards, half, 4)
-    far_2, up_0, down_0, up_1, down_1, other = together(far_2, *came)
-    got_2 = across(far_2)
-    chunk = add_up([chunk, other]).astype(jnp.bfloat16)
+    chunk = (add_up([chunk, chunks[0]]) + add_up(chunks[1:])).astype(jnp.bfloat16)
     going = packed(
-        side(near_0, got_0, 1) + up_0.astype(jnp.float32),
-        side(near_1, got_1, 1) + up_1.astype(jnp.float32),
-        side(near_2, got_2, 2),
-    )
-    last_01, down_2, other = together(
-        up(going), down(packed(side(near_2, got_2, 3))), plane_flip(chunk, 2)
-    )
-    chunk = add_up([chunk, other]).astype(jnp.bfloat16)
-    going = packed(side(near_2, got_2, 1) + last_01[2 * half :].astype(jnp.float32))
-    last_2, *chunks = together(up(going), *(dp_flip(chunk, k) for k in range(1, groups)))
+        side(near_2, got_2, 1) + up_2.astype(jnp.float32), side(near_0, got_0, 2), side(near_1, got_1, 2)
+    )
+    up_01, down_01, *chunks = together(
+        up(going),
+        down(packed(side(near_0, got_0, 3), side(near_1, got_1, 3))),
+        *(dp_flip(chunk, k) for k in range(1, groups)),
+    )
     near = jnp.stack([chunk, *chunks], axis=0)
-    far = across(near)
+    going = packed(
+        side(near_0, got_0, 1) + up_01[half : 2 * half].astype(jnp.float32),
+        side(near_1, got_1, 1) + up_01[2 * half :].astype(jnp.float32),
+    )
+    last_01, far = up(going), across(near)
     sums = scaled_sums(at, near, far, weight_one.shape[0], 1.0 / math.sqrt(items * groups * shards))
 
+    near_2 = after(near_2, *sums)
+    grads = finished([(near_2, got_2, down_2, 0, up_01, 0)], 2, tables, None)
+    last_01, grads = together(last_01, grads)
     grads = finished(
-        [(near_0, got_0, down_0, last_01, 0), (near_1, got_1, down_1, last_01, 1)], tables, None
-    )
-    grads = finished([(near_2, got_2, down_2, last_2, 0)], tables, grads)
+        [(near_0, got_0, down_01, 0, last_01, 0), (near_1, got_1, down_01, 1, last_01, 1)], 0, tables, grads
+    )
     table_grad = jnp.transpose(grads, (0, 2, 1))
     return (block_out, sums[0], sums[1], sums[2].reshape(width), sums[3].reshape(width), table_grad)
 

time: 211 us -> 199 us (0.943)
  waiting for transfers between devices: 99.8 us -> 92.4 us
  Pallas kernels: 66.3 us -> 61.3 us
  starting transfers between devices: 36.8 us -> 40.5 us
    ppermute x2 -> x0, waiting for transfers between devices: 37 us -> none  [plane_flip(): lax.ppermute(values, 'table', [(i, i ^ 2 * k) for i in range(shards)])]
    ppermute x13 -> x14, waiting for transfers between devices: 32 us -> 59.2 us  [table_shift(): lax.ppermute(values, 'table', [(i, (i + k) % shards) for i in range(shard...]
    pallas_call x2, Pallas kernels: 30.1 us -> 25.1 us  [add_rows(): pl.pallas_call(kernel, grid_spec=pltpu.PrefetchScalarGridSpec(num_scalar_...]
    ppermute x13 -> x14, starting transfers between devices: 18.2 us -> 22.5 us  [table_shift(): lax.ppermute(values, 'table', [(i, (i + k) % shards) for i in range(shard...]
    ppermute x12, waiting for transfers between devices: 7.02 us -> 9.64 us  [across(): return lax.ppermute(values, 'table', [(i, i ^ 1) for i in range(shards)])]
  transfers between devices with their start and end apart: 41 -> 40, of which waited for: 19 -> 21; matrix products, arithmetic and copies ran while one was open for 1% -> 1% of each run, Pallas kernels for 22% -> 21%
where the time goes in v4:
time: 199 us
  waiting for transfers between devices  92.4 us (46%)
  Pallas kernels  61.3 us (31%)
  starting transfers between devices  40.5 us (20%)
  local copies, waits for them, and re-layouts  2.69 us (1%)
    ppermute x14, waiting for transfers between devices, table_shift(): lax.ppermute(values, 'table', [(i, (i + k) % shards) for i in range(shard...  59.2 us
    pallas_call x2, Pallas kernels, add_rows(): pl.pallas_call(kernel, grid_spec=pltpu.PrefetchScalarGridSpec(num_scalar_...  25.1 us
    ppermute x14, waiting for transfers between devices, dp_flip(): return lax.ppermute(values, 'dp', [(i, i ^ k) for i in range(groups)])  23.6 us
    ppermute x14, starting transfers between devices, table_shift(): lax.ppermute(values, 'table', [(i, (i + k) % shards) for i in range(shard...  22.5 us
    pallas_call x3, Pallas kernels, look_up(): pl.pallas_call(kernel, grid_spec=pltpu.PrefetchScalarGridSpec(num_scalar_...  20.3 us
    ppermute x14, starting transfers between devices, dp_flip(): return lax.ppermute(values, 'dp', [(i, i ^ k) for i in range(groups)])  17.1 us
    pallas_call x1, Pallas kernels, both_layers(): pl.pallas_call(kernel, grid_spec=pltpu.PrefetchScalarGridSpec(num_scalar_...  10.3 us
    ppermute x12, waiting for transfers between devices, across(): return lax.ppermute(values, 'table', [(i, i ^ 1) for i in range(shards)])  9.64 us
  transfers between devices with their start and end apart: 40, of which 21 were waited for; matrix products, arithmetic and copies ran while one was open for 1% of the time, Pallas kernels for 21%

profile of v4, /device:TPU:0, one launch (start us, length us, event | category | flops | bytes accessed | tf_op | source)
XLA Modules:
  0.0 199.3 jit_solution(5042632109510704820)
XLA Ops:
  0.7 1.9 copy-done
  4.0 3.1 %collective-permute-start.5 = (bf16[2,1024,128]{2,1,0:T(8,128)(2,1)S(1)}, bf16[2,1024,128]{2,1,0:T(8,128)(2,1)S(1)}, u32[]{:S(2)}, u32[]{:S(2)}) collective-permute-start(bf16[2,1024,128]{2,1,0:T(8,128)(2,1)S(1)} %get-tuple-element.64), channel_id=1, source_target_pairs={{0,2},{1,3},{2,4},{3,5},{4,6},{5,7},{6,0},{7,1},{8,10},{9,11},{10,... | collective-permute-start | bytes 1572872 | tf_op jit(solution)/shard_map/ppermute | solution.py:653
  9.0 2.2 %collective-permute-start.3 = (bf16[2,1024,128]{2,1,0:T(8,128)(2,1)S(1)}, bf16[2,1024,128]{2,1,0:T(8,128)(2,1)S(1)}, u32[]{:S(2)}, u32[]{:S(2)}) collective-permute-start(bf16[2,1024,128]{2,1,0:T(8,128)(2,1)S(1)} %get-tuple-element.64), channel_id=1, source_target_pairs={{0,6},{1,7},{2,0},{3,1},{4,2},{5,3},{6,4},{7,5},{8,14},{9,15},{10,... | collective-permute-start | bytes 1572872 | tf_op jit(solution)/shard_map/ppermute | solution.py:653
  11.4 1.6 collective-permute-start.1
  13.0 2.5 %collective-permute-done.1 = s32[3,2,1600]{2,1,0:T(2,128)S(1)} collective-permute-done((s32[3,2,1600]{2,1,0:T(2,128)S(1)}, s32[3,2,1600]{2,1,0:T(2,128)S(1)}, u32[]{:S(2)}, u32[]{:S(2)}) %collective-permute-start.1) | collective-permute-done | bytes 38432 | tf_op jit(solution)/shard_map/ppermute | solution.py:650
  15.8 6.1 %collective-permute-done.5.refs_3_ = bf16[2,1024,128]{2,1,0:T(8,128)(2,1)S(1)} collective-permute-done((bf16[2,1024,128]{2,1,0:T(8,128)(2,1)S(1)}, bf16[2,1024,128]{2,1,0:T(8,128)(2,1)S(1)}, u32[]{:S(2)}, u32[]{:S(2)}) %collective-permute-start.5) | collective-permute-done | bytes 524320 | tf_op jit(solution)/shard_map/ppermute | solution.py:653
  21.9 11.1 %collective-permute-done.3.refs_1_ = bf16[2,1024,128]{2,1,0:T(8,128)(2,1)S(1)} collective-permute-done((bf16[2,1024,128]{2,1,0:T(8,128)(2,1)S(1)}, bf16[2,1024,128]{2,1,0:T(8,128)(2,1)S(1)}, u32[]{:S(2)}, u32[]{:S(2)}) %collective-permute-start.3) | collective-permute-done | bytes 524320 | tf_op jit(solution)/shard_map/ppermute | solution.py:653
  33.0 10.5 %collective-permute-done.9.refs_2_ = bf16[2,1024,128]{2,1,0:T(8,128)(2,1)S(1)} collective-permute-done((bf16[2,1024,128]{2,1,0:T(8,128)(2,1)S(1)}, bf16[2,1024,128]{2,1,0:T(8,128)(2,1)S(1)}, u32[]{:S(2)}, u32[]{:S(2)}) %collective-permute-start.9) | collective-permute-done | bytes 524320 | tf_op jit(solution)/shard_map/ppermute | solution.py:653
  43.8 3.9 %collective-permute-start.7 = (bf16[1,1024,128]{2,1,0:T(8,128)(2,1)S(1)}, bf16[1,1024,128]{2,1,0:T(8,128)(2,1)S(1)}, u32[]{:S(2)}, u32[]{:S(2)}) collective-permute-start(bf16[1,1024,128]{2,1,0:T(8,128)(2,1)S(1)} %get-tuple-element.65), channel_id=1, source_target_pairs={{0,6},{1,7},{2,0},{3,1},{4,2},{5,3},{6,4},{7,5},{8,14},{9,15},{10,... | collective-permute-start | bytes 786440 | tf_op jit(solution)/shard_map/ppermute | solution.py:653
  47.7 6.8 %look_up.3.refs_8_ = f32[3200,128]{1,0:T(8,128)S(1)} custom-call(s32[3200]{0:T(1024)S(1)} %get-tuple-element.117.low_ref.refs_0_, s32[3200]{0:T(1024)S(1)} %get-tuple-element.116.high_ref.refs_1_, bf16[3,1024,128]{2,1,0:T(8,128)(2,1)S(1)} %get-tuple-element.63.refs_0_, bf16[2,1024,128]{2,1,0:T(8,128)(2,1)S(1)} %collective-permute-done.3.refs_1_, ...), custom_call_target="tpu_custom_call" | custom-call | bytes 39321600 | tf_op jit(solution)/shard_map/look_up/pallas_call | solution.py:267
  54.7 6.8 %look_up.4.refs_8_ = f32[3200,128]{1,0:T(8,128)S(1)} custom-call(s32[3200]{0:T(1024)S(1)} %get-tuple-element.115.low_ref.refs_2_, s32[3200]{0:T(1024)S(1)} %get-tuple-element.114.high_ref.refs_3_, bf16[3,1024,128]{2,1,0:T(8,128)(2,1)S(1)} %get-tuple-element.63.refs_0_, bf16[2,1024,128]{2,1,0:T(8,128)(2,1)S(1)} %collective-permute-done.3.refs_1_, ...), custom_call_target="tpu_custom_call" | custom-call | bytes 39321600 | tf_op jit(solution)/shard_map/look_up/pallas_call | solution.py:267
  62.1 3.3 %collective-permute-done.11.refs_2_ = bf16[1,1024,128]{2,1,0:T(8,128)(2,1)S(1)} collective-permute-done((bf16[1,1024,128]{2,1,0:T(8,128)(2,1)S(1)}, bf16[1,1024,128]{2,1,0:T(8,128)(2,1)S(1)}, u32[]{:S(2)}, u32[]{:S(2)}) %collective-permute-start.11) | collective-permute-done | bytes 262176 | tf_op jit(solution)/shard_map/ppermute | solution.py:653
  66.9 6.8 %look_up.5 = bf16[3200,128]{1,0:T(8,128)(2,1)S(1)} custom-call(s32[3200]{0:T(1024)S(1)} %get-tuple-element.119.low_ref.refs_0_, s32[3200]{0:T(1024)S(1)} %get-tuple-element.118.high_ref.refs_1_, bf16[3,1024,128]{2,1,0:T(8,128)(2,1)S(1)} %get-tuple-element.63.refs_0_, bf16[1,1024,128]{2,1,0:T(8,128)(2,1)S(1)} %collective-permute-done.7.refs_1_, ...), custom_call_target="tpu_custom_call" | custom-call | bytes 39321600 | tf_op jit(solution)/shard_map/look_up/pallas_call | solution.py:267
  77.4 4.4 %collective-permute-done.15.refs_1_ = bf16[800,128]{1,0:T(8,128)(2,1)S(1)} collective-permute-done((bf16[800,128]{1,0:T(8,128)(2,1)S(1)}, bf16[800,128]{1,0:T(8,128)(2,1)S(1)}, u32[]{:S(2)}, u32[]{:S(2)}) %collective-permute-start.15) | collective-permute-done | bytes 204832 | tf_op jit(solution)/shard_map/ppermute | solution.py:650
  81.8 4.8 %collective-permute-done.16.refs_2_ = bf16[800,128]{1,0:T(8,128)(2,1)S(1)} collective-permute-done((bf16[800,128]{1,0:T(8,128)(2,1)S(1)}, bf16[800,128]{1,0:T(8,128)(2,1)S(1)}, u32[]{:S(2)}, u32[]{:S(2)}) %collective-permute-start.16) | collective-permute-done | bytes 204832 | tf_op jit(solution)/shard_map/ppermute | solution.py:650
  86.7 10.3 %both_layers.1 = (bf16[1600,256]{1,0:T(8,128)(2,1)}, bf16[800,128]{1,0:T(8,128)(2,1)S(1)}, bf16[800,128]{1,0:T(8,128)(2,1)S(1)}, bf16[800,128]{1,0:T(8,128)(2,1)...) custom-call(s32[2]{0:T(128)S(1)} %pad_add_fusion.1.at_ref.me_ref, ...), custom_call_target="tpu_custom_call" | custom-call | tf_op jit(solution)/shard_map/both_layers/pallas_call | solution.py:590
  102.7 3.1 %collective-permute-done.21.refs_5_.refs_7_ = bf16[800,128]{1,0:T(8,128)(2,1)S(1)} collective-permute-done((bf16[800,128]{1,0:T(8,128)(2,1)S(1)}, bf16[800,128]{1,0:T(8,128)(2,1)S(1)}, u32[]{:S(2)}, u32[]{:S(2)}) %collective-permute-start.21) | collective-permute-done | bytes 204832 | tf_op jit(solution)/shard_map/ppermute | solution.py:650
  105.8 4.0 %collective-permute-done.20.refs_4_.refs_6_ = bf16[800,128]{1,0:T(8,128)(2,1)S(1)} collective-permute-done((bf16[800,128]{1,0:T(8,128)(2,1)S(1)}, bf16[800,128]{1,0:T(8,128)(2,1)S(1)}, u32[]{:S(2)}, u32[]{:S(2)}) %collective-permute-start.20) | collective-permute-done | bytes 204832 | tf_op jit(solution)/shard_map/ppermute | solution.py:650
  110.3 9.6 %add_rows.2 = (bf16[4,1024,128]{2,1,0:T(8,128)(2,1)S(1)}, bf16[4,1024,128]{2,1,0:T(8,128)(2,1)S(1)}) custom-call(s32[3200]{0:T(1024)S(1)} %get-tuple-element.119.low_ref.refs_0_, s32[3200]{0:T(1024)S(1)} %get-tuple-element.118.high_ref.refs_1_, bf16[800,128]{1,0:T(8,128)(2,1)S(1)} %get-tuple-element.87.refs_2_.refs_4_, ...), custom_call_target="tpu_custom_call" | custom-call | bytes 41943040 | tf_op jit(solution)/shard_map/add_rows/pallas_call | solution.py:331
  122.8 3.8 %collective-permute-start.27 = (bf16[1024,128]{1,0:T(8,128)(2,1)S(1)}, bf16[1024,128]{1,0:T(8,128)(2,1)S(1)}, u32[]{:S(2)}, u32[]{:S(2)}) collective-permute-start(bf16[1024,128]{1,0:T(8,128)(2,1)S(1)} %get-tuple-element.126), channel_id=1, source_target_pairs={{0,6},{1,7},{2,0},{3,1},{4,2},{5,3},{6,4},{7,5},{8,14},{9,15},{10,... | collective-permute-start | bytes 786440 | tf_op jit(solution)/shard_map/ppermute | solution.py:653
  127.6 3.0 %collective-permute-start.30 = (bf16[208,256]{1,0:T(8,128)(2,1)S(1)}, bf16[208,256]{1,0:T(8,128)(2,1)S(1)}, u32[]{:S(2)}, u32[]{:S(2)}) collective-permute-start(bf16[208,256]{1,0:T(8,128)(2,1)S(1)} %add_convert_fusion.7), channel_id=1, source_target_pairs={{0,6},{1,7},{2,0},{3,1},{4,2},{5,3},{6,4},{7,5},{8,14},{9,15},{10,... | collective-permute-start | bytes 319496 | tf_op jit(solution)/shard_map/ppermute | solution.py:653
  130.6 15.5 %add_rows.3 = (bf16[4,1024,128]{2,1,0:T(8,128)(2,1)S(1)}, bf16[4,1024,128]{2,1,0:T(8,128)(2,1)S(1)}, bf16[4,1024,128]{2,1,0:T(8,128)(2,1)S(1)}, bf16[4,1024,128]{2,1,0:T(8,128)(2,1)S(1)}) custom-call(s32[3200]{0:T(1024)S(1)} %get-tuple-element.117.low_ref.refs_0_, s32[3200]{0:T(1024)S(1)} %get-tuple-element.116.high_ref.refs_1_, ...), custom_call_target="tpu_custom_call" | custom-call | bytes 83886080 | tf_op jit(solution)/shard_map/add_rows/pallas_call | solution.py:331
  146.3 2.6 %collective-permute-done.31.refs_1_ = bf16[4,1024,128]{2,1,0:T(8,128)(2,1)S(1)} collective-permute-done((bf16[4,1024,128]{2,1,0:T(8,128)(2,1)S(1)}, bf16[4,1024,128]{2,1,0:T(8,128)(2,1)S(1)}, u32[]{:S(2)}, u32[]{:S(2)}) %collective-permute-start.31) | collective-permute-done | bytes 1048608 | tf_op jit(solution)/shard_map/ppermute | solution.py:662
  149.3 2.3 %collective-permute-done.32.refs_5_ = bf16[4,1024,128]{2,1,0:T(8,128)(2,1)S(1)} collective-permute-done((bf16[4,1024,128]{2,1,0:T(8,128)(2,1)S(1)}, bf16[4,1024,128]{2,1,0:T(8,128)(2,1)S(1)}, u32[]{:S(2)}, u32[]{:S(2)}) %collective-permute-start.32) | collective-permute-done | bytes 1048608 | tf_op jit(solution)/shard_map/ppermute | solution.py:662
  151.9 3.9 %collective-permute-start.34 = (bf16[2048,128]{1,0:T(8,128)(2,1)S(1)}, bf16[2048,128]{1,0:T(8,128)(2,1)S(1)}, u32[]{:S(2)}, u32[]{:S(2)}) collective-permute-start(bf16[2048,128]{1,0:T(8,128)(2,1)S(1)} %pad_maximum_fusion.1), channel_id=1, source_target_pairs={{0,6},{1,7},{2,0},{3,1},{4,2},{5,3},{6,4},{7,5},{8,14},{9,15},{10,... | collective-permute-start | bytes 1572872 | tf_op jit(solution)/shard_map/ppermute | solution.py:653
  157.6 1.8 collective-permute-start.37
  159.4 2.0 %collective-permute-done.35 = bf16[208,256]{1,0:T(8,128)(2,1)S(1)} collective-permute-done((bf16[208,256]{1,0:T(8,128)(2,1)S(1)}, bf16[208,256]{1,0:T(8,128)(2,1)S(1)}, u32[]{:S(2)}, u32[]{:S(2)}) %collective-permute-start.35) | collective-permute-done | bytes 106528 | tf_op jit(solution)/shard_map/ppermute | solution.py:650
  161.4 2.2 %collective-permute-done.36 = bf16[208,256]{1,0:T(8,128)(2,1)S(1)} collective-permute-done((bf16[208,256]{1,0:T(8,128)(2,1)S(1)}, bf16[208,256]{1,0:T(8,128)(2,1)S(1)}, u32[]{:S(2)}, u32[]{:S(2)}) %collective-permute-start.36) | collective-permute-done | bytes 106528 | tf_op jit(solution)/shard_map/ppermute | solution.py:650
  163.6 19.2 %collective-permute-done.34.refs_2_.refs_6_ = bf16[2048,128]{1,0:T(8,128)(2,1)S(1)} collective-permute-done((bf16[2048,128]{1,0:T(8,128)(2,1)S(1)}, bf16[2048,128]{1,0:T(8,128)(2,1)S(1)}, u32[]{:S(2)}, u32[]{:S(2)}) %collective-permute-start.34) | collective-permute-done | bytes 524320 | tf_op jit(solution)/shard_map/ppermute | solution.py:653
  184.5 1.8 collective-permute-done.38.far_ref
  186.3 1.9 scaled_sums.1
  189.2 8.8 %collective-permute-done.39.refs_3_.refs_7_ = bf16[2048,128]{1,0:T(8,128)(2,1)S(1)} collective-permute-done((bf16[2048,128]{1,0:T(8,128)(2,1)S(1)}, bf16[2048,128]{1,0:T(8,128)(2,1)S(1)}, u32[]{:S(2)}, u32[]{:S(2)}) %collective-permute-start.39) | collective-permute-done | bytes 524320 | tf_op jit(solution)/shard_map/ppermute | solution.py:653
  (100 shorter events, 26.8 us)
Async XLA Ops:
  4.0 17.9 %collective-permute-start.5 = (bf16[2,1024,128]{2,1,0:T(8,128)(2,1)S(1)}, bf16[2,1024,128]{2,1,0:T(8,128)(2,1)S(1)}, u32[]{:S(2)}, u32[]{:S(2)}) collective-permute-start(bf16[2,1024,128]{2,1,0:T(8,128)(2,1)S(1)} %get-tuple-element.64), channel_id=1, source_target_pairs={{0,2},{1,3},{2,4},{3,5},{4,6},{5,7},{6,0},{7,1},{8,10},{9,11},{10,... | collective-permute-start | bytes 1572872 | tf_op jit(solution)/shard_map/ppermute | solution.py:653
  9.0 24.0 %collective-permute-start.3 = (bf16[2,1024,128]{2,1,0:T(8,128)(2,1)S(1)}, bf16[2,1024,128]{2,1,0:T(8,128)(2,1)S(1)}, u32[]{:S(2)}, u32[]{:S(2)}) collective-permute-start(bf16[2,1024,128]{2,1,0:T(8,128)(2,1)S(1)} %get-tuple-element.64), channel_id=1, source_target_pairs={{0,6},{1,7},{2,0},{3,1},{4,2},{5,3},{6,4},{7,5},{8,14},{9,15},{10,... | collective-permute-start | bytes 1572872 | tf_op jit(solution)/shard_map/ppermute | solution.py:653
  11.4 4.1 %collective-permute-start.1 = (s32[3,2,1600]{2,1,0:T(2,128)S(1)}, s32[3,2,1600]{2,1,0:T(2,128)S(1)}, u32[]{:S(2)}, u32[]{:S(2)}) collective-permute-start(s32[3,2,1600]{2,1,0:T(2,128)S(1)} %pad_add_fusion), channel_id=1, source_target_pairs={{0,16},{8,24},{16,0},{24,8},{1,17},{9,25},{17,1},{25,9},{2,18},{10... | collective-permute-start | bytes 115208 | tf_op jit(solution)/shard_map/ppermute | solution.py:650
  15.7 27.8 %collective-permute-start.2 = (bf16[3,1024,128]{2,1,0:T(8,128)(2,1)S(1)}, bf16[3,1024,128]{2,1,0:T(8,128)(2,1)S(1)}, u32[]{:S(2)}, u32[]{:S(2)}) collective-permute-start(bf16[3,1024,128]{2,1,0:T(8,128)(2,1)S(1)} %get-tuple-element.63.refs_0_), channel_id=1, source_target_pairs={{0,1},{1,0},{2,3},{3,2},{4,5},{5,4},{6,7},{7,6},{8,9},{9,8},{10,11... | collective-permute-start | bytes 2359304 | tf_op jit(solution)/shard_map/ppermute | solution.py:662
  21.9 21.6 %collective-permute-start.9 = (bf16[2,1024,128]{2,1,0:T(8,128)(2,1)S(1)}, bf16[2,1024,128]{2,1,0:T(8,128)(2,1)S(1)}, u32[]{:S(2)}, u32[]{:S(2)}) collective-permute-start(bf16[2,1024,128]{2,1,0:T(8,128)(2,1)S(1)} %collective-permute-done.5.refs_3_), channel_id=1, source_target_pairs={{0,2},{1,3},{2,4},{3,5},{4,6},{5,7},{6,0},{7,1},{8,10},{9,11},{10,... | collective-permute-start | bytes 1572872 | tf_op jit(solution)/shard_map/ppermute | solution.py:653
  21.9 21.6 %collective-permute-start.6 = (bf16[2,1024,128]{2,1,0:T(8,128)(2,1)S(1)}, bf16[2,1024,128]{2,1,0:T(8,128)(2,1)S(1)}, u32[]{:S(2)}, u32[]{:S(2)}) collective-permute-start(bf16[2,1024,128]{2,1,0:T(8,128)(2,1)S(1)} %collective-permute-done.5.refs_3_), channel_id=1, source_target_pairs={{0,1},{1,0},{2,3},{3,2},{4,5},{5,4},{6,7},{7,6},{8,9},{9,8},{10,11... | collective-permute-start | bytes 1572872 | tf_op jit(solution)/shard_map/ppermute | solution.py:662
  33.0 10.5 %collective-permute-start.4 = (bf16[2,1024,128]{2,1,0:T(8,128)(2,1)S(1)}, bf16[2,1024,128]{2,1,0:T(8,128)(2,1)S(1)}, u32[]{:S(2)}, u32[]{:S(2)}) collective-permute-start(bf16[2,1024,128]{2,1,0:T(8,128)(2,1)S(1)} %collective-permute-done.3.refs_1_), channel_id=1, source_target_pairs={{0,1},{1,0},{2,3},{3,2},{4,5},{5,4},{6,7},{7,6},{8,9},{9,8},{10,11... | collective-permute-start | bytes 1572872 | tf_op jit(solution)/shard_map/ppermute | solution.py:662
  43.5 4.1 %collective-permute-start.10 = (bf16[2,1024,128]{2,1,0:T(8,128)(2,1)S(1)}, bf16[2,1024,128]{2,1,0:T(8,128)(2,1)S(1)}, u32[]{:S(2)}, u32[]{:S(2)}) collective-permute-start(bf16[2,1024,128]{2,1,0:T(8,128)(2,1)S(1)} %collective-permute-done.9.refs_2_), channel_id=1, source_target_pairs={{0,1},{1,0},{2,3},{3,2},{4,5},{5,4},{6,7},{7,6},{8,9},{9,8},{10,11... | collective-permute-start | bytes 1572872 | tf_op jit(solution)/shard_map/ppermute | solution.py:662
  43.5 11.0 %collective-permute-start.8 = (bf16[1,1024,128]{2,1,0:T(8,128)(2,1)S(1)}, bf16[1,1024,128]{2,1,0:T(8,128)(2,1)S(1)}, u32[]{:S(2)}, u32[]{:S(2)}) collective-permute-start(bf16[1,1024,128]{2,1,0:T(8,128)(2,1)S(1)} %get-tuple-element.65), channel_id=1, source_target_pairs={{0,2},{1,3},{2,4},{3,5},{4,6},{5,7},{6,0},{7,1},{8,10},{9,11},{10,... | collective-permute-start | bytes 786440 | tf_op jit(solution)/shard_map/ppermute | solution.py:653
  43.8 17.8 %collective-permute-start.7 = (bf16[1,1024,128]{2,1,0:T(8,128)(2,1)S(1)}, bf16[1,1024,128]{2,1,0:T(8,128)(2,1)S(1)}, u32[]{:S(2)}, u32[]{:S(2)}) collective-permute-start(bf16[1,1024,128]{2,1,0:T(8,128)(2,1)S(1)} %get-tuple-element.65), channel_id=1, source_target_pairs={{0,6},{1,7},{2,0},{3,1},{4,2},{5,3},{6,4},{7,5},{8,14},{9,15},{10,... | collective-permute-start | bytes 786440 | tf_op jit(solution)/shard_map/ppermute | solution.py:653
  54.5 10.8 %collective-permute-start.11 = (bf16[1,1024,128]{2,1,0:T(8,128)(2,1)S(1)}, bf16[1,1024,128]{2,1,0:T(8,128)(2,1)S(1)}, u32[]{:S(2)}, u32[]{:S(2)}) collective-permute-start(bf16[1,1024,128]{2,1,0:T(8,128)(2,1)S(1)} %collective-permute-done.8.refs_3_), channel_id=1, source_target_pairs={{0,2},{1,3},{2,4},{3,5},{4,6},{5,7},{6,0},{7,1},{8,10},{9,11},{10,... | collective-permute-start | bytes 786440 | tf_op jit(solution)/shard_map/ppermute | solution.py:653
  61.5 3.9 %collective-permute-start.14 = (bf16[1,1024,128]{2,1,0:T(8,128)(2,1)S(1)}, bf16[1,1024,128]{2,1,0:T(8,128)(2,1)S(1)}, u32[]{:S(2)}, u32[]{:S(2)}) collective-permute-start(bf16[1,1024,128]{2,1,0:T(8,128)(2,1)S(1)} %collective-permute-done.8.refs_3_), channel_id=1, source_target_pairs={{0,1},{1,0},{2,3},{3,2},{4,5},{5,4},{6,7},{7,6},{8,9},{9,8},{10,11... | collective-permute-start | bytes 786440 | tf_op jit(solution)/shard_map/ppermute | solution.py:662
  73.8 8.0 %collective-permute-start.15 = (bf16[800,128]{1,0:T(8,128)(2,1)S(1)}, bf16[800,128]{1,0:T(8,128)(2,1)S(1)}, u32[]{:S(2)}, u32[]{:S(2)}) collective-permute-start(bf16[800,128]{1,0:T(8,128)(2,1)S(1)} %get-tuple-element.134), channel_id=1, source_target_pairs={{0,8},{8,0},{16,24},{24,16},{1,9},{9,1},{17,25},{25,17},{2,10},{10... | collective-permute-start | bytes 614408 | tf_op jit(solution)/shard_map/ppermute | solution.py:650
  75.4 11.2 %collective-permute-start.16 = (bf16[800,128]{1,0:T(8,128)(2,1)S(1)}, bf16[800,128]{1,0:T(8,128)(2,1)S(1)}, u32[]{:S(2)}, u32[]{:S(2)}) collective-permute-start(bf16[800,128]{1,0:T(8,128)(2,1)S(1)} %get-tuple-element.133), channel_id=1, source_target_pairs={{0,16},{8,24},{16,0},{24,8},{1,17},{9,25},{17,1},{25,9},{2,18},{10... | collective-permute-start | bytes 614408 | tf_op jit(solution)/shard_map/ppermute | solution.py:650
  76.9 9.7 %collective-permute-start.17 = (bf16[800,128]{1,0:T(8,128)(2,1)S(1)}, bf16[800,128]{1,0:T(8,128)(2,1)S(1)}, u32[]{:S(2)}, u32[]{:S(2)}) collective-permute-start(bf16[800,128]{1,0:T(8,128)(2,1)S(1)} %get-tuple-element.132), channel_id=1, source_target_pairs={{0,24},{8,16},{16,8},{24,0},{1,25},{9,17},{17,9},{25,1},{2,26},{10... | collective-permute-start | bytes 614408 | tf_op jit(solution)/shard_map/ppermute | solution.py:650
  97.0 8.8 %collective-permute-start.21 = (bf16[800,128]{1,0:T(8,128)(2,1)S(1)}, bf16[800,128]{1,0:T(8,128)(2,1)S(1)}, u32[]{:S(2)}, u32[]{:S(2)}) collective-permute-start(bf16[800,128]{1,0:T(8,128)(2,1)S(1)} %get-tuple-element.79), channel_id=1, source_target_pairs={{0,24},{8,16},{16,8},{24,0},{1,25},{9,17},{17,9},{25,1},{2,26},{10... | collective-permute-start | bytes 614408 | tf_op jit(solution)/shard_map/ppermute | solution.py:650
  98.5 11.4 %collective-permute-start.20 = (bf16[800,128]{1,0:T(8,128)(2,1)S(1)}, bf16[800,128]{1,0:T(8,128)(2,1)S(1)}, u32[]{:S(2)}, u32[]{:S(2)}) collective-permute-start(bf16[800,128]{1,0:T(8,128)(2,1)S(1)} %get-tuple-element.77), channel_id=1, source_target_pairs={{0,16},{8,24},{16,0},{24,8},{1,17},{9,25},{17,1},{25,9},{2,18},{10... | collective-permute-start | bytes 614408 | tf_op jit(solution)/shard_map/ppermute | solution.py:650
  99.7 10.6 %collective-permute-start.19 = (bf16[800,128]{1,0:T(8,128)(2,1)S(1)}, bf16[800,128]{1,0:T(8,128)(2,1)S(1)}, u32[]{:S(2)}, u32[]{:S(2)}) collective-permute-start(bf16[800,128]{1,0:T(8,128)(2,1)S(1)} %get-tuple-element.75), channel_id=1, source_target_pairs={{0,8},{8,0},{16,24},{24,16},{1,9},{9,1},{17,25},{25,17},{2,10},{10... | collective-permute-start | bytes 614408 | tf_op jit(solution)/shard_map/ppermute | solution.py:650
  100.6 19.2 %collective-permute-start.22 = (bf16[208,256]{1,0:T(8,128)(2,1)S(1)}, bf16[208,256]{1,0:T(8,128)(2,1)S(1)}, u32[]{:S(2)}, u32[]{:S(2)}) collective-permute-start(bf16[208,256]{1,0:T(8,128)(2,1)S(1)} %get-tuple-element.130), channel_id=1, source_target_pairs={{0,8},{8,0},{16,24},{24,16},{1,9},{9,1},{17,25},{25,17},{2,10},{10... | collective-permute-start | bytes 319496 | tf_op jit(solution)/shard_map/ppermute | solution.py:650
  101.9 18.0 %collective-permute-start.23 = (bf16[208,256]{1,0:T(8,128)(2,1)S(1)}, bf16[208,256]{1,0:T(8,128)(2,1)S(1)}, u32[]{:S(2)}, u32[]{:S(2)}) collective-permute-start(bf16[208,256]{1,0:T(8,128)(2,1)S(1)} %get-tuple-element.129), channel_id=1, source_target_pairs={{0,16},{8,24},{16,0},{24,8},{1,17},{9,25},{17,1},{25,9},{2,18},{10... | collective-permute-start | bytes 319496 | tf_op jit(solution)/shard_map/ppermute | solution.py:650
  119.9 6.7 %collective-permute-start.24 = (bf16[208,256]{1,0:T(8,128)(2,1)S(1)}, bf16[208,256]{1,0:T(8,128)(2,1)S(1)}, u32[]{:S(2)}, u32[]{:S(2)}) collective-permute-start(bf16[208,256]{1,0:T(8,128)(2,1)S(1)} %get-tuple-element.128), channel_id=1, source_target_pairs={{0,24},{8,16},{16,8},{24,0},{1,25},{9,17},{17,9},{25,1},{2,26},{10... | collective-permute-start | bytes 319496 | tf_op jit(solution)/shard_map/ppermute | solution.py:650
  122.7 23.5 %collective-permute-start.26 = (bf16[1024,128]{1,0:T(8,128)(2,1)S(1)}, bf16[1024,128]{1,0:T(8,128)(2,1)S(1)}, u32[]{:S(2)}, u32[]{:S(2)}) collective-permute-start(bf16[1024,128]{1,0:T(8,128)(2,1)S(1)} %get-tuple-element.127), channel_id=1, source_target_pairs={{0,2},{1,3},{2,4},{3,5},{4,6},{5,7},{6,0},{7,1},{8,10},{9,11},{10,... | collective-permute-start | bytes 786440 | tf_op jit(solution)/shard_map/ppermute | solution.py:653
  122.8 23.4 %collective-permute-start.27 = (bf16[1024,128]{1,0:T(8,128)(2,1)S(1)}, bf16[1024,128]{1,0:T(8,128)(2,1)S(1)}, u32[]{:S(2)}, u32[]{:S(2)}) collective-permute-start(bf16[1024,128]{1,0:T(8,128)(2,1)S(1)} %get-tuple-element.126), channel_id=1, source_target_pairs={{0,6},{1,7},{2,0},{3,1},{4,2},{5,3},{6,4},{7,5},{8,14},{9,15},{10,... | collective-permute-start | bytes 786440 | tf_op jit(solution)/shard_map/ppermute | solution.py:653
  126.6 19.5 %collective-permute-start.28 = (bf16[208,256]{1,0:T(8,128)(2,1)S(1)}, bf16[208,256]{1,0:T(8,128)(2,1)S(1)}, u32[]{:S(2)}, u32[]{:S(2)}) collective-permute-start(bf16[208,256]{1,0:T(8,128)(2,1)S(1)} %add_convert_fusion.7), channel_id=1, source_target_pairs={{0,4},{1,5},{2,6},{3,7},{4,0},{5,1},{6,2},{7,3},{8,12},{9,13},{10,... | collective-permute-start | bytes 319496 | tf_op jit(solution)/shard_map/ppermute | solution.py:653
  126.7 19.4 %collective-permute-start.29 = (bf16[208,256]{1,0:T(8,128)(2,1)S(1)}, bf16[208,256]{1,0:T(8,128)(2,1)S(1)}, u32[]{:S(2)}, u32[]{:S(2)}) collective-permute-start(bf16[208,256]{1,0:T(8,128)(2,1)S(1)} %add_convert_fusion.7), channel_id=1, source_target_pairs={{0,2},{1,3},{2,4},{3,5},{4,6},{5,7},{6,0},{7,1},{8,10},{9,11},{10,... | collective-permute-start | bytes 319496 | tf_op jit(solution)/shard_map/ppermute | solution.py:653
  127.6 18.5 %collective-permute-start.30 = (bf16[208,256]{1,0:T(8,128)(2,1)S(1)}, bf16[208,256]{1,0:T(8,128)(2,1)S(1)}, u32[]{:S(2)}, u32[]{:S(2)}) collective-permute-start(bf16[208,256]{1,0:T(8,128)(2,1)S(1)} %add_convert_fusion.7), channel_id=1, source_target_pairs={{0,6},{1,7},{2,0},{3,1},{4,2},{5,3},{6,4},{7,5},{8,14},{9,15},{10,... | collective-permute-start | bytes 319496 | tf_op jit(solution)/shard_map/ppermute | solution.py:653
  151.8 31.0 %collective-permute-start.33 = (bf16[3072,128]{1,0:T(8,128)(2,1)S(1)}, bf16[3072,128]{1,0:T(8,128)(2,1)S(1)}, u32[]{:S(2)}, u32[]{:S(2)}) collective-permute-start(bf16[3072,128]{1,0:T(8,128)(2,1)S(1)} %pad_maximum_fusion), channel_id=1, source_target_pairs={{0,2},{1,3},{2,4},{3,5},{4,6},{5,7},{6,0},{7,1},{8,10},{9,11},{10,... | collective-permute-start | bytes 2359304 | tf_op jit(solution)/shard_map/ppermute | solution.py:653
  151.9 30.9 %collective-permute-start.34 = (bf16[2048,128]{1,0:T(8,128)(2,1)S(1)}, bf16[2048,128]{1,0:T(8,128)(2,1)S(1)}, u32[]{:S(2)}, u32[]{:S(2)}) collective-permute-start(bf16[2048,128]{1,0:T(8,128)(2,1)S(1)} %pad_maximum_fusion.1), channel_id=1, source_target_pairs={{0,6},{1,7},{2,0},{3,1},{4,2},{5,3},{6,4},{7,5},{8,14},{9,15},{10,... | collective-permute-start | bytes 1572872 | tf_op jit(solution)/shard_map/ppermute | solution.py:653
  155.8 5.6 %collective-permute-start.35 = (bf16[208,256]{1,0:T(8,128)(2,1)S(1)}, bf16[208,256]{1,0:T(8,128)(2,1)S(1)}, u32[]{:S(2)}, u32[]{:S(2)}) collective-permute-start(bf16[208,256]{1,0:T(8,128)(2,1)S(1)} %add_convert_fusion.6), channel_id=1, source_target_pairs={{0,8},{8,0},{16,24},{24,16},{1,9},{9,1},{17,25},{25,17},{2,10},{10... | collective-permute-start | bytes 319496 | tf_op jit(solution)/shard_map/ppermute | solution.py:650
  156.7 6.9 %collective-permute-start.36 = (bf16[208,256]{1,0:T(8,128)(2,1)S(1)}, bf16[208,256]{1,0:T(8,128)(2,1)S(1)}, u32[]{:S(2)}, u32[]{:S(2)}) collective-permute-start(bf16[208,256]{1,0:T(8,128)(2,1)S(1)} %add_convert_fusion.6), channel_id=1, source_target_pairs={{0,16},{8,24},{16,0},{24,8},{1,17},{9,25},{17,1},{25,9},{2,18},{10... | collective-permute-start | bytes 319496 | tf_op jit(solution)/shard_map/ppermute | solution.py:650
  157.6 6.0 %collective-permute-start.37 = (bf16[208,256]{1,0:T(8,128)(2,1)S(1)}, bf16[208,256]{1,0:T(8,128)(2,1)S(1)}, u32[]{:S(2)}, u32[]{:S(2)}) collective-permute-start(bf16[208,256]{1,0:T(8,128)(2,1)S(1)} %add_convert_fusion.6), channel_id=1, source_target_pairs={{0,24},{8,16},{16,8},{24,0},{1,25},{9,17},{17,9},{25,1},{2,26},{10... | collective-permute-start | bytes 319496 | tf_op jit(solution)/shard_map/ppermute | solution.py:650
  183.0 15.0 %collective-permute-start.39 = (bf16[2048,128]{1,0:T(8,128)(2,1)S(1)}, bf16[2048,128]{1,0:T(8,128)(2,1)S(1)}, u32[]{:S(2)}, u32[]{:S(2)}) collective-permute-start(bf16[2048,128]{1,0:T(8,128)(2,1)S(1)} %pad_maximum_fusion.2), channel_id=1, source_target_pairs={{0,2},{1,3},{2,4},{3,5},{4,6},{5,7},{6,0},{7,1},{8,10},{9,11},{10,... | collective-permute-start | bytes 1572872 | tf_op jit(solution)/shard_map/ppermute | solution.py:653
  (16 other events, 97.9 us)

commit v5 on v4

--- a/solution.py
+++ b/solution.py
@@ -12,7 +12,6 @@
 LANES = 128
 MIB = 2**20
 
-CHAINS = 4
 UNROLL = 16
 ROWS = 40
 
@@ -174,6 +173,7 @@
         and groups > 1
         and (groups & (groups - 1)) == 0
         and sessions % 4 == 0
+        and sessions <= 16
         and run % 16 == 0
         and run % ROWS == 0
         and (groups * sessions * length // 2) % (4 * UNROLL) == 0
@@ -246,14 +246,14 @@
         low = low_lanes(1)
 
         def some(step, carry):
-            for j in range(16):
-                i = step * 16 + j
+            for j in range(2 * UNROLL):
+                i = step * 2 * UNROLL + j
                 for_low = rows[pl.ds(low_ref[i], 1), :]
                 for_high = rows[pl.ds(high_ref[i], 1), :]
                 found[pl.ds(i, 1), :] = jnp.where(low, for_low, for_high)
             return carry
 
-        lax.fori_loop(0, count // 16, some, 0)
+        lax.fori_loop(0, count // (2 * UNROLL), some, 0)
         result = found[...]
         if total_ref is not None:
             result = result + total_ref[...]
@@ -388,15 +388,18 @@
     return -(-(2 * tall + 16) // (32 * groups)) * 16
 
 
-def scaled_sums(at, near, far, tall, scale):
-    groups, chunk, width = near.shape
+def scaled_sums(at, near, far, tall, width, scale):
+    groups = near.shape[0]
+    chunk = near.shape[1] * LANES // width
 
     def kernel(at_ref, near_ref, far_ref, one_ref, two_ref, gain_one_ref, gain_two_ref, flat):
         me, core = at_ref[0], at_ref[1]
         for k in range(groups):
             for part_ref, side in ((near_ref, core), (far_ref, 1 - core)):
                 begin = pl.multiple_of((side * groups + (me ^ k)) * chunk, 16)
-                flat[pl.ds(begin, chunk), :] = part_ref[k].astype(jnp.float32) * scale
+                for n in range(width // LANES):
+                    values = part_ref[k, n * chunk : (n + 1) * chunk, :].astype(jnp.float32)
+                    flat[pl.ds(begin, chunk), n * LANES : (n + 1) * LANES] = values * scale
         one_ref[...] = flat[:tall, :]
         two_ref[...] = flat[tall : 2 * tall, :]
         gain_one_ref[...] = flat[2 * tall : 2 * tall + 1, :]
@@ -431,21 +434,18 @@
         w_one_ref, g_one_ref, w_two_ref, g_two_ref, top_ref, out_ref, *refs = refs
         grad_refs, refs = refs[:groups], refs[groups:]
         kept_ref, given_ref, held, packed, sum_one, sum_two, sum_gains, flat, turned_one, turned_two = refs
-        step = pl.program_id(0)
         me_at, core = me_ref[0], me_ref[1]
         low = low_lanes(run)
         place = lax.broadcasted_iota(jnp.int32, (run, width), 0)
         place = jnp.where(place >= length, place - length, place)
 
-        @pl.when(step == 0)
-        def _():
-            sum_one[...] = jnp.zeros_like(sum_one)
-            sum_two[...] = jnp.zeros_like(sum_two)
-            sum_gains[...] = jnp.zeros_like(sum_gains)
-            for weight_ref, turned_ref in ((w_one_ref, turned_one), (w_two_ref, turned_two)):
-                for k in range(tall // width):
-                    at = slice(k * width, (k + 1) * width)
-                    turned_ref[at, :] = weight_ref[at, :].T
+        sum_one[...] = jnp.zeros_like(sum_one)
+        sum_two[...] = jnp.zeros_like(sum_two)
+        sum_gains[...] = jnp.zeros_like(sum_gains)
+        for weight_ref, turned_ref in ((w_one_ref, turned_one), (w_two_ref, turned_two)):
+            for k in range(tall // width):
+                at = slice(k * width, (k + 1) * width)
+                turned_ref[at, :] = weight_ref[at, :].T
 
         def taps(values, gap):
             one = jnp.where(place >= gap, pltpu.roll(values, gap, 0), 0.0)
@@ -497,19 +497,20 @@
         for k in range(groups):
             held[k] = block_refs[k][...].astype(jnp.float32)
         gain_one_at, gain_two_at = g_one_ref[...], g_two_ref[...]
-        back_to = [None, None]
-
-        def one_side(side):
+        back_to = [None] * (2 * steps)
+
+        def one_part(n):
+            side, packed_rows = n % 2, pl.ds(n // 2 * run, run)
             columns = []
             for q in range(0, groups, 2):
-                left = held[q ^ me_at]
-                right = held[(q + 1) ^ me_at]
+                left = held[q ^ me_at, packed_rows, :]
+                right = held[(q + 1) ^ me_at, packed_rows, :]
                 if side == 0:
                     columns.append(jnp.where(low, left, swap_halves(right)))
                 else:
                     columns.append(jnp.where(low, swap_halves(left), right))
             embedded = jnp.concatenate(columns, axis=1)
-            rows = pl.ds(side * run, run)
+            rows = pl.ds(n * run, run)
             top = top_ref[rows, :].astype(jnp.float32)
             stacked = taps(embedded, 1)
             yield
@@ -541,66 +542,65 @@
 
             (before,) = by_rows(third, grad, normal, inv_std, slope)
             yield
-            back_to[side] = top + products(before, embedded, turned_one, 1, sum_one)
-
-        sides = [one_side(0), one_side(1)]
-        next(sides[0])
-        while sides:
-            for one in sides[::-1]:
+            back_to[n] = top + products(before, embedded, turned_one, 1, sum_one)
+            if side == 0:
+                return
+            for q in range(groups):
+                at = slice((q // 2) * LANES, (q // 2 + 1) * LANES)
+                first, second = back_to[n - 1][:, at], back_to[n][:, at]
+                if q % 2 == 0:
+                    pair = jnp.where(low, first, swap_halves(second))
+                else:
+                    pair = jnp.where(low, swap_halves(first), second)
+                packed[q ^ me_at, packed_rows, :] = pair
+
+        waiting = [one_part(n) for n in range(2 * steps)]
+        active = [waiting.pop(0)]
+        next(active[0])
+        while active:
+            if len(active) < 2 and waiting:
+                active.append(waiting.pop(0))
+            for one in active[::-1]:
                 if next(one, "done") == "done":
-                    sides.remove(one)
-
-        for q in range(groups):
-            at = slice((q // 2) * LANES, (q // 2 + 1) * LANES)
-            first, second = back_to[0][:, at], back_to[1][:, at]
-            if q % 2 == 0:
-                pair = jnp.where(low, first, swap_halves(second))
-            else:
-                pair = jnp.where(low, swap_halves(first), second)
-            packed[q ^ me_at] = pair
+                    active.remove(one)
         for k in range(groups):
             grad_refs[k][...] = packed[k].astype(jnp.bfloat16)
 
-        @pl.when(step == steps - 1)
-        def _():
-            for n, total in enumerate((sum_one, sum_two)):
-                for k in range(tall // width):
-                    flat[n * tall + k * width : n * tall + (k + 1) * width, :] = total[
-                        :, k * width : (k + 1) * width
-                    ].astype(jnp.bfloat16)
-            gains = [jnp.sum(sum_gains[n], axis=0, keepdims=True) for n in range(2)]
-            flat[2 * tall : 2 * tall + 16, :] = jnp.concatenate(
-                gains + [jnp.zeros((14, width), jnp.float32)], axis=0
-            ).astype(jnp.bfloat16)
-            if 2 * groups * chunk > 2 * tall + 16:
-                flat[2 * tall + 16 :, :] = jnp.zeros(
-                    (2 * groups * chunk - 2 * tall - 16, width), jnp.bfloat16
-                )
-            for k in range(groups):
-                for part_ref, side in ((kept_ref, core), (given_ref, 1 - core)):
-                    begin = pl.multiple_of((side * groups + (me_at ^ k)) * chunk, 16)
-                    part_ref[k] = flat[pl.ds(begin, chunk), :]
+        for n, total in enumerate((sum_one, sum_two)):
+            for k in range(tall // width):
+                flat[n * tall + k * width : n * tall + (k + 1) * width, :] = total[
+                    :, k * width : (k + 1) * width
+                ].astype(jnp.bfloat16)
+        gains = [jnp.sum(sum_gains[n], axis=0, keepdims=True) for n in range(2)]
+        flat[2 * tall : 2 * tall + 16, :] = jnp.concatenate(
+            gains + [jnp.zeros((14, width), jnp.float32)], axis=0
+        ).astype(jnp.bfloat16)
+        if 2 * groups * chunk > 2 * tall + 16:
+            flat[2 * tall + 16 :, :] = jnp.zeros(
+                (2 * groups * chunk - 2 * tall - 16, width), jnp.bfloat16
+            )
+        for k in range(groups):
+            for part_ref, side in ((kept_ref, core), (given_ref, 1 - core)):
+                begin = pl.multiple_of((side * groups + (me_at ^ k)) * chunk, 16)
+                part_ref[k] = flat[pl.ds(begin, chunk), :]
 
     def whole(shape):
         return pl.BlockSpec(shape, lambda j, m: (0, 0))
-
-    def by_step(rows, columns):
-        return pl.BlockSpec((rows, columns), lambda j, m: (j, 0))
 
     return pl.pallas_call(
         kernel,
         grid_spec=pltpu.PrefetchScalarGridSpec(
             num_scalar_prefetch=1,
-            grid=(steps,),
-            in_specs=[by_step(run, LANES)] * groups
+            grid=(1,),
+            in_specs=[whole((items // 2, LANES))] * groups
             + [whole((tall, width)), whole((1, width))] * 2
-            + [by_step(2 * run, width)],
-            out_specs=[by_step(2 * run, width)]
-            + [by_step(run, LANES)] * groups
+            + [whole((items, width))],
+            out_specs=[whole((items, width))]
+            + [whole((items // 2, LANES))] * groups
             + [pl.BlockSpec((groups, chunk, width), lambda j, m: (0, 0, 0))] * 2,
             scratch_shapes=[
-                pltpu.VMEM((groups, run, LANES), jnp.float32),
-                pltpu.VMEM((groups, run, LANES), jnp.float32),
+                pltpu.VMEM((groups, items // 2, LANES), jnp.float32),
+                pltpu.VMEM((groups, items // 2, LANES), jnp.float32),
                 pltpu.VMEM((width, tall), jnp.float32),
                 pltpu.VMEM((width, tall), jnp.float32),
                 pltpu.VMEM((2, 8, width), jnp.float32),
@@ -670,7 +670,6 @@
     mine = jnp.transpose(mine, (3, 0, 1, 2)).reshape(tables, 2, items // 2)
 
     first, last, own = own_columns(at, table)
-    mine = after(mine, own)
     all_codes = mine
     for k in range((groups - 1).bit_length()):
         all_codes = jnp.concatenate([all_codes, dp_flip(all_codes, 2**k)], axis=2)
@@ -727,22 +726,24 @@
         return jnp.concatenate([value.astype(jnp.bfloat16) for value in values], axis=0)
 
     ((near_2, far_2),) = add_rows(codes[2:], blocks, shards, half, 4)
-    far_2, *chunks[:-1] = together(far_2, *chunks[:-1])
-    chunk = add_up(chunks).astype(jnp.bfloat16)
+    far_2, *chunks = together(far_2, *chunks)
+    chunk = add_up(chunks)
+    chunk = packed(*(chunk[:, n : n + LANES] for n in range(0, width, LANES)))
     got_2 = across(far_2)
-    going = [packed(side(near_2, got_2, 2)), packed(side(near_2, got_2, 3)), chunk]
-    came = [up(going[0]), down(going[1]), *(table_shift(chunk, k) for k in (shards // 2, 2, -2))]
+    going = [packed(side(near_2, got_2, 2), chunk), packed(side(near_2, got_2, 3), chunk)]
+    came = [up(going[0]), down(going[1])]
     blocks = [after(block, *going) for block in blocks]
     (near_0, far_0), (near_1, far_1) = add_rows(codes[:2], blocks, shards, half, 2)
-    far_0, up_2, down_2, *chunks = together(far_0, *came)
+    far_0, far_1, up_2, down_2 = together(far_0, far_1, *came)
+    opposite = up(up_2[half:])
     got_0 = across(far_0)
-    got_1 = across(after(far_1, got_0))
-    chunk = (add_up([chunk, chunks[0]]) + add_up(chunks[1:])).astype(jnp.bfloat16)
+    got_1 = across(far_1)
+    chunk = (add_up([chunk, opposite]) + add_up([up_2[half:], down_2[half:]])).astype(jnp.bfloat16)
     going = packed(
-        side(near_2, got_2, 1) + up_2.astype(jnp.float32), side(near_0, got_0, 2), side(near_1, got_1, 2)
+        side(near_2, got_2, 1) + up_2[:half].astype(jnp.float32), side(near_0, got_0, 2), side(near_1, got_1, 2)
     )
     up_01, down_01, *chunks = together(
-        up(going),
+        up(after(going, chunk)),
         down(packed(side(near_0, got_0, 3), side(near_1, got_1, 3))),
         *(dp_flip(chunk, k) for k in range(1, groups)),
     )
@@ -752,7 +753,7 @@
         side(near_1, got_1, 1) + up_01[2 * half :].astype(jnp.float32),
     )
     last_01, far = up(going), across(near)
-    sums = scaled_sums(at, near, far, weight_one.shape[0], 1.0 / math.sqrt(items * groups * shards))
+    sums = scaled_sums(at, near, far, weight_one.shape[0], width, 1.0 / math.sqrt(items * groups * shards))
 
     near_2 = after(near_2, *sums)
     grads = finished([(near_2, got_2, down_2, 0, up_01, 0)], 2, tables, None)

time: 199 us -> 196 us (0.985)
  starting transfers between devices: 40.5 us -> 35.8 us
    ppermute x14 -> x12, waiting for transfers between devices: 59.2 us -> 66.7 us  [table_shift(): lax.ppermute(values, 'table', [(i, (i + k) % shards) for i in range(shard...]
    ppermute x14 -> x12, starting transfers between devices: 22.5 us -> 17.1 us  [table_shift(): lax.ppermute(values, 'table', [(i, (i + k) % shards) for i in range(shard...]
    ppermute x12, waiting for transfers between devices: 9.64 us -> 5.87 us  [across(): return lax.ppermute(values, 'table', [(i, i ^ 1) for i in range(shards)])]
  transfers between devices with their start and end apart: 40 -> 38, of which waited for: 21 -> 21; matrix products, arithmetic and copies ran while one was open for 1% -> 1% of each run, Pallas kernels for 21% -> 21%
where the time goes in v5:
time: 196 us; the launch traced here: 195 us
  waiting for transfers between devices  94.2 us (48%)
  Pallas kernels  60.1 us (31%)
  starting transfers between devices  35.8 us (18%)
  local copies, waits for them, and re-layouts  2.71 us (1%)
    ppermute x12, waiting for transfers between devices, table_shift(): lax.ppermute(values, 'table', [(i, (i + k) % shards) for i in range(shard...  66.7 us
    pallas_call x2, Pallas kernels, add_rows(): pl.pallas_call(kernel, grid_spec=pltpu.PrefetchScalarGridSpec(num_scalar_...  25.3 us
    ppermute x14, waiting for transfers between devices, dp_flip(): return lax.ppermute(values, 'dp', [(i, i ^ k) for i in range(groups)])  21.7 us
    pallas_call x3, Pallas kernels, look_up(): pl.pallas_call(kernel, grid_spec=pltpu.PrefetchScalarGridSpec(num_scalar_...  19.3 us
    ppermute x14, starting transfers between devices, dp_flip(): return lax.ppermute(values, 'dp', [(i, i ^ k) for i in range(groups)])  17.3 us
    ppermute x12, starting transfers between devices, table_shift(): lax.ppermute(values, 'table', [(i, (i + k) % shards) for i in range(shard...  17.1 us
    pallas_call x1, Pallas kernels, both_layers(): pl.pallas_call(kernel, grid_spec=pltpu.PrefetchScalarGridSpec(num_scalar_...  10 us
    ppermute x12, waiting for transfers between devices, across(): return lax.ppermute(values, 'table', [(i, i ^ 1) for i in range(shards)])  5.87 us
  transfers between devices with their start and end apart: 38, of which 21 were waited for; matrix products, arithmetic and copies ran while one was open for 1% of the time, Pallas kernels for 21%

profile of v5, /device:TPU:0, one launch (start us, length us, event | category | flops | bytes accessed | tf_op | source)
XLA Modules:
  0.0 195.4 jit_solution(3323389443046802136)
XLA Ops:
  0.7 1.9 copy-done
  4.0 3.1 %collective-permute-start.5 = (bf16[2,1024,128]{2,1,0:T(8,128)(2,1)S(1)}, bf16[2,1024,128]{2,1,0:T(8,128)(2,1)S(1)}, u32[]{:S(2)}, u32[]{:S(2)}) collective-permute-start(bf16[2,1024,128]{2,1,0:T(8,128)(2,1)S(1)} %get-tuple-element.61), channel_id=1, source_target_pairs={{0,2},{1,3},{2,4},{3,5},{4,6},{5,7},{6,0},{7,1},{8,10},{9,11},{10,... | collective-permute-start | bytes 1572872 | tf_op jit(solution)/shard_map/ppermute | solution.py:653
  9.0 2.2 %collective-permute-start.3 = (bf16[2,1024,128]{2,1,0:T(8,128)(2,1)S(1)}, bf16[2,1024,128]{2,1,0:T(8,128)(2,1)S(1)}, u32[]{:S(2)}, u32[]{:S(2)}) collective-permute-start(bf16[2,1024,128]{2,1,0:T(8,128)(2,1)S(1)} %get-tuple-element.61), channel_id=1, source_target_pairs={{0,6},{1,7},{2,0},{3,1},{4,2},{5,3},{6,4},{7,5},{8,14},{9,15},{10,... | collective-permute-start | bytes 1572872 | tf_op jit(solution)/shard_map/ppermute | solution.py:653
  11.4 1.6 collective-permute-start.1
  13.0 2.5 %collective-permute-done.1 = s32[3,2,1600]{2,1,0:T(2,128)S(1)} collective-permute-done((s32[3,2,1600]{2,1,0:T(2,128)S(1)}, s32[3,2,1600]{2,1,0:T(2,128)S(1)}, u32[]{:S(2)}, u32[]{:S(2)}) %collective-permute-start.1) | collective-permute-done | bytes 38432 | tf_op jit(solution)/shard_map/ppermute | solution.py:650
  15.8 6.1 %collective-permute-done.5.refs_3_ = bf16[2,1024,128]{2,1,0:T(8,128)(2,1)S(1)} collective-permute-done((bf16[2,1024,128]{2,1,0:T(8,128)(2,1)S(1)}, bf16[2,1024,128]{2,1,0:T(8,128)(2,1)S(1)}, u32[]{:S(2)}, u32[]{:S(2)}) %collective-permute-start.5) | collective-permute-done | bytes 524320 | tf_op jit(solution)/shard_map/ppermute | solution.py:653
  21.9 11.1 %collective-permute-done.3.refs_1_ = bf16[2,1024,128]{2,1,0:T(8,128)(2,1)S(1)} collective-permute-done((bf16[2,1024,128]{2,1,0:T(8,128)(2,1)S(1)}, bf16[2,1024,128]{2,1,0:T(8,128)(2,1)S(1)}, u32[]{:S(2)}, u32[]{:S(2)}) %collective-permute-start.3) | collective-permute-done | bytes 524320 | tf_op jit(solution)/shard_map/ppermute | solution.py:653
  33.0 10.5 %collective-permute-done.9.refs_2_ = bf16[2,1024,128]{2,1,0:T(8,128)(2,1)S(1)} collective-permute-done((bf16[2,1024,128]{2,1,0:T(8,128)(2,1)S(1)}, bf16[2,1024,128]{2,1,0:T(8,128)(2,1)S(1)}, u32[]{:S(2)}, u32[]{:S(2)}) %collective-permute-start.9) | collective-permute-done | bytes 524320 | tf_op jit(solution)/shard_map/ppermute | solution.py:653
  43.8 3.9 %collective-permute-start.7 = (bf16[1,1024,128]{2,1,0:T(8,128)(2,1)S(1)}, bf16[1,1024,128]{2,1,0:T(8,128)(2,1)S(1)}, u32[]{:S(2)}, u32[]{:S(2)}) collective-permute-start(bf16[1,1024,128]{2,1,0:T(8,128)(2,1)S(1)} %get-tuple-element.62), channel_id=1, source_target_pairs={{0,6},{1,7},{2,0},{3,1},{4,2},{5,3},{6,4},{7,5},{8,14},{9,15},{10,... | collective-permute-start | bytes 786440 | tf_op jit(solution)/shard_map/ppermute | solution.py:653
  47.7 6.3 %look_up.3.refs_8_ = f32[3200,128]{1,0:T(8,128)S(1)} custom-call(s32[3200]{0:T(1024)S(1)} %get-tuple-element.113.low_ref.refs_0_, s32[3200]{0:T(1024)S(1)} %get-tuple-element.112.high_ref.refs_1_, bf16[3,1024,128]{2,1,0:T(8,128)(2,1)S(1)} %get-tuple-element.60.refs_0_, bf16[2,1024,128]{2,1,0:T(8,128)(2,1)S(1)} %collective-permute-done.3.refs_1_, ...), custom_call_target="tpu_custom_call" | custom-call | bytes 39321600 | tf_op jit(solution)/shard_map/look_up/pallas_call | solution.py:267
  54.5 6.4 %look_up.4.refs_8_ = f32[3200,128]{1,0:T(8,128)S(1)} custom-call(s32[3200]{0:T(1024)S(1)} %get-tuple-element.111.low_ref.refs_2_, s32[3200]{0:T(1024)S(1)} %get-tuple-element.110.high_ref.refs_3_, bf16[3,1024,128]{2,1,0:T(8,128)(2,1)S(1)} %get-tuple-element.60.refs_0_, bf16[2,1024,128]{2,1,0:T(8,128)(2,1)S(1)} %collective-permute-done.3.refs_1_, ...), custom_call_target="tpu_custom_call" | custom-call | bytes 39321600 | tf_op jit(solution)/shard_map/look_up/pallas_call | solution.py:267
  61.5 3.9 %collective-permute-done.11.refs_2_ = bf16[1,1024,128]{2,1,0:T(8,128)(2,1)S(1)} collective-permute-done((bf16[1,1024,128]{2,1,0:T(8,128)(2,1)S(1)}, bf16[1,1024,128]{2,1,0:T(8,128)(2,1)S(1)}, u32[]{:S(2)}, u32[]{:S(2)}) %collective-permute-start.11) | collective-permute-done | bytes 262176 | tf_op jit(solution)/shard_map/ppermute | solution.py:653
  66.9 6.5 %look_up.5 = bf16[3200,128]{1,0:T(8,128)(2,1)S(1)} custom-call(s32[3200]{0:T(1024)S(1)} %get-tuple-element.115.low_ref.refs_0_, s32[3200]{0:T(1024)S(1)} %get-tuple-element.114.high_ref.refs_1_, bf16[3,1024,128]{2,1,0:T(8,128)(2,1)S(1)} %get-tuple-element.60.refs_0_, bf16[1,1024,128]{2,1,0:T(8,128)(2,1)S(1)} %collective-permute-done.7.refs_1_, ...), custom_call_target="tpu_custom_call" | custom-call | bytes 39321600 | tf_op jit(solution)/shard_map/look_up/pallas_call | solution.py:267
  73.6 1.6 collective-permute-start.15
  77.1 4.4 %collective-permute-done.15.refs_1_ = bf16[800,128]{1,0:T(8,128)(2,1)S(1)} collective-permute-done((bf16[800,128]{1,0:T(8,128)(2,1)S(1)}, bf16[800,128]{1,0:T(8,128)(2,1)S(1)}, u32[]{:S(2)}, u32[]{:S(2)}) %collective-permute-start.15) | collective-permute-done | bytes 204832 | tf_op jit(solution)/shard_map/ppermute | solution.py:650
  81.6 4.8 %collective-permute-done.16.refs_2_ = bf16[800,128]{1,0:T(8,128)(2,1)S(1)} collective-permute-done((bf16[800,128]{1,0:T(8,128)(2,1)S(1)}, bf16[800,128]{1,0:T(8,128)(2,1)S(1)}, u32[]{:S(2)}, u32[]{:S(2)}) %collective-permute-start.16) | collective-permute-done | bytes 204832 | tf_op jit(solution)/shard_map/ppermute | solution.py:650
  86.4 10.0 %both_layers.1 = (bf16[1600,256]{1,0:T(8,128)(2,1)}, bf16[800,128]{1,0:T(8,128)(2,1)S(1)}, bf16[800,128]{1,0:T(8,128)(2,1)S(1)}, bf16[800,128]{1,0:T(8,128)(2,1)...) custom-call(s32[2]{0:T(128)S(1)} %pad_add_fusion.1.at_ref.me_ref, ...), custom_call_target="tpu_custom_call" | custom-call | tf_op jit(solution)/shard_map/both_layers/pallas_call | solution.py:590
  102.2 3.1 %collective-permute-done.21.refs_5_.refs_7_ = bf16[800,128]{1,0:T(8,128)(2,1)S(1)} collective-permute-done((bf16[800,128]{1,0:T(8,128)(2,1)S(1)}, bf16[800,128]{1,0:T(8,128)(2,1)S(1)}, u32[]{:S(2)}, u32[]{:S(2)}) %collective-permute-start.21) | collective-permute-done | bytes 204832 | tf_op jit(solution)/shard_map/ppermute | solution.py:650
  106.7 2.5 %collective-permute-done.20.refs_4_.refs_6_ = bf16[800,128]{1,0:T(8,128)(2,1)S(1)} collective-permute-done((bf16[800,128]{1,0:T(8,128)(2,1)S(1)}, bf16[800,128]{1,0:T(8,128)(2,1)S(1)}, u32[]{:S(2)}, u32[]{:S(2)}) %collective-permute-start.20) | collective-permute-done | bytes 204832 | tf_op jit(solution)/shard_map/ppermute | solution.py:650
  109.7 9.8 %add_rows.2 = (bf16[4,1024,128]{2,1,0:T(8,128)(2,1)S(1)}, bf16[4,1024,128]{2,1,0:T(8,128)(2,1)S(1)}) custom-call(s32[3200]{0:T(1024)S(1)} %get-tuple-element.115.low_ref.refs_0_, s32[3200]{0:T(1024)S(1)} %get-tuple-element.114.high_ref.refs_1_, bf16[800,128]{1,0:T(8,128)(2,1)S(1)} %get-tuple-element.85.refs_2_.refs_4_, ...), custom_call_target="tpu_custom_call" | custom-call | bytes 41943040 | tf_op jit(solution)/shard_map/add_rows/pallas_call | solution.py:331
  119.7 2.6 %collective-permute-done.25.refs_1_ = bf16[4,1024,128]{2,1,0:T(8,128)(2,1)S(1)} collective-permute-done((bf16[4,1024,128]{2,1,0:T(8,128)(2,1)S(1)}, bf16[4,1024,128]{2,1,0:T(8,128)(2,1)S(1)}, u32[]{:S(2)}, u32[]{:S(2)}) %collective-permute-start.25) | collective-permute-done | bytes 1048608 | tf_op jit(solution)/shard_map/ppermute | solution.py:662
  122.5 3.8 %collective-permute-start.27 = (bf16[1440,128]{1,0:T(8,128)(2,1)S(1)}, bf16[1440,128]{1,0:T(8,128)(2,1)S(1)}, u32[]{:S(2)}, u32[]{:S(2)}) collective-permute-start(bf16[1440,128]{1,0:T(8,128)(2,1)S(1)} %get-tuple-element.134), channel_id=1, source_target_pairs={{0,6},{1,7},{2,0},{3,1},{4,2},{5,3},{6,4},{7,5},{8,14},{9,15},{10,... | collective-permute-start | bytes 1105928 | tf_op jit(solution)/shard_map/ppermute | solution.py:653
  126.3 15.5 %add_rows.3 = (bf16[4,1024,128]{2,1,0:T(8,128)(2,1)S(1)}, bf16[4,1024,128]{2,1,0:T(8,128)(2,1)S(1)}, bf16[4,1024,128]{2,1,0:T(8,128)(2,1)S(1)}, bf16[4,1024,128]{2,1,0:T(8,128)(2,1)S(1)}) custom-call(s32[3200]{0:T(1024)S(1)} %get-tuple-element.113.low_ref.refs_0_, s32[3200]{0:T(1024)S(1)} %get-tuple-element.112.high_ref.refs_1_, ...), custom_call_target="tpu_custom_call" | custom-call | bytes 83886080 | tf_op jit(solution)/shard_map/add_rows/pallas_call | solution.py:331
  142.6 6.6 %collective-permute-done.28 = bf16[416,128]{1,0:T(8,128)(2,1)S(1)} collective-permute-done((bf16[416,128]{1,0:T(8,128)(2,1)S(1)}, bf16[416,128]{1,0:T(8,128)(2,1)S(1)}, u32[]{:S(2)}, u32[]{:S(2)}) %collective-permute-start.28) | collective-permute-done | bytes 106528 | tf_op jit(solution)/shard_map/ppermute | solution.py:653
  149.8 3.9 %collective-permute-start.32 = (bf16[2048,128]{1,0:T(8,128)(2,1)S(1)}, bf16[2048,128]{1,0:T(8,128)(2,1)S(1)}, u32[]{:S(2)}, u32[]{:S(2)}) collective-permute-start(bf16[2048,128]{1,0:T(8,128)(2,1)S(1)} %pad_maximum_fusion.1), channel_id=1, source_target_pairs={{0,6},{1,7},{2,0},{3,1},{4,2},{5,3},{6,4},{7,5},{8,14},{9,15},{10,... | collective-permute-start | bytes 1572872 | tf_op jit(solution)/shard_map/ppermute | solution.py:653
  155.4 1.8 collective-permute-start.35
  157.2 1.8 collective-permute-done.33
  159.4 1.6 collective-permute-done.35
  161.0 18.8 %collective-permute-done.32.refs_2_.refs_6_ = bf16[2048,128]{1,0:T(8,128)(2,1)S(1)} collective-permute-done((bf16[2048,128]{1,0:T(8,128)(2,1)S(1)}, bf16[2048,128]{1,0:T(8,128)(2,1)S(1)}, u32[]{:S(2)}, u32[]{:S(2)}) %collective-permute-start.32) | collective-permute-done | bytes 524320 | tf_op jit(solution)/shard_map/ppermute | solution.py:653
  180.3 1.8 collective-permute-done.36.far_ref
  182.0 1.9 scaled_sums.1
  184.9 9.2 %collective-permute-done.37.refs_3_.refs_7_ = bf16[2048,128]{1,0:T(8,128)(2,1)S(1)} collective-permute-done((bf16[2048,128]{1,0:T(8,128)(2,1)S(1)}, bf16[2048,128]{1,0:T(8,128)(2,1)S(1)}, u32[]{:S(2)}, u32[]{:S(2)}) %collective-permute-start.37) | collective-permute-done | bytes 524320 | tf_op jit(solution)/shard_map/ppermute | solution.py:653
  (99 shorter events, 23.0 us)
Async XLA Ops:
  4.0 17.9 %collective-permute-start.5 = (bf16[2,1024,128]{2,1,0:T(8,128)(2,1)S(1)}, bf16[2,1024,128]{2,1,0:T(8,128)(2,1)S(1)}, u32[]{:S(2)}, u32[]{:S(2)}) collective-permute-start(bf16[2,1024,128]{2,1,0:T(8,128)(2,1)S(1)} %get-tuple-element.61), channel_id=1, source_target_pairs={{0,2},{1,3},{2,4},{3,5},{4,6},{5,7},{6,0},{7,1},{8,10},{9,11},{10,... | collective-permute-start | bytes 1572872 | tf_op jit(solution)/shard_map/ppermute | solution.py:653
  9.0 24.0 %collective-permute-start.3 = (bf16[2,1024,128]{2,1,0:T(8,128)(2,1)S(1)}, bf16[2,1024,128]{2,1,0:T(8,128)(2,1)S(1)}, u32[]{:S(2)}, u32[]{:S(2)}) collective-permute-start(bf16[2,1024,128]{2,1,0:T(8,128)(2,1)S(1)} %get-tuple-element.61), channel_id=1, source_target_pairs={{0,6},{1,7},{2,0},{3,1},{4,2},{5,3},{6,4},{7,5},{8,14},{9,15},{10,... | collective-permute-start | bytes 1572872 | tf_op jit(solution)/shard_map/ppermute | solution.py:653
  15.7 27.8 %collective-permute-start.2 = (bf16[3,1024,128]{2,1,0:T(8,128)(2,1)S(1)}, bf16[3,1024,128]{2,1,0:T(8,128)(2,1)S(1)}, u32[]{:S(2)}, u32[]{:S(2)}) collective-permute-start(bf16[3,1024,128]{2,1,0:T(8,128)(2,1)S(1)} %get-tuple-element.60.refs_0_), channel_id=1, source_target_pairs={{0,1},{1,0},{2,3},{3,2},{4,5},{5,4},{6,7},{7,6},{8,9},{9,8},{10,11... | collective-permute-start | bytes 2359304 | tf_op jit(solution)/shard_map/ppermute | solution.py:662
  21.9 21.6 %collective-permute-start.9 = (bf16[2,1024,128]{2,1,0:T(8,128)(2,1)S(1)}, bf16[2,1024,128]{2,1,0:T(8,128)(2,1)S(1)}, u32[]{:S(2)}, u32[]{:S(2)}) collective-permute-start(bf16[2,1024,128]{2,1,0:T(8,128)(2,1)S(1)} %collective-permute-done.5.refs_3_), channel_id=1, source_target_pairs={{0,2},{1,3},{2,4},{3,5},{4,6},{5,7},{6,0},{7,1},{8,10},{9,11},{10,... | collective-permute-start | bytes 1572872 | tf_op jit(solution)/shard_map/ppermute | solution.py:653
  21.9 21.6 %collective-permute-start.6 = (bf16[2,1024,128]{2,1,0:T(8,128)(2,1)S(1)}, bf16[2,1024,128]{2,1,0:T(8,128)(2,1)S(1)}, u32[]{:S(2)}, u32[]{:S(2)}) collective-permute-start(bf16[2,1024,128]{2,1,0:T(8,128)(2,1)S(1)} %collective-permute-done.5.refs_3_), channel_id=1, source_target_pairs={{0,1},{1,0},{2,3},{3,2},{4,5},{5,4},{6,7},{7,6},{8,9},{9,8},{10,11... | collective-permute-start | bytes 1572872 | tf_op jit(solution)/shard_map/ppermute | solution.py:662
  33.0 10.5 %collective-permute-start.4 = (bf16[2,1024,128]{2,1,0:T(8,128)(2,1)S(1)}, bf16[2,1024,128]{2,1,0:T(8,128)(2,1)S(1)}, u32[]{:S(2)}, u32[]{:S(2)}) collective-permute-start(bf16[2,1024,128]{2,1,0:T(8,128)(2,1)S(1)} %collective-permute-done.3.refs_1_), channel_id=1, source_target_pairs={{0,1},{1,0},{2,3},{3,2},{4,5},{5,4},{6,7},{7,6},{8,9},{9,8},{10,11... | collective-permute-start | bytes 1572872 | tf_op jit(solution)/shard_map/ppermute | solution.py:662
  43.5 4.1 %collective-permute-start.10 = (bf16[2,1024,128]{2,1,0:T(8,128)(2,1)S(1)}, bf16[2,1024,128]{2,1,0:T(8,128)(2,1)S(1)}, u32[]{:S(2)}, u32[]{:S(2)}) collective-permute-start(bf16[2,1024,128]{2,1,0:T(8,128)(2,1)S(1)} %collective-permute-done.9.refs_2_), channel_id=1, source_target_pairs={{0,1},{1,0},{2,3},{3,2},{4,5},{5,4},{6,7},{7,6},{8,9},{9,8},{10,11... | collective-permute-start | bytes 1572872 | tf_op jit(solution)/shard_map/ppermute | solution.py:662
  43.5 11.0 %collective-permute-start.8 = (bf16[1,1024,128]{2,1,0:T(8,128)(2,1)S(1)}, bf16[1,1024,128]{2,1,0:T(8,128)(2,1)S(1)}, u32[]{:S(2)}, u32[]{:S(2)}) collective-permute-start(bf16[1,1024,128]{2,1,0:T(8,128)(2,1)S(1)} %get-tuple-element.62), channel_id=1, source_target_pairs={{0,2},{1,3},{2,4},{3,5},{4,6},{5,7},{6,0},{7,1},{8,10},{9,11},{10,... | collective-permute-start | bytes 786440 | tf_op jit(solution)/shard_map/ppermute | solution.py:653
  43.8 17.2 %collective-permute-start.7 = (bf16[1,1024,128]{2,1,0:T(8,128)(2,1)S(1)}, bf16[1,1024,128]{2,1,0:T(8,128)(2,1)S(1)}, u32[]{:S(2)}, u32[]{:S(2)}) collective-permute-start(bf16[1,1024,128]{2,1,0:T(8,128)(2,1)S(1)} %get-tuple-element.62), channel_id=1, source_target_pairs={{0,6},{1,7},{2,0},{3,1},{4,2},{5,3},{6,4},{7,5},{8,14},{9,15},{10,... | collective-permute-start | bytes 786440 | tf_op jit(solution)/shard_map/ppermute | solution.py:653
  54.5 10.8 %collective-permute-start.11 = (bf16[1,1024,128]{2,1,0:T(8,128)(2,1)S(1)}, bf16[1,1024,128]{2,1,0:T(8,128)(2,1)S(1)}, u32[]{:S(2)}, u32[]{:S(2)}) collective-permute-start(bf16[1,1024,128]{2,1,0:T(8,128)(2,1)S(1)} %collective-permute-done.8.refs_3_), channel_id=1, source_target_pairs={{0,2},{1,3},{2,4},{3,5},{4,6},{5,7},{6,0},{7,1},{8,10},{9,11},{10,... | collective-permute-start | bytes 786440 | tf_op jit(solution)/shard_map/ppermute | solution.py:653
  60.9 4.5 %collective-permute-start.14 = (bf16[1,1024,128]{2,1,0:T(8,128)(2,1)S(1)}, bf16[1,1024,128]{2,1,0:T(8,128)(2,1)S(1)}, u32[]{:S(2)}, u32[]{:S(2)}) collective-permute-start(bf16[1,1024,128]{2,1,0:T(8,128)(2,1)S(1)} %collective-permute-done.8.refs_3_), channel_id=1, source_target_pairs={{0,1},{1,0},{2,3},{3,2},{4,5},{5,4},{6,7},{7,6},{8,9},{9,8},{10,11... | collective-permute-start | bytes 786440 | tf_op jit(solution)/shard_map/ppermute | solution.py:662
  61.0 4.4 %collective-permute-start.12 = (bf16[1,1024,128]{2,1,0:T(8,128)(2,1)S(1)}, bf16[1,1024,128]{2,1,0:T(8,128)(2,1)S(1)}, u32[]{:S(2)}, u32[]{:S(2)}) collective-permute-start(bf16[1,1024,128]{2,1,0:T(8,128)(2,1)S(1)} %collective-permute-done.7.refs_1_), channel_id=1, source_target_pairs={{0,1},{1,0},{2,3},{3,2},{4,5},{5,4},{6,7},{7,6},{8,9},{9,8},{10,11... | collective-permute-start | bytes 786440 | tf_op jit(solution)/shard_map/ppermute | solution.py:662
  73.6 8.0 %collective-permute-start.15 = (bf16[800,128]{1,0:T(8,128)(2,1)S(1)}, bf16[800,128]{1,0:T(8,128)(2,1)S(1)}, u32[]{:S(2)}, u32[]{:S(2)}) collective-permute-start(bf16[800,128]{1,0:T(8,128)(2,1)S(1)} %get-tuple-element.130), channel_id=1, source_target_pairs={{0,8},{8,0},{16,24},{24,16},{1,9},{9,1},{17,25},{25,17},{2,10},{10... | collective-permute-start | bytes 614408 | tf_op jit(solution)/shard_map/ppermute | solution.py:650
  75.2 11.2 %collective-permute-start.16 = (bf16[800,128]{1,0:T(8,128)(2,1)S(1)}, bf16[800,128]{1,0:T(8,128)(2,1)S(1)}, u32[]{:S(2)}, u32[]{:S(2)}) collective-permute-start(bf16[800,128]{1,0:T(8,128)(2,1)S(1)} %get-tuple-element.129), channel_id=1, source_target_pairs={{0,16},{8,24},{16,0},{24,8},{1,17},{9,25},{17,1},{25,9},{2,18},{10... | collective-permute-start | bytes 614408 | tf_op jit(solution)/shard_map/ppermute | solution.py:650
  76.7 9.7 %collective-permute-start.17 = (bf16[800,128]{1,0:T(8,128)(2,1)S(1)}, bf16[800,128]{1,0:T(8,128)(2,1)S(1)}, u32[]{:S(2)}, u32[]{:S(2)}) collective-permute-start(bf16[800,128]{1,0:T(8,128)(2,1)S(1)} %get-tuple-element.128), channel_id=1, source_target_pairs={{0,24},{8,16},{16,8},{24,0},{1,25},{9,17},{17,9},{25,1},{2,26},{10... | collective-permute-start | bytes 614408 | tf_op jit(solution)/shard_map/ppermute | solution.py:650
  96.4 8.8 %collective-permute-start.21 = (bf16[800,128]{1,0:T(8,128)(2,1)S(1)}, bf16[800,128]{1,0:T(8,128)(2,1)S(1)}, u32[]{:S(2)}, u32[]{:S(2)}) collective-permute-start(bf16[800,128]{1,0:T(8,128)(2,1)S(1)} %get-tuple-element.76), channel_id=1, source_target_pairs={{0,24},{8,16},{16,8},{24,0},{1,25},{9,17},{17,9},{25,1},{2,26},{10... | collective-permute-start | bytes 614408 | tf_op jit(solution)/shard_map/ppermute | solution.py:650
  97.9 11.4 %collective-permute-start.20 = (bf16[800,128]{1,0:T(8,128)(2,1)S(1)}, bf16[800,128]{1,0:T(8,128)(2,1)S(1)}, u32[]{:S(2)}, u32[]{:S(2)}) collective-permute-start(bf16[800,128]{1,0:T(8,128)(2,1)S(1)} %get-tuple-element.74), channel_id=1, source_target_pairs={{0,16},{8,24},{16,0},{24,8},{1,17},{9,25},{17,1},{25,9},{2,18},{10... | collective-permute-start | bytes 614408 | tf_op jit(solution)/shard_map/ppermute | solution.py:650
  99.1 10.6 %collective-permute-start.19 = (bf16[800,128]{1,0:T(8,128)(2,1)S(1)}, bf16[800,128]{1,0:T(8,128)(2,1)S(1)}, u32[]{:S(2)}, u32[]{:S(2)}) collective-permute-start(bf16[800,128]{1,0:T(8,128)(2,1)S(1)} %get-tuple-element.72), channel_id=1, source_target_pairs={{0,8},{8,0},{16,24},{24,16},{1,9},{9,1},{17,25},{25,17},{2,10},{10... | collective-permute-start | bytes 614408 | tf_op jit(solution)/shard_map/ppermute | solution.py:650
  100.0 19.4 %collective-permute-start.22 = (bf16[208,256]{1,0:T(8,128)(2,1)S(1)}, bf16[208,256]{1,0:T(8,128)(2,1)S(1)}, u32[]{:S(2)}, u32[]{:S(2)}) collective-permute-start(bf16[208,256]{1,0:T(8,128)(2,1)S(1)} %get-tuple-element.126), channel_id=1, source_target_pairs={{0,8},{8,0},{16,24},{24,16},{1,9},{9,1},{17,25},{25,17},{2,10},{10... | collective-permute-start | bytes 319496 | tf_op jit(solution)/shard_map/ppermute | solution.py:650
  101.3 18.2 %collective-permute-start.23 = (bf16[208,256]{1,0:T(8,128)(2,1)S(1)}, bf16[208,256]{1,0:T(8,128)(2,1)S(1)}, u32[]{:S(2)}, u32[]{:S(2)}) collective-permute-start(bf16[208,256]{1,0:T(8,128)(2,1)S(1)} %get-tuple-element.125), channel_id=1, source_target_pairs={{0,16},{8,24},{16,0},{24,8},{1,17},{9,25},{17,1},{25,9},{2,18},{10... | collective-permute-start | bytes 319496 | tf_op jit(solution)/shard_map/ppermute | solution.py:650
  105.3 14.2 %collective-permute-start.24 = (bf16[208,256]{1,0:T(8,128)(2,1)S(1)}, bf16[208,256]{1,0:T(8,128)(2,1)S(1)}, u32[]{:S(2)}, u32[]{:S(2)}) collective-permute-start(bf16[208,256]{1,0:T(8,128)(2,1)S(1)} %get-tuple-element.124), channel_id=1, source_target_pairs={{0,24},{8,16},{16,8},{24,0},{1,25},{9,17},{17,9},{25,1},{2,26},{10... | collective-permute-start | bytes 319496 | tf_op jit(solution)/shard_map/ppermute | solution.py:650
  122.4 19.4 %collective-permute-start.26 = (bf16[1440,128]{1,0:T(8,128)(2,1)S(1)}, bf16[1440,128]{1,0:T(8,128)(2,1)S(1)}, u32[]{:S(2)}, u32[]{:S(2)}) collective-permute-start(bf16[1440,128]{1,0:T(8,128)(2,1)S(1)} %get-tuple-element.135), channel_id=1, source_target_pairs={{0,2},{1,3},{2,4},{3,5},{4,6},{5,7},{6,0},{7,1},{8,10},{9,11},{10,... | collective-permute-start | bytes 1105928 | tf_op jit(solution)/shard_map/ppermute | solution.py:653
  122.5 19.4 %collective-permute-start.27 = (bf16[1440,128]{1,0:T(8,128)(2,1)S(1)}, bf16[1440,128]{1,0:T(8,128)(2,1)S(1)}, u32[]{:S(2)}, u32[]{:S(2)}) collective-permute-start(bf16[1440,128]{1,0:T(8,128)(2,1)S(1)} %get-tuple-element.134), channel_id=1, source_target_pairs={{0,6},{1,7},{2,0},{3,1},{4,2},{5,3},{6,4},{7,5},{8,14},{9,15},{10,... | collective-permute-start | bytes 1105928 | tf_op jit(solution)/shard_map/ppermute | solution.py:653
  141.9 7.5 %collective-permute-start.29 = (bf16[4,1024,128]{2,1,0:T(8,128)(2,1)S(1)}, bf16[4,1024,128]{2,1,0:T(8,128)(2,1)S(1)}, u32[]{:S(2)}, u32[]{:S(2)}) collective-permute-start(bf16[4,1024,128]{2,1,0:T(8,128)(2,1)S(1)} %get-tuple-element.94), channel_id=1, source_target_pairs={{0,1},{1,0},{2,3},{3,2},{4,5},{5,4},{6,7},{7,6},{8,9},{9,8},{10,11... | collective-permute-start | bytes 3145736 | tf_op jit(solution)/shard_map/ppermute | solution.py:662
  141.9 7.5 %collective-permute-start.30 = (bf16[4,1024,128]{2,1,0:T(8,128)(2,1)S(1)}, bf16[4,1024,128]{2,1,0:T(8,128)(2,1)S(1)}, u32[]{:S(2)}, u32[]{:S(2)}) collective-permute-start(bf16[4,1024,128]{2,1,0:T(8,128)(2,1)S(1)} %get-tuple-element.96), channel_id=1, source_target_pairs={{0,1},{1,0},{2,3},{3,2},{4,5},{5,4},{6,7},{7,6},{8,9},{9,8},{10,11... | collective-permute-start | bytes 3145736 | tf_op jit(solution)/shard_map/ppermute | solution.py:662
  142.5 6.8 %collective-permute-start.28 = (bf16[416,128]{1,0:T(8,128)(2,1)S(1)}, bf16[416,128]{1,0:T(8,128)(2,1)S(1)}, u32[]{:S(2)}, u32[]{:S(2)}) collective-permute-start(bf16[416,128]{1,0:T(8,128)(2,1)S(1)} %slice.170), channel_id=1, source_target_pairs={{0,2},{1,3},{2,4},{3,5},{4,6},{5,7},{6,0},{7,1},{8,10},{9,11},{10,... | collective-permute-start | bytes 319496 | tf_op jit(solution)/shard_map/ppermute | solution.py:653
  149.7 30.1 %collective-permute-start.31 = (bf16[3072,128]{1,0:T(8,128)(2,1)S(1)}, bf16[3072,128]{1,0:T(8,128)(2,1)S(1)}, u32[]{:S(2)}, u32[]{:S(2)}) collective-permute-start(bf16[3072,128]{1,0:T(8,128)(2,1)S(1)} %pad_maximum_fusion), channel_id=1, source_target_pairs={{0,2},{1,3},{2,4},{3,5},{4,6},{5,7},{6,0},{7,1},{8,10},{9,11},{10,... | collective-permute-start | bytes 2359304 | tf_op jit(solution)/shard_map/ppermute | solution.py:653
  149.8 30.0 %collective-permute-start.32 = (bf16[2048,128]{1,0:T(8,128)(2,1)S(1)}, bf16[2048,128]{1,0:T(8,128)(2,1)S(1)}, u32[]{:S(2)}, u32[]{:S(2)}) collective-permute-start(bf16[2048,128]{1,0:T(8,128)(2,1)S(1)} %pad_maximum_fusion.1), channel_id=1, source_target_pairs={{0,6},{1,7},{2,0},{3,1},{4,2},{5,3},{6,4},{7,5},{8,14},{9,15},{10,... | collective-permute-start | bytes 1572872 | tf_op jit(solution)/shard_map/ppermute | solution.py:653
  153.7 5.3 %collective-permute-start.33 = (bf16[416,128]{1,0:T(8,128)(2,1)S(1)}, bf16[416,128]{1,0:T(8,128)(2,1)S(1)}, u32[]{:S(2)}, u32[]{:S(2)}) collective-permute-start(bf16[416,128]{1,0:T(8,128)(2,1)S(1)} %add_convert_fusion.6), channel_id=1, source_target_pairs={{0,8},{8,0},{16,24},{24,16},{1,9},{9,1},{17,25},{25,17},{2,10},{10... | collective-permute-start | bytes 319496 | tf_op jit(solution)/shard_map/ppermute | solution.py:650
  154.5 5.0 %collective-permute-start.34 = (bf16[416,128]{1,0:T(8,128)(2,1)S(1)}, bf16[416,128]{1,0:T(8,128)(2,1)S(1)}, u32[]{:S(2)}, u32[]{:S(2)}) collective-permute-start(bf16[416,128]{1,0:T(8,128)(2,1)S(1)} %add_convert_fusion.6), channel_id=1, source_target_pairs={{0,16},{8,24},{16,0},{24,8},{1,17},{9,25},{17,1},{25,9},{2,18},{10... | collective-permute-start | bytes 319496 | tf_op jit(solution)/shard_map/ppermute | solution.py:650
  155.4 5.6 %collective-permute-start.35 = (bf16[416,128]{1,0:T(8,128)(2,1)S(1)}, bf16[416,128]{1,0:T(8,128)(2,1)S(1)}, u32[]{:S(2)}, u32[]{:S(2)}) collective-permute-start(bf16[416,128]{1,0:T(8,128)(2,1)S(1)} %add_convert_fusion.6), channel_id=1, source_target_pairs={{0,24},{8,16},{16,8},{24,0},{1,25},{9,17},{17,9},{25,1},{2,26},{10... | collective-permute-start | bytes 319496 | tf_op jit(solution)/shard_map/ppermute | solution.py:650
  180.1 14.0 %collective-permute-start.37 = (bf16[2048,128]{1,0:T(8,128)(2,1)S(1)}, bf16[2048,128]{1,0:T(8,128)(2,1)S(1)}, u32[]{:S(2)}, u32[]{:S(2)}) collective-permute-start(bf16[2048,128]{1,0:T(8,128)(2,1)S(1)} %pad_maximum_fusion.2), channel_id=1, source_target_pairs={{0,2},{1,3},{2,4},{3,5},{4,6},{5,7},{6,0},{7,1},{8,10},{9,11},{10,... | collective-permute-start | bytes 1572872 | tf_op jit(solution)/shard_map/ppermute | solution.py:653
  (14 other events, 92.8 us)

commit v6 on v5

--- a/solution.py
+++ b/solution.py
@@ -13,7 +13,6 @@
 MIB = 2**20
 
 UNROLL = 16
-ROWS = 40
 
 
 def shifted(values, spacing):
@@ -175,7 +174,6 @@
         and sessions % 4 == 0
         and sessions <= 16
         and run % 16 == 0
-        and run % ROWS == 0
         and (groups * sessions * length // 2) % (4 * UNROLL) == 0
         and rows_dev % 32 == 0
         and 4 * shards * rows_dev * LANES * 4 <= 40 * MIB
@@ -457,10 +455,6 @@
             two = jnp.where(place < length - 2 * gap, pltpu.roll(values, run - 2 * gap, 0), 0.0)
             return [x.astype(jnp.bfloat16) for x in (values, one, two)]
 
-        def by_rows(work, *arrays):
-            parts = [work(*(a[r : r + ROWS] for a in arrays)) for r in range(0, run, ROWS)]
-            return [jnp.concatenate(values, axis=0) for values in zip(*parts)]
-
         def activate(before, gain):
             centred = before - jnp.mean(before, axis=-1, keepdims=True)
             inv_std = lax.rsqrt(jnp.mean(centred * centred, axis=-1, keepdims=True) + 1e-05)
@@ -521,7 +515,7 @@
                 normal, inv_std, output, slope = activate(before, gain_one_at)
                 return normal, inv_std, output.astype(jnp.bfloat16).astype(jnp.float32), slope
 
-            normal, inv_std, hidden, slope = by_rows(first, before)
+            normal, inv_std, hidden, slope = first(before)
             stacked = taps(hidden, 2)
             yield
             before = jnp.dot(stacked, w_two_ref[...], preferred_element_type=jnp.float32)
@@ -531,16 +525,13 @@
                 normal, inv_std, output, slope = activate(before, gain_two_at)
                 return values + output, unwind(grad, normal, inv_std, slope, gain_two_at, 1)
 
-            output, before = by_rows(second, before, embedded, top)
+            output, before = second(before, embedded, top)
             out_ref[rows, :] = output.astype(jnp.bfloat16)
             yield
             grad = products(before, hidden, turned_two, 2, sum_two)
             yield
 
-            def third(grad, normal, inv_std, slope):
-                return (unwind(grad, normal, inv_std, slope, gain_one_at, 0),)
-
-            (before,) = by_rows(third, grad, normal, inv_std, slope)
+            before = unwind(grad, normal, inv_std, slope, gain_one_at, 0)
             yield
             back_to[n] = top + products(before, embedded, turned_one, 1, sum_one)
             if side == 0:

time: 196 us -> 195 us (level)
  no operation moved by 1% of the time
where the time goes in v6:
time: 195 us
  waiting for transfers between devices  94.2 us (48%)
  Pallas kernels  59.6 us (31%)
  starting transfers between devices  35.8 us (18%)
  local copies, waits for them, and re-layouts  2.71 us (1%)
    ppermute x12, waiting for transfers between devices, table_shift(): lax.ppermute(values, 'table', [(i, (i + k) % shards) for i in range(shard...  66.7 us
    pallas_call x2, Pallas kernels, add_rows(): pl.pallas_call(kernel, grid_spec=pltpu.PrefetchScalarGridSpec(num_scalar_...  25.3 us
    ppermute x14, waiting for transfers between devices, dp_flip(): return lax.ppermute(values, 'dp', [(i, i ^ k) for i in range(groups)])  21.7 us
    pallas_call x3, Pallas kernels, look_up(): pl.pallas_call(kernel, grid_spec=pltpu.PrefetchScalarGridSpec(num_scalar_...  19.3 us
    ppermute x14, starting transfers between devices, dp_flip(): return lax.ppermute(values, 'dp', [(i, i ^ k) for i in range(groups)])  17.3 us
    ppermute x12, starting transfers between devices, table_shift(): lax.ppermute(values, 'table', [(i, (i + k) % shards) for i in range(shard...  17.1 us
    pallas_call x1, Pallas kernels, both_layers(): pl.pallas_call(kernel, grid_spec=pltpu.PrefetchScalarGridSpec(num_scalar_...  9.52 us
    ppermute x12, waiting for transfers between devices, across(): return lax.ppermute(values, 'table', [(i, i ^ 1) for i in range(shards)])  5.87 us
  transfers between devices with their start and end apart: 38, of which 21 were waited for; matrix products, arithmetic and copies ran while one was open for 1% of the time, Pallas kernels for 21%

profile of v6, /device:TPU:0, one launch (start us, length us, event | category | flops | bytes accessed | tf_op | source)
XLA Modules:
  0.0 194.9 jit_solution(15782287500801705505)
XLA Ops:
  0.7 1.9 copy-done
  4.0 3.1 %collective-permute-start.5 = (bf16[2,1024,128]{2,1,0:T(8,128)(2,1)S(1)}, bf16[2,1024,128]{2,1,0:T(8,128)(2,1)S(1)}, u32[]{:S(2)}, u32[]{:S(2)}) collective-permute-start(bf16[2,1024,128]{2,1,0:T(8,128)(2,1)S(1)} %get-tuple-element.61), channel_id=1, source_target_pairs={{0,2},{1,3},{2,4},{3,5},{4,6},{5,7},{6,0},{7,1},{8,10},{9,11},{10,... | collective-permute-start | bytes 1572872 | tf_op jit(solution)/shard_map/ppermute | solution.py:644
  9.0 2.2 %collective-permute-start.3 = (bf16[2,1024,128]{2,1,0:T(8,128)(2,1)S(1)}, bf16[2,1024,128]{2,1,0:T(8,128)(2,1)S(1)}, u32[]{:S(2)}, u32[]{:S(2)}) collective-permute-start(bf16[2,1024,128]{2,1,0:T(8,128)(2,1)S(1)} %get-tuple-element.61), channel_id=1, source_target_pairs={{0,6},{1,7},{2,0},{3,1},{4,2},{5,3},{6,4},{7,5},{8,14},{9,15},{10,... | collective-permute-start | bytes 1572872 | tf_op jit(solution)/shard_map/ppermute | solution.py:644
  11.4 1.6 collective-permute-start.1
  13.0 2.5 %collective-permute-done.1 = s32[3,2,1600]{2,1,0:T(2,128)S(1)} collective-permute-done((s32[3,2,1600]{2,1,0:T(2,128)S(1)}, s32[3,2,1600]{2,1,0:T(2,128)S(1)}, u32[]{:S(2)}, u32[]{:S(2)}) %collective-permute-start.1) | collective-permute-done | bytes 38432 | tf_op jit(solution)/shard_map/ppermute | solution.py:641
  15.8 6.1 %collective-permute-done.5.refs_3_ = bf16[2,1024,128]{2,1,0:T(8,128)(2,1)S(1)} collective-permute-done((bf16[2,1024,128]{2,1,0:T(8,128)(2,1)S(1)}, bf16[2,1024,128]{2,1,0:T(8,128)(2,1)S(1)}, u32[]{:S(2)}, u32[]{:S(2)}) %collective-permute-start.5) | collective-permute-done | bytes 524320 | tf_op jit(solution)/shard_map/ppermute | solution.py:644
  21.9 11.1 %collective-permute-done.3.refs_1_ = bf16[2,1024,128]{2,1,0:T(8,128)(2,1)S(1)} collective-permute-done((bf16[2,1024,128]{2,1,0:T(8,128)(2,1)S(1)}, bf16[2,1024,128]{2,1,0:T(8,128)(2,1)S(1)}, u32[]{:S(2)}, u32[]{:S(2)}) %collective-permute-start.3) | collective-permute-done | bytes 524320 | tf_op jit(solution)/shard_map/ppermute | solution.py:644
  33.0 10.5 %collective-permute-done.9.refs_2_ = bf16[2,1024,128]{2,1,0:T(8,128)(2,1)S(1)} collective-permute-done((bf16[2,1024,128]{2,1,0:T(8,128)(2,1)S(1)}, bf16[2,1024,128]{2,1,0:T(8,128)(2,1)S(1)}, u32[]{:S(2)}, u32[]{:S(2)}) %collective-permute-start.9) | collective-permute-done | bytes 524320 | tf_op jit(solution)/shard_map/ppermute | solution.py:644
  43.8 3.9 %collective-permute-start.7 = (bf16[1,1024,128]{2,1,0:T(8,128)(2,1)S(1)}, bf16[1,1024,128]{2,1,0:T(8,128)(2,1)S(1)}, u32[]{:S(2)}, u32[]{:S(2)}) collective-permute-start(bf16[1,1024,128]{2,1,0:T(8,128)(2,1)S(1)} %get-tuple-element.62), channel_id=1, source_target_pairs={{0,6},{1,7},{2,0},{3,1},{4,2},{5,3},{6,4},{7,5},{8,14},{9,15},{10,... | collective-permute-start | bytes 786440 | tf_op jit(solution)/shard_map/ppermute | solution.py:644
  47.7 6.3 %look_up.3.refs_8_ = f32[3200,128]{1,0:T(8,128)S(1)} custom-call(s32[3200]{0:T(1024)S(1)} %get-tuple-element.113.low_ref.refs_0_, s32[3200]{0:T(1024)S(1)} %get-tuple-element.112.high_ref.refs_1_, bf16[3,1024,128]{2,1,0:T(8,128)(2,1)S(1)} %get-tuple-element.60.refs_0_, bf16[2,1024,128]{2,1,0:T(8,128)(2,1)S(1)} %collective-permute-done.3.refs_1_, ...), custom_call_target="tpu_custom_call" | custom-call | bytes 39321600 | tf_op jit(solution)/shard_map/look_up/pallas_call | solution.py:265
  54.5 6.4 %look_up.4.refs_8_ = f32[3200,128]{1,0:T(8,128)S(1)} custom-call(s32[3200]{0:T(1024)S(1)} %get-tuple-element.111.low_ref.refs_2_, s32[3200]{0:T(1024)S(1)} %get-tuple-element.110.high_ref.refs_3_, bf16[3,1024,128]{2,1,0:T(8,128)(2,1)S(1)} %get-tuple-element.60.refs_0_, bf16[2,1024,128]{2,1,0:T(8,128)(2,1)S(1)} %collective-permute-done.3.refs_1_, ...), custom_call_target="tpu_custom_call" | custom-call | bytes 39321600 | tf_op jit(solution)/shard_map/look_up/pallas_call | solution.py:265
  61.5 3.9 %collective-permute-done.11.refs_2_ = bf16[1,1024,128]{2,1,0:T(8,128)(2,1)S(1)} collective-permute-done((bf16[1,1024,128]{2,1,0:T(8,128)(2,1)S(1)}, bf16[1,1024,128]{2,1,0:T(8,128)(2,1)S(1)}, u32[]{:S(2)}, u32[]{:S(2)}) %collective-permute-start.11) | collective-permute-done | bytes 262176 | tf_op jit(solution)/shard_map/ppermute | solution.py:644
  66.9 6.5 %look_up.5 = bf16[3200,128]{1,0:T(8,128)(2,1)S(1)} custom-call(s32[3200]{0:T(1024)S(1)} %get-tuple-element.115.low_ref.refs_0_, s32[3200]{0:T(1024)S(1)} %get-tuple-element.114.high_ref.refs_1_, bf16[3,1024,128]{2,1,0:T(8,128)(2,1)S(1)} %get-tuple-element.60.refs_0_, bf16[1,1024,128]{2,1,0:T(8,128)(2,1)S(1)} %collective-permute-done.7.refs_1_, ...), custom_call_target="tpu_custom_call" | custom-call | bytes 39321600 | tf_op jit(solution)/shard_map/look_up/pallas_call | solution.py:265
  73.6 1.6 collective-permute-start.15
  77.1 4.4 %collective-permute-done.15.refs_1_ = bf16[800,128]{1,0:T(8,128)(2,1)S(1)} collective-permute-done((bf16[800,128]{1,0:T(8,128)(2,1)S(1)}, bf16[800,128]{1,0:T(8,128)(2,1)S(1)}, u32[]{:S(2)}, u32[]{:S(2)}) %collective-permute-start.15) | collective-permute-done | bytes 204832 | tf_op jit(solution)/shard_map/ppermute | solution.py:641
  81.6 4.8 %collective-permute-done.16.refs_2_ = bf16[800,128]{1,0:T(8,128)(2,1)S(1)} collective-permute-done((bf16[800,128]{1,0:T(8,128)(2,1)S(1)}, bf16[800,128]{1,0:T(8,128)(2,1)S(1)}, u32[]{:S(2)}, u32[]{:S(2)}) %collective-permute-start.16) | collective-permute-done | bytes 204832 | tf_op jit(solution)/shard_map/ppermute | solution.py:641
  86.4 9.5 %both_layers.1 = (bf16[1600,256]{1,0:T(8,128)(2,1)}, bf16[800,128]{1,0:T(8,128)(2,1)S(1)}, bf16[800,128]{1,0:T(8,128)(2,1)S(1)}, bf16[800,128]{1,0:T(8,128)(2,1)...) custom-call(s32[2]{0:T(128)S(1)} %pad_add_fusion.1.at_ref.me_ref, ...), custom_call_target="tpu_custom_call" | custom-call | tf_op jit(solution)/shard_map/both_layers/pallas_call | solution.py:581
  101.7 3.1 %collective-permute-done.21.refs_5_.refs_7_ = bf16[800,128]{1,0:T(8,128)(2,1)S(1)} collective-permute-done((bf16[800,128]{1,0:T(8,128)(2,1)S(1)}, bf16[800,128]{1,0:T(8,128)(2,1)S(1)}, u32[]{:S(2)}, u32[]{:S(2)}) %collective-permute-start.21) | collective-permute-done | bytes 204832 | tf_op jit(solution)/shard_map/ppermute | solution.py:641
  106.3 2.5 %collective-permute-done.20.refs_4_.refs_6_ = bf16[800,128]{1,0:T(8,128)(2,1)S(1)} collective-permute-done((bf16[800,128]{1,0:T(8,128)(2,1)S(1)}, bf16[800,128]{1,0:T(8,128)(2,1)S(1)}, u32[]{:S(2)}, u32[]{:S(2)}) %collective-permute-start.20) | collective-permute-done | bytes 204832 | tf_op jit(solution)/shard_map/ppermute | solution.py:641
  109.2 9.8 %add_rows.2 = (bf16[4,1024,128]{2,1,0:T(8,128)(2,1)S(1)}, bf16[4,1024,128]{2,1,0:T(8,128)(2,1)S(1)}) custom-call(s32[3200]{0:T(1024)S(1)} %get-tuple-element.115.low_ref.refs_0_, s32[3200]{0:T(1024)S(1)} %get-tuple-element.114.high_ref.refs_1_, bf16[800,128]{1,0:T(8,128)(2,1)S(1)} %get-tuple-element.85.refs_2_.refs_4_, ...), custom_call_target="tpu_custom_call" | custom-call | bytes 41943040 | tf_op jit(solution)/shard_map/add_rows/pallas_call | solution.py:329
  119.2 2.6 %collective-permute-done.25.refs_1_ = bf16[4,1024,128]{2,1,0:T(8,128)(2,1)S(1)} collective-permute-done((bf16[4,1024,128]{2,1,0:T(8,128)(2,1)S(1)}, bf16[4,1024,128]{2,1,0:T(8,128)(2,1)S(1)}, u32[]{:S(2)}, u32[]{:S(2)}) %collective-permute-start.25) | collective-permute-done | bytes 1048608 | tf_op jit(solution)/shard_map/ppermute | solution.py:653
  122.0 3.8 %collective-permute-start.27 = (bf16[1440,128]{1,0:T(8,128)(2,1)S(1)}, bf16[1440,128]{1,0:T(8,128)(2,1)S(1)}, u32[]{:S(2)}, u32[]{:S(2)}) collective-permute-start(bf16[1440,128]{1,0:T(8,128)(2,1)S(1)} %get-tuple-element.134), channel_id=1, source_target_pairs={{0,6},{1,7},{2,0},{3,1},{4,2},{5,3},{6,4},{7,5},{8,14},{9,15},{10,... | collective-permute-start | bytes 1105928 | tf_op jit(solution)/shard_map/ppermute | solution.py:644
  125.8 15.5 %add_rows.3 = (bf16[4,1024,128]{2,1,0:T(8,128)(2,1)S(1)}, bf16[4,1024,128]{2,1,0:T(8,128)(2,1)S(1)}, bf16[4,1024,128]{2,1,0:T(8,128)(2,1)S(1)}, bf16[4,1024,128]{2,1,0:T(8,128)(2,1)S(1)}) custom-call(s32[3200]{0:T(1024)S(1)} %get-tuple-element.113.low_ref.refs_0_, s32[3200]{0:T(1024)S(1)} %get-tuple-element.112.high_ref.refs_1_, ...), custom_call_target="tpu_custom_call" | custom-call | bytes 83886080 | tf_op jit(solution)/shard_map/add_rows/pallas_call | solution.py:329
  142.1 6.6 %collective-permute-done.28 = bf16[416,128]{1,0:T(8,128)(2,1)S(1)} collective-permute-done((bf16[416,128]{1,0:T(8,128)(2,1)S(1)}, bf16[416,128]{1,0:T(8,128)(2,1)S(1)}, u32[]{:S(2)}, u32[]{:S(2)}) %collective-permute-start.28) | collective-permute-done | bytes 106528 | tf_op jit(solution)/shard_map/ppermute | solution.py:644
  149.3 3.9 %collective-permute-start.32 = (bf16[2048,128]{1,0:T(8,128)(2,1)S(1)}, bf16[2048,128]{1,0:T(8,128)(2,1)S(1)}, u32[]{:S(2)}, u32[]{:S(2)}) collective-permute-start(bf16[2048,128]{1,0:T(8,128)(2,1)S(1)} %pad_maximum_fusion.1), channel_id=1, source_target_pairs={{0,6},{1,7},{2,0},{3,1},{4,2},{5,3},{6,4},{7,5},{8,14},{9,15},{10,... | collective-permute-start | bytes 1572872 | tf_op jit(solution)/shard_map/ppermute | solution.py:644
  154.9 1.8 collective-permute-start.35
  156.7 1.8 collective-permute-done.33
  159.0 1.6 collective-permute-done.35
  160.5 18.8 %collective-permute-done.32.refs_2_.refs_6_ = bf16[2048,128]{1,0:T(8,128)(2,1)S(1)} collective-permute-done((bf16[2048,128]{1,0:T(8,128)(2,1)S(1)}, bf16[2048,128]{1,0:T(8,128)(2,1)S(1)}, u32[]{:S(2)}, u32[]{:S(2)}) %collective-permute-start.32) | collective-permute-done | bytes 524320 | tf_op jit(solution)/shard_map/ppermute | solution.py:644
  179.8 1.8 collective-permute-done.36.far_ref
  181.5 1.9 scaled_sums.1
  184.4 9.2 %collective-permute-done.37.refs_3_.refs_7_ = bf16[2048,128]{1,0:T(8,128)(2,1)S(1)} collective-permute-done((bf16[2048,128]{1,0:T(8,128)(2,1)S(1)}, bf16[2048,128]{1,0:T(8,128)(2,1)S(1)}, u32[]{:S(2)}, u32[]{:S(2)}) %collective-permute-start.37) | collective-permute-done | bytes 524320 | tf_op jit(solution)/shard_map/ppermute | solution.py:644
  (99 shorter events, 23.1 us)
Async XLA Ops:
  4.0 17.9 %collective-permute-start.5 = (bf16[2,1024,128]{2,1,0:T(8,128)(2,1)S(1)}, bf16[2,1024,128]{2,1,0:T(8,128)(2,1)S(1)}, u32[]{:S(2)}, u32[]{:S(2)}) collective-permute-start(bf16[2,1024,128]{2,1,0:T(8,128)(2,1)S(1)} %get-tuple-element.61), channel_id=1, source_target_pairs={{0,2},{1,3},{2,4},{3,5},{4,6},{5,7},{6,0},{7,1},{8,10},{9,11},{10,... | collective-permute-start | bytes 1572872 | tf_op jit(solution)/shard_map/ppermute | solution.py:644
  9.0 24.0 %collective-permute-start.3 = (bf16[2,1024,128]{2,1,0:T(8,128)(2,1)S(1)}, bf16[2,1024,128]{2,1,0:T(8,128)(2,1)S(1)}, u32[]{:S(2)}, u32[]{:S(2)}) collective-permute-start(bf16[2,1024,128]{2,1,0:T(8,128)(2,1)S(1)} %get-tuple-element.61), channel_id=1, source_target_pairs={{0,6},{1,7},{2,0},{3,1},{4,2},{5,3},{6,4},{7,5},{8,14},{9,15},{10,... | collective-permute-start | bytes 1572872 | tf_op jit(solution)/shard_map/ppermute | solution.py:644
  15.7 27.8 %collective-permute-start.2 = (bf16[3,1024,128]{2,1,0:T(8,128)(2,1)S(1)}, bf16[3,1024,128]{2,1,0:T(8,128)(2,1)S(1)}, u32[]{:S(2)}, u32[]{:S(2)}) collective-permute-start(bf16[3,1024,128]{2,1,0:T(8,128)(2,1)S(1)} %get-tuple-element.60.refs_0_), channel_id=1, source_target_pairs={{0,1},{1,0},{2,3},{3,2},{4,5},{5,4},{6,7},{7,6},{8,9},{9,8},{10,11... | collective-permute-start | bytes 2359304 | tf_op jit(solution)/shard_map/ppermute | solution.py:653
  21.9 21.6 %collective-permute-start.9 = (bf16[2,1024,128]{2,1,0:T(8,128)(2,1)S(1)}, bf16[2,1024,128]{2,1,0:T(8,128)(2,1)S(1)}, u32[]{:S(2)}, u32[]{:S(2)}) collective-permute-start(bf16[2,1024,128]{2,1,0:T(8,128)(2,1)S(1)} %collective-permute-done.5.refs_3_), channel_id=1, source_target_pairs={{0,2},{1,3},{2,4},{3,5},{4,6},{5,7},{6,0},{7,1},{8,10},{9,11},{10,... | collective-permute-start | bytes 1572872 | tf_op jit(solution)/shard_map/ppermute | solution.py:644
  21.9 21.6 %collective-permute-start.6 = (bf16[2,1024,128]{2,1,0:T(8,128)(2,1)S(1)}, bf16[2,1024,128]{2,1,0:T(8,128)(2,1)S(1)}, u32[]{:S(2)}, u32[]{:S(2)}) collective-permute-start(bf16[2,1024,128]{2,1,0:T(8,128)(2,1)S(1)} %collective-permute-done.5.refs_3_), channel_id=1, source_target_pairs={{0,1},{1,0},{2,3},{3,2},{4,5},{5,4},{6,7},{7,6},{8,9},{9,8},{10,11... | collective-permute-start | bytes 1572872 | tf_op jit(solution)/shard_map/ppermute | solution.py:653
  33.0 10.5 %collective-permute-start.4 = (bf16[2,1024,128]{2,1,0:T(8,128)(2,1)S(1)}, bf16[2,1024,128]{2,1,0:T(8,128)(2,1)S(1)}, u32[]{:S(2)}, u32[]{:S(2)}) collective-permute-start(bf16[2,1024,128]{2,1,0:T(8,128)(2,1)S(1)} %collective-permute-done.3.refs_1_), channel_id=1, source_target_pairs={{0,1},{1,0},{2,3},{3,2},{4,5},{5,4},{6,7},{7,6},{8,9},{9,8},{10,11... | collective-permute-start | bytes 1572872 | tf_op jit(solution)/shard_map/ppermute | solution.py:653
  43.5 4.1 %collective-permute-start.10 = (bf16[2,1024,128]{2,1,0:T(8,128)(2,1)S(1)}, bf16[2,1024,128]{2,1,0:T(8,128)(2,1)S(1)}, u32[]{:S(2)}, u32[]{:S(2)}) collective-permute-start(bf16[2,1024,128]{2,1,0:T(8,128)(2,1)S(1)} %collective-permute-done.9.refs_2_), channel_id=1, source_target_pairs={{0,1},{1,0},{2,3},{3,2},{4,5},{5,4},{6,7},{7,6},{8,9},{9,8},{10,11... | collective-permute-start | bytes 1572872 | tf_op jit(solution)/shard_map/ppermute | solution.py:653
  43.5 11.0 %collective-permute-start.8 = (bf16[1,1024,128]{2,1,0:T(8,128)(2,1)S(1)}, bf16[1,1024,128]{2,1,0:T(8,128)(2,1)S(1)}, u32[]{:S(2)}, u32[]{:S(2)}) collective-permute-start(bf16[1,1024,128]{2,1,0:T(8,128)(2,1)S(1)} %get-tuple-element.62), channel_id=1, source_target_pairs={{0,2},{1,3},{2,4},{3,5},{4,6},{5,7},{6,0},{7,1},{8,10},{9,11},{10,... | collective-permute-start | bytes 786440 | tf_op jit(solution)/shard_map/ppermute | solution.py:644
  43.8 17.2 %collective-permute-start.7 = (bf16[1,1024,128]{2,1,0:T(8,128)(2,1)S(1)}, bf16[1,1024,128]{2,1,0:T(8,128)(2,1)S(1)}, u32[]{:S(2)}, u32[]{:S(2)}) collective-permute-start(bf16[1,1024,128]{2,1,0:T(8,128)(2,1)S(1)} %get-tuple-element.62), channel_id=1, source_target_pairs={{0,6},{1,7},{2,0},{3,1},{4,2},{5,3},{6,4},{7,5},{8,14},{9,15},{10,... | collective-permute-start | bytes 786440 | tf_op jit(solution)/shard_map/ppermute | solution.py:644
  54.5 10.8 %collective-permute-start.11 = (bf16[1,1024,128]{2,1,0:T(8,128)(2,1)S(1)}, bf16[1,1024,128]{2,1,0:T(8,128)(2,1)S(1)}, u32[]{:S(2)}, u32[]{:S(2)}) collective-permute-start(bf16[1,1024,128]{2,1,0:T(8,128)(2,1)S(1)} %collective-permute-done.8.refs_3_), channel_id=1, source_target_pairs={{0,2},{1,3},{2,4},{3,5},{4,6},{5,7},{6,0},{7,1},{8,10},{9,11},{10,... | collective-permute-start | bytes 786440 | tf_op jit(solution)/shard_map/ppermute | solution.py:644
  60.9 4.5 %collective-permute-start.14 = (bf16[1,1024,128]{2,1,0:T(8,128)(2,1)S(1)}, bf16[1,1024,128]{2,1,0:T(8,128)(2,1)S(1)}, u32[]{:S(2)}, u32[]{:S(2)}) collective-permute-start(bf16[1,1024,128]{2,1,0:T(8,128)(2,1)S(1)} %collective-permute-done.8.refs_3_), channel_id=1, source_target_pairs={{0,1},{1,0},{2,3},{3,2},{4,5},{5,4},{6,7},{7,6},{8,9},{9,8},{10,11... | collective-permute-start | bytes 786440 | tf_op jit(solution)/shard_map/ppermute | solution.py:653
  61.0 4.4 %collective-permute-start.12 = (bf16[1,1024,128]{2,1,0:T(8,128)(2,1)S(1)}, bf16[1,1024,128]{2,1,0:T(8,128)(2,1)S(1)}, u32[]{:S(2)}, u32[]{:S(2)}) collective-permute-start(bf16[1,1024,128]{2,1,0:T(8,128)(2,1)S(1)} %collective-permute-done.7.refs_1_), channel_id=1, source_target_pairs={{0,1},{1,0},{2,3},{3,2},{4,5},{5,4},{6,7},{7,6},{8,9},{9,8},{10,11... | collective-permute-start | bytes 786440 | tf_op jit(solution)/shard_map/ppermute | solution.py:653
  73.6 8.0 %collective-permute-start.15 = (bf16[800,128]{1,0:T(8,128)(2,1)S(1)}, bf16[800,128]{1,0:T(8,128)(2,1)S(1)}, u32[]{:S(2)}, u32[]{:S(2)}) collective-permute-start(bf16[800,128]{1,0:T(8,128)(2,1)S(1)} %get-tuple-element.130), channel_id=1, source_target_pairs={{0,8},{8,0},{16,24},{24,16},{1,9},{9,1},{17,25},{25,17},{2,10},{10... | collective-permute-start | bytes 614408 | tf_op jit(solution)/shard_map/ppermute | solution.py:641
  75.2 11.2 %collective-permute-start.16 = (bf16[800,128]{1,0:T(8,128)(2,1)S(1)}, bf16[800,128]{1,0:T(8,128)(2,1)S(1)}, u32[]{:S(2)}, u32[]{:S(2)}) collective-permute-start(bf16[800,128]{1,0:T(8,128)(2,1)S(1)} %get-tuple-element.129), channel_id=1, source_target_pairs={{0,16},{8,24},{16,0},{24,8},{1,17},{9,25},{17,1},{25,9},{2,18},{10... | collective-permute-start | bytes 614408 | tf_op jit(solution)/shard_map/ppermute | solution.py:641
  76.7 9.7 %collective-permute-start.17 = (bf16[800,128]{1,0:T(8,128)(2,1)S(1)}, bf16[800,128]{1,0:T(8,128)(2,1)S(1)}, u32[]{:S(2)}, u32[]{:S(2)}) collective-permute-start(bf16[800,128]{1,0:T(8,128)(2,1)S(1)} %get-tuple-element.128), channel_id=1, source_target_pairs={{0,24},{8,16},{16,8},{24,0},{1,25},{9,17},{17,9},{25,1},{2,26},{10... | collective-permute-start | bytes 614408 | tf_op jit(solution)/shard_map/ppermute | solution.py:641
  95.9 8.8 %collective-permute-start.21 = (bf16[800,128]{1,0:T(8,128)(2,1)S(1)}, bf16[800,128]{1,0:T(8,128)(2,1)S(1)}, u32[]{:S(2)}, u32[]{:S(2)}) collective-permute-start(bf16[800,128]{1,0:T(8,128)(2,1)S(1)} %get-tuple-element.76), channel_id=1, source_target_pairs={{0,24},{8,16},{16,8},{24,0},{1,25},{9,17},{17,9},{25,1},{2,26},{10... | collective-permute-start | bytes 614408 | tf_op jit(solution)/shard_map/ppermute | solution.py:641
  97.4 11.3 %collective-permute-start.20 = (bf16[800,128]{1,0:T(8,128)(2,1)S(1)}, bf16[800,128]{1,0:T(8,128)(2,1)S(1)}, u32[]{:S(2)}, u32[]{:S(2)}) collective-permute-start(bf16[800,128]{1,0:T(8,128)(2,1)S(1)} %get-tuple-element.74), channel_id=1, source_target_pairs={{0,16},{8,24},{16,0},{24,8},{1,17},{9,25},{17,1},{25,9},{2,18},{10... | collective-permute-start | bytes 614408 | tf_op jit(solution)/shard_map/ppermute | solution.py:641
  98.6 10.6 %collective-permute-start.19 = (bf16[800,128]{1,0:T(8,128)(2,1)S(1)}, bf16[800,128]{1,0:T(8,128)(2,1)S(1)}, u32[]{:S(2)}, u32[]{:S(2)}) collective-permute-start(bf16[800,128]{1,0:T(8,128)(2,1)S(1)} %get-tuple-element.72), channel_id=1, source_target_pairs={{0,8},{8,0},{16,24},{24,16},{1,9},{9,1},{17,25},{25,17},{2,10},{10... | collective-permute-start | bytes 614408 | tf_op jit(solution)/shard_map/ppermute | solution.py:641
  99.5 19.4 %collective-permute-start.22 = (bf16[208,256]{1,0:T(8,128)(2,1)S(1)}, bf16[208,256]{1,0:T(8,128)(2,1)S(1)}, u32[]{:S(2)}, u32[]{:S(2)}) collective-permute-start(bf16[208,256]{1,0:T(8,128)(2,1)S(1)} %get-tuple-element.126), channel_id=1, source_target_pairs={{0,8},{8,0},{16,24},{24,16},{1,9},{9,1},{17,25},{25,17},{2,10},{10... | collective-permute-start | bytes 319496 | tf_op jit(solution)/shard_map/ppermute | solution.py:641
  100.8 18.2 %collective-permute-start.23 = (bf16[208,256]{1,0:T(8,128)(2,1)S(1)}, bf16[208,256]{1,0:T(8,128)(2,1)S(1)}, u32[]{:S(2)}, u32[]{:S(2)}) collective-permute-start(bf16[208,256]{1,0:T(8,128)(2,1)S(1)} %get-tuple-element.125), channel_id=1, source_target_pairs={{0,16},{8,24},{16,0},{24,8},{1,17},{9,25},{17,1},{25,9},{2,18},{10... | collective-permute-start | bytes 319496 | tf_op jit(solution)/shard_map/ppermute | solution.py:641
  104.8 14.2 %collective-permute-start.24 = (bf16[208,256]{1,0:T(8,128)(2,1)S(1)}, bf16[208,256]{1,0:T(8,128)(2,1)S(1)}, u32[]{:S(2)}, u32[]{:S(2)}) collective-permute-start(bf16[208,256]{1,0:T(8,128)(2,1)S(1)} %get-tuple-element.124), channel_id=1, source_target_pairs={{0,24},{8,16},{16,8},{24,0},{1,25},{9,17},{17,9},{25,1},{2,26},{10... | collective-permute-start | bytes 319496 | tf_op jit(solution)/shard_map/ppermute | solution.py:641
  121.9 19.4 %collective-permute-start.26 = (bf16[1440,128]{1,0:T(8,128)(2,1)S(1)}, bf16[1440,128]{1,0:T(8,128)(2,1)S(1)}, u32[]{:S(2)}, u32[]{:S(2)}) collective-permute-start(bf16[1440,128]{1,0:T(8,128)(2,1)S(1)} %get-tuple-element.135), channel_id=1, source_target_pairs={{0,2},{1,3},{2,4},{3,5},{4,6},{5,7},{6,0},{7,1},{8,10},{9,11},{10,... | collective-permute-start | bytes 1105928 | tf_op jit(solution)/shard_map/ppermute | solution.py:644
  122.0 19.4 %collective-permute-start.27 = (bf16[1440,128]{1,0:T(8,128)(2,1)S(1)}, bf16[1440,128]{1,0:T(8,128)(2,1)S(1)}, u32[]{:S(2)}, u32[]{:S(2)}) collective-permute-start(bf16[1440,128]{1,0:T(8,128)(2,1)S(1)} %get-tuple-element.134), channel_id=1, source_target_pairs={{0,6},{1,7},{2,0},{3,1},{4,2},{5,3},{6,4},{7,5},{8,14},{9,15},{10,... | collective-permute-start | bytes 1105928 | tf_op jit(solution)/shard_map/ppermute | solution.py:644
  141.4 7.5 %collective-permute-start.29 = (bf16[4,1024,128]{2,1,0:T(8,128)(2,1)S(1)}, bf16[4,1024,128]{2,1,0:T(8,128)(2,1)S(1)}, u32[]{:S(2)}, u32[]{:S(2)}) collective-permute-start(bf16[4,1024,128]{2,1,0:T(8,128)(2,1)S(1)} %get-tuple-element.94), channel_id=1, source_target_pairs={{0,1},{1,0},{2,3},{3,2},{4,5},{5,4},{6,7},{7,6},{8,9},{9,8},{10,11... | collective-permute-start | bytes 3145736 | tf_op jit(solution)/shard_map/ppermute | solution.py:653
  141.5 7.5 %collective-permute-start.30 = (bf16[4,1024,128]{2,1,0:T(8,128)(2,1)S(1)}, bf16[4,1024,128]{2,1,0:T(8,128)(2,1)S(1)}, u32[]{:S(2)}, u32[]{:S(2)}) collective-permute-start(bf16[4,1024,128]{2,1,0:T(8,128)(2,1)S(1)} %get-tuple-element.96), channel_id=1, source_target_pairs={{0,1},{1,0},{2,3},{3,2},{4,5},{5,4},{6,7},{7,6},{8,9},{9,8},{10,11... | collective-permute-start | bytes 3145736 | tf_op jit(solution)/shard_map/ppermute | solution.py:653
  142.0 6.8 %collective-permute-start.28 = (bf16[416,128]{1,0:T(8,128)(2,1)S(1)}, bf16[416,128]{1,0:T(8,128)(2,1)S(1)}, u32[]{:S(2)}, u32[]{:S(2)}) collective-permute-start(bf16[416,128]{1,0:T(8,128)(2,1)S(1)} %slice.170), channel_id=1, source_target_pairs={{0,2},{1,3},{2,4},{3,5},{4,6},{5,7},{6,0},{7,1},{8,10},{9,11},{10,... | collective-permute-start | bytes 319496 | tf_op jit(solution)/shard_map/ppermute | solution.py:644
  149.2 30.1 %collective-permute-start.31 = (bf16[3072,128]{1,0:T(8,128)(2,1)S(1)}, bf16[3072,128]{1,0:T(8,128)(2,1)S(1)}, u32[]{:S(2)}, u32[]{:S(2)}) collective-permute-start(bf16[3072,128]{1,0:T(8,128)(2,1)S(1)} %pad_maximum_fusion), channel_id=1, source_target_pairs={{0,2},{1,3},{2,4},{3,5},{4,6},{5,7},{6,0},{7,1},{8,10},{9,11},{10,... | collective-permute-start | bytes 2359304 | tf_op jit(solution)/shard_map/ppermute | solution.py:644
  149.3 30.0 %collective-permute-start.32 = (bf16[2048,128]{1,0:T(8,128)(2,1)S(1)}, bf16[2048,128]{1,0:T(8,128)(2,1)S(1)}, u32[]{:S(2)}, u32[]{:S(2)}) collective-permute-start(bf16[2048,128]{1,0:T(8,128)(2,1)S(1)} %pad_maximum_fusion.1), channel_id=1, source_target_pairs={{0,6},{1,7},{2,0},{3,1},{4,2},{5,3},{6,4},{7,5},{8,14},{9,15},{10,... | collective-permute-start | bytes 1572872 | tf_op jit(solution)/shard_map/ppermute | solution.py:644
  153.2 5.3 %collective-permute-start.33 = (bf16[416,128]{1,0:T(8,128)(2,1)S(1)}, bf16[416,128]{1,0:T(8,128)(2,1)S(1)}, u32[]{:S(2)}, u32[]{:S(2)}) collective-permute-start(bf16[416,128]{1,0:T(8,128)(2,1)S(1)} %add_convert_fusion.6), channel_id=1, source_target_pairs={{0,8},{8,0},{16,24},{24,16},{1,9},{9,1},{17,25},{25,17},{2,10},{10... | collective-permute-start | bytes 319496 | tf_op jit(solution)/shard_map/ppermute | solution.py:641
  154.0 5.0 %collective-permute-start.34 = (bf16[416,128]{1,0:T(8,128)(2,1)S(1)}, bf16[416,128]{1,0:T(8,128)(2,1)S(1)}, u32[]{:S(2)}, u32[]{:S(2)}) collective-permute-start(bf16[416,128]{1,0:T(8,128)(2,1)S(1)} %add_convert_fusion.6), channel_id=1, source_target_pairs={{0,16},{8,24},{16,0},{24,8},{1,17},{9,25},{17,1},{25,9},{2,18},{10... | collective-permute-start | bytes 319496 | tf_op jit(solution)/shard_map/ppermute | solution.py:641
  154.9 5.6 %collective-permute-start.35 = (bf16[416,128]{1,0:T(8,128)(2,1)S(1)}, bf16[416,128]{1,0:T(8,128)(2,1)S(1)}, u32[]{:S(2)}, u32[]{:S(2)}) collective-permute-start(bf16[416,128]{1,0:T(8,128)(2,1)S(1)} %add_convert_fusion.6), channel_id=1, source_target_pairs={{0,24},{8,16},{16,8},{24,0},{1,25},{9,17},{17,9},{25,1},{2,26},{10... | collective-permute-start | bytes 319496 | tf_op jit(solution)/shard_map/ppermute | solution.py:641
  179.6 14.0 %collective-permute-start.37 = (bf16[2048,128]{1,0:T(8,128)(2,1)S(1)}, bf16[2048,128]{1,0:T(8,128)(2,1)S(1)}, u32[]{:S(2)}, u32[]{:S(2)}) collective-permute-start(bf16[2048,128]{1,0:T(8,128)(2,1)S(1)} %pad_maximum_fusion.2), channel_id=1, source_target_pairs={{0,2},{1,3},{2,4},{3,5},{4,6},{5,7},{6,0},{7,1},{8,10},{9,11},{10,... | collective-permute-start | bytes 1572872 | tf_op jit(solution)/shard_map/ppermute | solution.py:644
  (14 other events, 92.8 us)

commit v7 on v6

--- a/solution.py
+++ b/solution.py
@@ -12,7 +12,7 @@
 LANES = 128
 MIB = 2**20
 
-UNROLL = 16
+UNROLL = 25
 
 
 def shifted(values, spacing):
@@ -551,7 +551,7 @@
         while active:
             if len(active) < 2 and waiting:
                 active.append(waiting.pop(0))
-            for one in active[::-1]:
+            for one in list(active):
                 if next(one, "done") == "done":
                     active.remove(one)
         for k in range(groups):

time: 195 us -> 195 us (level)
  no operation moved by 1% of the time
where the time goes in v7:
time: 195 us; the launch traced here: 194 us
  waiting for transfers between devices  94.5 us (48%)
  Pallas kernels  59 us (30%)
  starting transfers between devices  35.8 us (18%)
  local copies, waits for them, and re-layouts  2.71 us (1%)
    ppermute x12, waiting for transfers between devices, table_shift(): lax.ppermute(values, 'table', [(i, (i + k) % shards) for i in range(shard...  67 us
    pallas_call x2, Pallas kernels, add_rows(): pl.pallas_call(kernel, grid_spec=pltpu.PrefetchScalarGridSpec(num_scalar_...  25.1 us
    ppermute x14, waiting for transfers between devices, dp_flip(): return lax.ppermute(values, 'dp', [(i, i ^ k) for i in range(groups)])  21.7 us
    pallas_call x3, Pallas kernels, look_up(): pl.pallas_call(kernel, grid_spec=pltpu.PrefetchScalarGridSpec(num_scalar_...  18.9 us
    ppermute x14, starting transfers between devices, dp_flip(): return lax.ppermute(values, 'dp', [(i, i ^ k) for i in range(groups)])  17.3 us
    ppermute x12, starting transfers between devices, table_shift(): lax.ppermute(values, 'table', [(i, (i + k) % shards) for i in range(shard...  17.1 us
    pallas_call x1, Pallas kernels, both_layers(): pl.pallas_call(kernel, grid_spec=pltpu.PrefetchScalarGridSpec(num_scalar_...  9.41 us
    ppermute x12, waiting for transfers between devices, across(): return lax.ppermute(values, 'table', [(i, i ^ 1) for i in range(shards)])  5.87 us
  transfers between devices with their start and end apart: 38, of which 21 were waited for; matrix products, arithmetic and copies ran while one was open for 1% of the time, Pallas kernels for 21%

profile of v7, /device:TPU:0, one launch (start us, length us, event | category | flops | bytes accessed | tf_op | source)
XLA Modules:
  0.0 194.5 jit_solution(12357354390050479423)
XLA Ops:
  0.7 1.9 copy-done
  4.0 3.1 %collective-permute-start.5 = (bf16[2,1024,128]{2,1,0:T(8,128)(2,1)S(1)}, bf16[2,1024,128]{2,1,0:T(8,128)(2,1)S(1)}, u32[]{:S(2)}, u32[]{:S(2)}) collective-permute-start(bf16[2,1024,128]{2,1,0:T(8,128)(2,1)S(1)} %get-tuple-element.61), channel_id=1, source_target_pairs={{0,2},{1,3},{2,4},{3,5},{4,6},{5,7},{6,0},{7,1},{8,10},{9,11},{10,... | collective-permute-start | bytes 1572872 | tf_op jit(solution)/shard_map/ppermute | solution.py:644
  9.0 2.2 %collective-permute-start.3 = (bf16[2,1024,128]{2,1,0:T(8,128)(2,1)S(1)}, bf16[2,1024,128]{2,1,0:T(8,128)(2,1)S(1)}, u32[]{:S(2)}, u32[]{:S(2)}) collective-permute-start(bf16[2,1024,128]{2,1,0:T(8,128)(2,1)S(1)} %get-tuple-element.61), channel_id=1, source_target_pairs={{0,6},{1,7},{2,0},{3,1},{4,2},{5,3},{6,4},{7,5},{8,14},{9,15},{10,... | collective-permute-start | bytes 1572872 | tf_op jit(solution)/shard_map/ppermute | solution.py:644
  11.4 1.6 collective-permute-start.1
  13.0 2.5 %collective-permute-done.1 = s32[3,2,1600]{2,1,0:T(2,128)S(1)} collective-permute-done((s32[3,2,1600]{2,1,0:T(2,128)S(1)}, s32[3,2,1600]{2,1,0:T(2,128)S(1)}, u32[]{:S(2)}, u32[]{:S(2)}) %collective-permute-start.1) | collective-permute-done | bytes 38432 | tf_op jit(solution)/shard_map/ppermute | solution.py:641
  15.8 6.1 %collective-permute-done.5.refs_3_ = bf16[2,1024,128]{2,1,0:T(8,128)(2,1)S(1)} collective-permute-done((bf16[2,1024,128]{2,1,0:T(8,128)(2,1)S(1)}, bf16[2,1024,128]{2,1,0:T(8,128)(2,1)S(1)}, u32[]{:S(2)}, u32[]{:S(2)}) %collective-permute-start.5) | collective-permute-done | bytes 524320 | tf_op jit(solution)/shard_map/ppermute | solution.py:644
  21.9 11.1 %collective-permute-done.3.refs_1_ = bf16[2,1024,128]{2,1,0:T(8,128)(2,1)S(1)} collective-permute-done((bf16[2,1024,128]{2,1,0:T(8,128)(2,1)S(1)}, bf16[2,1024,128]{2,1,0:T(8,128)(2,1)S(1)}, u32[]{:S(2)}, u32[]{:S(2)}) %collective-permute-start.3) | collective-permute-done | bytes 524320 | tf_op jit(solution)/shard_map/ppermute | solution.py:644
  33.0 10.5 %collective-permute-done.9.refs_2_ = bf16[2,1024,128]{2,1,0:T(8,128)(2,1)S(1)} collective-permute-done((bf16[2,1024,128]{2,1,0:T(8,128)(2,1)S(1)}, bf16[2,1024,128]{2,1,0:T(8,128)(2,1)S(1)}, u32[]{:S(2)}, u32[]{:S(2)}) %collective-permute-start.9) | collective-permute-done | bytes 524320 | tf_op jit(solution)/shard_map/ppermute | solution.py:644
  43.8 3.9 %collective-permute-start.7 = (bf16[1,1024,128]{2,1,0:T(8,128)(2,1)S(1)}, bf16[1,1024,128]{2,1,0:T(8,128)(2,1)S(1)}, u32[]{:S(2)}, u32[]{:S(2)}) collective-permute-start(bf16[1,1024,128]{2,1,0:T(8,128)(2,1)S(1)} %get-tuple-element.62), channel_id=1, source_target_pairs={{0,6},{1,7},{2,0},{3,1},{4,2},{5,3},{6,4},{7,5},{8,14},{9,15},{10,... | collective-permute-start | bytes 786440 | tf_op jit(solution)/shard_map/ppermute | solution.py:644
  47.7 6.2 %look_up.3.refs_8_ = f32[3200,128]{1,0:T(8,128)S(1)} custom-call(s32[3200]{0:T(1024)S(1)} %get-tuple-element.113.low_ref.refs_0_, s32[3200]{0:T(1024)S(1)} %get-tuple-element.112.high_ref.refs_1_, bf16[3,1024,128]{2,1,0:T(8,128)(2,1)S(1)} %get-tuple-element.60.refs_0_, bf16[2,1024,128]{2,1,0:T(8,128)(2,1)S(1)} %collective-permute-done.3.refs_1_, ...), custom_call_target="tpu_custom_call" | custom-call | bytes 39321600 | tf_op jit(solution)/shard_map/look_up/pallas_call | solution.py:265
  54.5 6.3 %look_up.4.refs_8_ = f32[3200,128]{1,0:T(8,128)S(1)} custom-call(s32[3200]{0:T(1024)S(1)} %get-tuple-element.111.low_ref.refs_2_, s32[3200]{0:T(1024)S(1)} %get-tuple-element.110.high_ref.refs_3_, bf16[3,1024,128]{2,1,0:T(8,128)(2,1)S(1)} %get-tuple-element.60.refs_0_, bf16[2,1024,128]{2,1,0:T(8,128)(2,1)S(1)} %collective-permute-done.3.refs_1_, ...), custom_call_target="tpu_custom_call" | custom-call | bytes 39321600 | tf_op jit(solution)/shard_map/look_up/pallas_call | solution.py:265
  61.4 4.0 %collective-permute-done.11.refs_2_ = bf16[1,1024,128]{2,1,0:T(8,128)(2,1)S(1)} collective-permute-done((bf16[1,1024,128]{2,1,0:T(8,128)(2,1)S(1)}, bf16[1,1024,128]{2,1,0:T(8,128)(2,1)S(1)}, u32[]{:S(2)}, u32[]{:S(2)}) %collective-permute-start.11) | collective-permute-done | bytes 262176 | tf_op jit(solution)/shard_map/ppermute | solution.py:644
  66.9 6.4 %look_up.5 = bf16[3200,128]{1,0:T(8,128)(2,1)S(1)} custom-call(s32[3200]{0:T(1024)S(1)} %get-tuple-element.115.low_ref.refs_0_, s32[3200]{0:T(1024)S(1)} %get-tuple-element.114.high_ref.refs_1_, bf16[3,1024,128]{2,1,0:T(8,128)(2,1)S(1)} %get-tuple-element.60.refs_0_, bf16[1,1024,128]{2,1,0:T(8,128)(2,1)S(1)} %collective-permute-done.7.refs_1_, ...), custom_call_target="tpu_custom_call" | custom-call | bytes 39321600 | tf_op jit(solution)/shard_map/look_up/pallas_call | solution.py:265
  73.5 1.6 collective-permute-start.15
  77.0 4.4 %collective-permute-done.15.refs_1_ = bf16[800,128]{1,0:T(8,128)(2,1)S(1)} collective-permute-done((bf16[800,128]{1,0:T(8,128)(2,1)S(1)}, bf16[800,128]{1,0:T(8,128)(2,1)S(1)}, u32[]{:S(2)}, u32[]{:S(2)}) %collective-permute-start.15) | collective-permute-done | bytes 204832 | tf_op jit(solution)/shard_map/ppermute | solution.py:641
  81.5 4.8 %collective-permute-done.16.refs_2_ = bf16[800,128]{1,0:T(8,128)(2,1)S(1)} collective-permute-done((bf16[800,128]{1,0:T(8,128)(2,1)S(1)}, bf16[800,128]{1,0:T(8,128)(2,1)S(1)}, u32[]{:S(2)}, u32[]{:S(2)}) %collective-permute-start.16) | collective-permute-done | bytes 204832 | tf_op jit(solution)/shard_map/ppermute | solution.py:641
  86.3 9.4 %both_layers.1 = (bf16[1600,256]{1,0:T(8,128)(2,1)}, bf16[800,128]{1,0:T(8,128)(2,1)S(1)}, bf16[800,128]{1,0:T(8,128)(2,1)S(1)}, bf16[800,128]{1,0:T(8,128)(2,1)...) custom-call(s32[2]{0:T(128)S(1)} %pad_add_fusion.1.at_ref.me_ref, ...), custom_call_target="tpu_custom_call" | custom-call | tf_op jit(solution)/shard_map/both_layers/pallas_call | solution.py:581
  101.4 3.1 %collective-permute-done.21.refs_5_.refs_7_ = bf16[800,128]{1,0:T(8,128)(2,1)S(1)} collective-permute-done((bf16[800,128]{1,0:T(8,128)(2,1)S(1)}, bf16[800,128]{1,0:T(8,128)(2,1)S(1)}, u32[]{:S(2)}, u32[]{:S(2)}) %collective-permute-start.21) | collective-permute-done | bytes 204832 | tf_op jit(solution)/shard_map/ppermute | solution.py:641
  106.0 2.5 %collective-permute-done.20.refs_4_.refs_6_ = bf16[800,128]{1,0:T(8,128)(2,1)S(1)} collective-permute-done((bf16[800,128]{1,0:T(8,128)(2,1)S(1)}, bf16[800,128]{1,0:T(8,128)(2,1)S(1)}, u32[]{:S(2)}, u32[]{:S(2)}) %collective-permute-start.20) | collective-permute-done | bytes 204832 | tf_op jit(solution)/shard_map/ppermute | solution.py:641
  109.0 9.7 %add_rows.2 = (bf16[4,1024,128]{2,1,0:T(8,128)(2,1)S(1)}, bf16[4,1024,128]{2,1,0:T(8,128)(2,1)S(1)}) custom-call(s32[3200]{0:T(1024)S(1)} %get-tuple-element.115.low_ref.refs_0_, s32[3200]{0:T(1024)S(1)} %get-tuple-element.114.high_ref.refs_1_, bf16[800,128]{1,0:T(8,128)(2,1)S(1)} %get-tuple-element.85.refs_2_.refs_4_, ...), custom_call_target="tpu_custom_call" | custom-call | bytes 41943040 | tf_op jit(solution)/shard_map/add_rows/pallas_call | solution.py:329
  118.9 2.6 %collective-permute-done.25.refs_1_ = bf16[4,1024,128]{2,1,0:T(8,128)(2,1)S(1)} collective-permute-done((bf16[4,1024,128]{2,1,0:T(8,128)(2,1)S(1)}, bf16[4,1024,128]{2,1,0:T(8,128)(2,1)S(1)}, u32[]{:S(2)}, u32[]{:S(2)}) %collective-permute-start.25) | collective-permute-done | bytes 1048608 | tf_op jit(solution)/shard_map/ppermute | solution.py:653
  121.7 3.8 %collective-permute-start.27 = (bf16[1440,128]{1,0:T(8,128)(2,1)S(1)}, bf16[1440,128]{1,0:T(8,128)(2,1)S(1)}, u32[]{:S(2)}, u32[]{:S(2)}) collective-permute-start(bf16[1440,128]{1,0:T(8,128)(2,1)S(1)} %get-tuple-element.134), channel_id=1, source_target_pairs={{0,6},{1,7},{2,0},{3,1},{4,2},{5,3},{6,4},{7,5},{8,14},{9,15},{10,... | collective-permute-start | bytes 1105928 | tf_op jit(solution)/shard_map/ppermute | solution.py:644
  125.5 15.4 %add_rows.3 = (bf16[4,1024,128]{2,1,0:T(8,128)(2,1)S(1)}, bf16[4,1024,128]{2,1,0:T(8,128)(2,1)S(1)}, bf16[4,1024,128]{2,1,0:T(8,128)(2,1)S(1)}, bf16[4,1024,128]{2,1,0:T(8,128)(2,1)S(1)}) custom-call(s32[3200]{0:T(1024)S(1)} %get-tuple-element.113.low_ref.refs_0_, s32[3200]{0:T(1024)S(1)} %get-tuple-element.112.high_ref.refs_1_, ...), custom_call_target="tpu_custom_call" | custom-call | bytes 83886080 | tf_op jit(solution)/shard_map/add_rows/pallas_call | solution.py:329
  141.7 6.6 %collective-permute-done.28 = bf16[416,128]{1,0:T(8,128)(2,1)S(1)} collective-permute-done((bf16[416,128]{1,0:T(8,128)(2,1)S(1)}, bf16[416,128]{1,0:T(8,128)(2,1)S(1)}, u32[]{:S(2)}, u32[]{:S(2)}) %collective-permute-start.28) | collective-permute-done | bytes 106528 | tf_op jit(solution)/shard_map/ppermute | solution.py:644
  148.9 3.9 %collective-permute-start.32 = (bf16[2048,128]{1,0:T(8,128)(2,1)S(1)}, bf16[2048,128]{1,0:T(8,128)(2,1)S(1)}, u32[]{:S(2)}, u32[]{:S(2)}) collective-permute-start(bf16[2048,128]{1,0:T(8,128)(2,1)S(1)} %pad_maximum_fusion.1), channel_id=1, source_target_pairs={{0,6},{1,7},{2,0},{3,1},{4,2},{5,3},{6,4},{7,5},{8,14},{9,15},{10,... | collective-permute-start | bytes 1572872 | tf_op jit(solution)/shard_map/ppermute | solution.py:644
  154.5 1.8 collective-permute-start.35
  156.3 1.8 collective-permute-done.33
  158.5 1.6 collective-permute-done.35
  160.1 18.8 %collective-permute-done.32.refs_2_.refs_6_ = bf16[2048,128]{1,0:T(8,128)(2,1)S(1)} collective-permute-done((bf16[2048,128]{1,0:T(8,128)(2,1)S(1)}, bf16[2048,128]{1,0:T(8,128)(2,1)S(1)}, u32[]{:S(2)}, u32[]{:S(2)}) %collective-permute-start.32) | collective-permute-done | bytes 524320 | tf_op jit(solution)/shard_map/ppermute | solution.py:644
  179.4 1.8 collective-permute-done.36.far_ref
  181.1 1.9 scaled_sums.1
  184.0 9.2 %collective-permute-done.37.refs_3_.refs_7_ = bf16[2048,128]{1,0:T(8,128)(2,1)S(1)} collective-permute-done((bf16[2048,128]{1,0:T(8,128)(2,1)S(1)}, bf16[2048,128]{1,0:T(8,128)(2,1)S(1)}, u32[]{:S(2)}, u32[]{:S(2)}) %collective-permute-start.37) | collective-permute-done | bytes 524320 | tf_op jit(solution)/shard_map/ppermute | solution.py:644
  (99 shorter events, 23.2 us)
Async XLA Ops:
  4.0 17.9 %collective-permute-start.5 = (bf16[2,1024,128]{2,1,0:T(8,128)(2,1)S(1)}, bf16[2,1024,128]{2,1,0:T(8,128)(2,1)S(1)}, u32[]{:S(2)}, u32[]{:S(2)}) collective-permute-start(bf16[2,1024,128]{2,1,0:T(8,128)(2,1)S(1)} %get-tuple-element.61), channel_id=1, source_target_pairs={{0,2},{1,3},{2,4},{3,5},{4,6},{5,7},{6,0},{7,1},{8,10},{9,11},{10,... | collective-permute-start | bytes 1572872 | tf_op jit(solution)/shard_map/ppermute | solution.py:644
  9.0 24.0 %collective-permute-start.3 = (bf16[2,1024,128]{2,1,0:T(8,128)(2,1)S(1)}, bf16[2,1024,128]{2,1,0:T(8,128)(2,1)S(1)}, u32[]{:S(2)}, u32[]{:S(2)}) collective-permute-start(bf16[2,1024,128]{2,1,0:T(8,128)(2,1)S(1)} %get-tuple-element.61), channel_id=1, source_target_pairs={{0,6},{1,7},{2,0},{3,1},{4,2},{5,3},{6,4},{7,5},{8,14},{9,15},{10,... | collective-permute-start | bytes 1572872 | tf_op jit(solution)/shard_map/ppermute | solution.py:644
  15.7 27.8 %collective-permute-start.2 = (bf16[3,1024,128]{2,1,0:T(8,128)(2,1)S(1)}, bf16[3,1024,128]{2,1,0:T(8,128)(2,1)S(1)}, u32[]{:S(2)}, u32[]{:S(2)}) collective-permute-start(bf16[3,1024,128]{2,1,0:T(8,128)(2,1)S(1)} %get-tuple-element.60.refs_0_), channel_id=1, source_target_pairs={{0,1},{1,0},{2,3},{3,2},{4,5},{5,4},{6,7},{7,6},{8,9},{9,8},{10,11... | collective-permute-start | bytes 2359304 | tf_op jit(solution)/shard_map/ppermute | solution.py:653
  21.9 21.6 %collective-permute-start.9 = (bf16[2,1024,128]{2,1,0:T(8,128)(2,1)S(1)}, bf16[2,1024,128]{2,1,0:T(8,128)(2,1)S(1)}, u32[]{:S(2)}, u32[]{:S(2)}) collective-permute-start(bf16[2,1024,128]{2,1,0:T(8,128)(2,1)S(1)} %collective-permute-done.5.refs_3_), channel_id=1, source_target_pairs={{0,2},{1,3},{2,4},{3,5},{4,6},{5,7},{6,0},{7,1},{8,10},{9,11},{10,... | collective-permute-start | bytes 1572872 | tf_op jit(solution)/shard_map/ppermute | solution.py:644
  21.9 21.6 %collective-permute-start.6 = (bf16[2,1024,128]{2,1,0:T(8,128)(2,1)S(1)}, bf16[2,1024,128]{2,1,0:T(8,128)(2,1)S(1)}, u32[]{:S(2)}, u32[]{:S(2)}) collective-permute-start(bf16[2,1024,128]{2,1,0:T(8,128)(2,1)S(1)} %collective-permute-done.5.refs_3_), channel_id=1, source_target_pairs={{0,1},{1,0},{2,3},{3,2},{4,5},{5,4},{6,7},{7,6},{8,9},{9,8},{10,11... | collective-permute-start | bytes 1572872 | tf_op jit(solution)/shard_map/ppermute | solution.py:653
  33.0 10.5 %collective-permute-start.4 = (bf16[2,1024,128]{2,1,0:T(8,128)(2,1)S(1)}, bf16[2,1024,128]{2,1,0:T(8,128)(2,1)S(1)}, u32[]{:S(2)}, u32[]{:S(2)}) collective-permute-start(bf16[2,1024,128]{2,1,0:T(8,128)(2,1)S(1)} %collective-permute-done.3.refs_1_), channel_id=1, source_target_pairs={{0,1},{1,0},{2,3},{3,2},{4,5},{5,4},{6,7},{7,6},{8,9},{9,8},{10,11... | collective-permute-start | bytes 1572872 | tf_op jit(solution)/shard_map/ppermute | solution.py:653
  43.5 4.1 %collective-permute-start.10 = (bf16[2,1024,128]{2,1,0:T(8,128)(2,1)S(1)}, bf16[2,1024,128]{2,1,0:T(8,128)(2,1)S(1)}, u32[]{:S(2)}, u32[]{:S(2)}) collective-permute-start(bf16[2,1024,128]{2,1,0:T(8,128)(2,1)S(1)} %collective-permute-done.9.refs_2_), channel_id=1, source_target_pairs={{0,1},{1,0},{2,3},{3,2},{4,5},{5,4},{6,7},{7,6},{8,9},{9,8},{10,11... | collective-permute-start | bytes 1572872 | tf_op jit(solution)/shard_map/ppermute | solution.py:653
  43.5 11.0 %collective-permute-start.8 = (bf16[1,1024,128]{2,1,0:T(8,128)(2,1)S(1)}, bf16[1,1024,128]{2,1,0:T(8,128)(2,1)S(1)}, u32[]{:S(2)}, u32[]{:S(2)}) collective-permute-start(bf16[1,1024,128]{2,1,0:T(8,128)(2,1)S(1)} %get-tuple-element.62), channel_id=1, source_target_pairs={{0,2},{1,3},{2,4},{3,5},{4,6},{5,7},{6,0},{7,1},{8,10},{9,11},{10,... | collective-permute-start | bytes 786440 | tf_op jit(solution)/shard_map/ppermute | solution.py:644
  43.8 17.1 %collective-permute-start.7 = (bf16[1,1024,128]{2,1,0:T(8,128)(2,1)S(1)}, bf16[1,1024,128]{2,1,0:T(8,128)(2,1)S(1)}, u32[]{:S(2)}, u32[]{:S(2)}) collective-permute-start(bf16[1,1024,128]{2,1,0:T(8,128)(2,1)S(1)} %get-tuple-element.62), channel_id=1, source_target_pairs={{0,6},{1,7},{2,0},{3,1},{4,2},{5,3},{6,4},{7,5},{8,14},{9,15},{10,... | collective-permute-start | bytes 786440 | tf_op jit(solution)/shard_map/ppermute | solution.py:644
  54.5 10.8 %collective-permute-start.11 = (bf16[1,1024,128]{2,1,0:T(8,128)(2,1)S(1)}, bf16[1,1024,128]{2,1,0:T(8,128)(2,1)S(1)}, u32[]{:S(2)}, u32[]{:S(2)}) collective-permute-start(bf16[1,1024,128]{2,1,0:T(8,128)(2,1)S(1)} %collective-permute-done.8.refs_3_), channel_id=1, source_target_pairs={{0,2},{1,3},{2,4},{3,5},{4,6},{5,7},{6,0},{7,1},{8,10},{9,11},{10,... | collective-permute-start | bytes 786440 | tf_op jit(solution)/shard_map/ppermute | solution.py:644
  60.8 4.6 %collective-permute-start.14 = (bf16[1,1024,128]{2,1,0:T(8,128)(2,1)S(1)}, bf16[1,1024,128]{2,1,0:T(8,128)(2,1)S(1)}, u32[]{:S(2)}, u32[]{:S(2)}) collective-permute-start(bf16[1,1024,128]{2,1,0:T(8,128)(2,1)S(1)} %collective-permute-done.8.refs_3_), channel_id=1, source_target_pairs={{0,1},{1,0},{2,3},{3,2},{4,5},{5,4},{6,7},{7,6},{8,9},{9,8},{10,11... | collective-permute-start | bytes 786440 | tf_op jit(solution)/shard_map/ppermute | solution.py:653
  60.9 4.5 %collective-permute-start.12 = (bf16[1,1024,128]{2,1,0:T(8,128)(2,1)S(1)}, bf16[1,1024,128]{2,1,0:T(8,128)(2,1)S(1)}, u32[]{:S(2)}, u32[]{:S(2)}) collective-permute-start(bf16[1,1024,128]{2,1,0:T(8,128)(2,1)S(1)} %collective-permute-done.7.refs_1_), channel_id=1, source_target_pairs={{0,1},{1,0},{2,3},{3,2},{4,5},{5,4},{6,7},{7,6},{8,9},{9,8},{10,11... | collective-permute-start | bytes 786440 | tf_op jit(solution)/shard_map/ppermute | solution.py:653
  73.5 8.0 %collective-permute-start.15 = (bf16[800,128]{1,0:T(8,128)(2,1)S(1)}, bf16[800,128]{1,0:T(8,128)(2,1)S(1)}, u32[]{:S(2)}, u32[]{:S(2)}) collective-permute-start(bf16[800,128]{1,0:T(8,128)(2,1)S(1)} %get-tuple-element.130), channel_id=1, source_target_pairs={{0,8},{8,0},{16,24},{24,16},{1,9},{9,1},{17,25},{25,17},{2,10},{10... | collective-permute-start | bytes 614408 | tf_op jit(solution)/shard_map/ppermute | solution.py:641
  75.0 11.2 %collective-permute-start.16 = (bf16[800,128]{1,0:T(8,128)(2,1)S(1)}, bf16[800,128]{1,0:T(8,128)(2,1)S(1)}, u32[]{:S(2)}, u32[]{:S(2)}) collective-permute-start(bf16[800,128]{1,0:T(8,128)(2,1)S(1)} %get-tuple-element.129), channel_id=1, source_target_pairs={{0,16},{8,24},{16,0},{24,8},{1,17},{9,25},{17,1},{25,9},{2,18},{10... | collective-permute-start | bytes 614408 | tf_op jit(solution)/shard_map/ppermute | solution.py:641
  76.6 9.7 %collective-permute-start.17 = (bf16[800,128]{1,0:T(8,128)(2,1)S(1)}, bf16[800,128]{1,0:T(8,128)(2,1)S(1)}, u32[]{:S(2)}, u32[]{:S(2)}) collective-permute-start(bf16[800,128]{1,0:T(8,128)(2,1)S(1)} %get-tuple-element.128), channel_id=1, source_target_pairs={{0,24},{8,16},{16,8},{24,0},{1,25},{9,17},{17,9},{25,1},{2,26},{10... | collective-permute-start | bytes 614408 | tf_op jit(solution)/shard_map/ppermute | solution.py:641
  95.7 8.8 %collective-permute-start.21 = (bf16[800,128]{1,0:T(8,128)(2,1)S(1)}, bf16[800,128]{1,0:T(8,128)(2,1)S(1)}, u32[]{:S(2)}, u32[]{:S(2)}) collective-permute-start(bf16[800,128]{1,0:T(8,128)(2,1)S(1)} %get-tuple-element.76), channel_id=1, source_target_pairs={{0,24},{8,16},{16,8},{24,0},{1,25},{9,17},{17,9},{25,1},{2,26},{10... | collective-permute-start | bytes 614408 | tf_op jit(solution)/shard_map/ppermute | solution.py:641
  97.2 11.4 %collective-permute-start.20 = (bf16[800,128]{1,0:T(8,128)(2,1)S(1)}, bf16[800,128]{1,0:T(8,128)(2,1)S(1)}, u32[]{:S(2)}, u32[]{:S(2)}) collective-permute-start(bf16[800,128]{1,0:T(8,128)(2,1)S(1)} %get-tuple-element.74), channel_id=1, source_target_pairs={{0,16},{8,24},{16,0},{24,8},{1,17},{9,25},{17,1},{25,9},{2,18},{10... | collective-permute-start | bytes 614408 | tf_op jit(solution)/shard_map/ppermute | solution.py:641
  98.4 10.6 %collective-permute-start.19 = (bf16[800,128]{1,0:T(8,128)(2,1)S(1)}, bf16[800,128]{1,0:T(8,128)(2,1)S(1)}, u32[]{:S(2)}, u32[]{:S(2)}) collective-permute-start(bf16[800,128]{1,0:T(8,128)(2,1)S(1)} %get-tuple-element.72), channel_id=1, source_target_pairs={{0,8},{8,0},{16,24},{24,16},{1,9},{9,1},{17,25},{25,17},{2,10},{10... | collective-permute-start | bytes 614408 | tf_op jit(solution)/shard_map/ppermute | solution.py:641
  99.3 19.4 %collective-permute-start.22 = (bf16[208,256]{1,0:T(8,128)(2,1)S(1)}, bf16[208,256]{1,0:T(8,128)(2,1)S(1)}, u32[]{:S(2)}, u32[]{:S(2)}) collective-permute-start(bf16[208,256]{1,0:T(8,128)(2,1)S(1)} %get-tuple-element.126), channel_id=1, source_target_pairs={{0,8},{8,0},{16,24},{24,16},{1,9},{9,1},{17,25},{25,17},{2,10},{10... | collective-permute-start | bytes 319496 | tf_op jit(solution)/shard_map/ppermute | solution.py:641
  100.6 18.1 %collective-permute-start.23 = (bf16[208,256]{1,0:T(8,128)(2,1)S(1)}, bf16[208,256]{1,0:T(8,128)(2,1)S(1)}, u32[]{:S(2)}, u32[]{:S(2)}) collective-permute-start(bf16[208,256]{1,0:T(8,128)(2,1)S(1)} %get-tuple-element.125), channel_id=1, source_target_pairs={{0,16},{8,24},{16,0},{24,8},{1,17},{9,25},{17,1},{25,9},{2,18},{10... | collective-permute-start | bytes 319496 | tf_op jit(solution)/shard_map/ppermute | solution.py:641
  104.5 14.2 %collective-permute-start.24 = (bf16[208,256]{1,0:T(8,128)(2,1)S(1)}, bf16[208,256]{1,0:T(8,128)(2,1)S(1)}, u32[]{:S(2)}, u32[]{:S(2)}) collective-permute-start(bf16[208,256]{1,0:T(8,128)(2,1)S(1)} %get-tuple-element.124), channel_id=1, source_target_pairs={{0,24},{8,16},{16,8},{24,0},{1,25},{9,17},{17,9},{25,1},{2,26},{10... | collective-permute-start | bytes 319496 | tf_op jit(solution)/shard_map/ppermute | solution.py:641
  121.6 19.3 %collective-permute-start.26 = (bf16[1440,128]{1,0:T(8,128)(2,1)S(1)}, bf16[1440,128]{1,0:T(8,128)(2,1)S(1)}, u32[]{:S(2)}, u32[]{:S(2)}) collective-permute-start(bf16[1440,128]{1,0:T(8,128)(2,1)S(1)} %get-tuple-element.135), channel_id=1, source_target_pairs={{0,2},{1,3},{2,4},{3,5},{4,6},{5,7},{6,0},{7,1},{8,10},{9,11},{10,... | collective-permute-start | bytes 1105928 | tf_op jit(solution)/shard_map/ppermute | solution.py:644
  121.7 19.2 %collective-permute-start.27 = (bf16[1440,128]{1,0:T(8,128)(2,1)S(1)}, bf16[1440,128]{1,0:T(8,128)(2,1)S(1)}, u32[]{:S(2)}, u32[]{:S(2)}) collective-permute-start(bf16[1440,128]{1,0:T(8,128)(2,1)S(1)} %get-tuple-element.134), channel_id=1, source_target_pairs={{0,6},{1,7},{2,0},{3,1},{4,2},{5,3},{6,4},{7,5},{8,14},{9,15},{10,... | collective-permute-start | bytes 1105928 | tf_op jit(solution)/shard_map/ppermute | solution.py:644
  141.0 7.5 %collective-permute-start.29 = (bf16[4,1024,128]{2,1,0:T(8,128)(2,1)S(1)}, bf16[4,1024,128]{2,1,0:T(8,128)(2,1)S(1)}, u32[]{:S(2)}, u32[]{:S(2)}) collective-permute-start(bf16[4,1024,128]{2,1,0:T(8,128)(2,1)S(1)} %get-tuple-element.94), channel_id=1, source_target_pairs={{0,1},{1,0},{2,3},{3,2},{4,5},{5,4},{6,7},{7,6},{8,9},{9,8},{10,11... | collective-permute-start | bytes 3145736 | tf_op jit(solution)/shard_map/ppermute | solution.py:653
  141.0 7.5 %collective-permute-start.30 = (bf16[4,1024,128]{2,1,0:T(8,128)(2,1)S(1)}, bf16[4,1024,128]{2,1,0:T(8,128)(2,1)S(1)}, u32[]{:S(2)}, u32[]{:S(2)}) collective-permute-start(bf16[4,1024,128]{2,1,0:T(8,128)(2,1)S(1)} %get-tuple-element.96), channel_id=1, source_target_pairs={{0,1},{1,0},{2,3},{3,2},{4,5},{5,4},{6,7},{7,6},{8,9},{9,8},{10,11... | collective-permute-start | bytes 3145736 | tf_op jit(solution)/shard_map/ppermute | solution.py:653
  141.6 6.8 %collective-permute-start.28 = (bf16[416,128]{1,0:T(8,128)(2,1)S(1)}, bf16[416,128]{1,0:T(8,128)(2,1)S(1)}, u32[]{:S(2)}, u32[]{:S(2)}) collective-permute-start(bf16[416,128]{1,0:T(8,128)(2,1)S(1)} %slice.170), channel_id=1, source_target_pairs={{0,2},{1,3},{2,4},{3,5},{4,6},{5,7},{6,0},{7,1},{8,10},{9,11},{10,... | collective-permute-start | bytes 319496 | tf_op jit(solution)/shard_map/ppermute | solution.py:644
  148.8 30.1 %collective-permute-start.31 = (bf16[3072,128]{1,0:T(8,128)(2,1)S(1)}, bf16[3072,128]{1,0:T(8,128)(2,1)S(1)}, u32[]{:S(2)}, u32[]{:S(2)}) collective-permute-start(bf16[3072,128]{1,0:T(8,128)(2,1)S(1)} %pad_maximum_fusion), channel_id=1, source_target_pairs={{0,2},{1,3},{2,4},{3,5},{4,6},{5,7},{6,0},{7,1},{8,10},{9,11},{10,... | collective-permute-start | bytes 2359304 | tf_op jit(solution)/shard_map/ppermute | solution.py:644
  148.9 30.0 %collective-permute-start.32 = (bf16[2048,128]{1,0:T(8,128)(2,1)S(1)}, bf16[2048,128]{1,0:T(8,128)(2,1)S(1)}, u32[]{:S(2)}, u32[]{:S(2)}) collective-permute-start(bf16[2048,128]{1,0:T(8,128)(2,1)S(1)} %pad_maximum_fusion.1), channel_id=1, source_target_pairs={{0,6},{1,7},{2,0},{3,1},{4,2},{5,3},{6,4},{7,5},{8,14},{9,15},{10,... | collective-permute-start | bytes 1572872 | tf_op jit(solution)/shard_map/ppermute | solution.py:644
  152.8 5.3 %collective-permute-start.33 = (bf16[416,128]{1,0:T(8,128)(2,1)S(1)}, bf16[416,128]{1,0:T(8,128)(2,1)S(1)}, u32[]{:S(2)}, u32[]{:S(2)}) collective-permute-start(bf16[416,128]{1,0:T(8,128)(2,1)S(1)} %add_convert_fusion.6), channel_id=1, source_target_pairs={{0,8},{8,0},{16,24},{24,16},{1,9},{9,1},{17,25},{25,17},{2,10},{10... | collective-permute-start | bytes 319496 | tf_op jit(solution)/shard_map/ppermute | solution.py:641
  153.6 5.0 %collective-permute-start.34 = (bf16[416,128]{1,0:T(8,128)(2,1)S(1)}, bf16[416,128]{1,0:T(8,128)(2,1)S(1)}, u32[]{:S(2)}, u32[]{:S(2)}) collective-permute-start(bf16[416,128]{1,0:T(8,128)(2,1)S(1)} %add_convert_fusion.6), channel_id=1, source_target_pairs={{0,16},{8,24},{16,0},{24,8},{1,17},{9,25},{17,1},{25,9},{2,18},{10... | collective-permute-start | bytes 319496 | tf_op jit(solution)/shard_map/ppermute | solution.py:641
  154.5 5.6 %collective-permute-start.35 = (bf16[416,128]{1,0:T(8,128)(2,1)S(1)}, bf16[416,128]{1,0:T(8,128)(2,1)S(1)}, u32[]{:S(2)}, u32[]{:S(2)}) collective-permute-start(bf16[416,128]{1,0:T(8,128)(2,1)S(1)} %add_convert_fusion.6), channel_id=1, source_target_pairs={{0,24},{8,16},{16,8},{24,0},{1,25},{9,17},{17,9},{25,1},{2,26},{10... | collective-permute-start | bytes 319496 | tf_op jit(solution)/shard_map/ppermute | solution.py:641
  179.1 14.0 %collective-permute-start.37 = (bf16[2048,128]{1,0:T(8,128)(2,1)S(1)}, bf16[2048,128]{1,0:T(8,128)(2,1)S(1)}, u32[]{:S(2)}, u32[]{:S(2)}) collective-permute-start(bf16[2048,128]{1,0:T(8,128)(2,1)S(1)} %pad_maximum_fusion.2), channel_id=1, source_target_pairs={{0,2},{1,3},{2,4},{3,5},{4,6},{5,7},{6,0},{7,1},{8,10},{9,11},{10,... | collective-permute-start | bytes 1572872 | tf_op jit(solution)/shard_map/ppermute | solution.py:644
  (14 other events, 92.8 us)
